TPU v7x, 32 devices: a whole 2x2x4 slice. The times are simulated.
32 devices in a mesh: parts: 2 (over x), tm: 16 (over z, y, core).
Axes of the slice: x: 2, y: 2, z: 4, core: 2. Of those that a mesh axis runs over, the one named last changes fastest.
Arguments:
- observations: float32 [256, 2048], P(('parts', 'tm')), parts along dimension 0, may hold values from -6 to 6
- outage_mask: int32 [256, 16], P(('parts', 'tm')), parts along dimension 0, may hold values 0 or 1
- group_length: int32 [32], P(('parts', 'tm')), parts along dimension 0, may hold values from 1 to 8, 96 in all
- prior_mean: float32 [4096], P('parts'), parts along dimension 0, may hold values from -8 to 8
- transition: float32 [16, 128, 128], replicated, may hold values from -1 to 1, as said below
- filter_gain: float32 [16, 128, 128], replicated, may hold values from -1 to 1, as said below
- smoother_gain: float32 [16, 128, 128], replicated, may hold values from -1 to 1, as said below
Outputs:
- smoothed: float32 [256, 2048], P(('parts', 'tm')), parts along dimension 0
There are 2 independent parts, one for each index of `parts`. A program takes and returns all parts, laid end to end along the dimension named above; an argument that names none is the same for every part. Nothing has to cross between parts.
Inputs may be any that keep to these rules, and one draw needn't show every extreme that they name: `group_length`: live steps of each tm index; they sum to 96 and one entry equals 8. `transition`: nonzero only between states 2p and 2p + 1 of a block; spectral norm below 1. `filter_gain`: Symmetric, eigenvalues between 0 and 1. `smoother_gain`: spectral norm below 1.
All inputs are finite; a program needn't handle non-finite values. No bound on the sum of `outage_mask` or of `group_length` on one device may be relied on, other than what follows from the above.
Results may differ from a plain program's by a relative error of at most 0.0003.
Values sent between devices are 32-bit elements; how exact they have to be, the bound alone decides.
No kernel may reach another device: no remote copies, remote signals or barrier semaphores. Data moves between devices by JAX's collectives and lax.ppermute only.
A program may use at most 320 MiB of HBM per device.

v0:
```python
import jax
import jax.numpy as jnp
from jax import lax
from jax.sharding import PartitionSpec as P

highest = lax.Precision.HIGHEST


def carried_in(part, axis, combine, identity, reverse):
    count = lax.axis_size(axis)
    place = lax.axis_index(axis)
    ahead = count - 1 - place if reverse else place
    gathered = jax.tree.map(lambda a: lax.all_gather(a, axis), part)
    state = jax.tree.map(lambda a, e: jnp.zeros_like(a) + jnp.asarray(e, a.dtype), part, identity)

    def one(hop, state):
        source = count - 1 - hop if reverse else hop
        return combine(
            state, jax.tree.map(lambda a: lax.dynamic_index_in_dim(a, source, 0, False), gathered)
        )

    return lax.fori_loop(0, ahead, one, state)


def mat_mul(left, right):
    return jnp.einsum("bij,bjk->bik", left, right, precision=highest)


def mat_vec(matrix, vector):
    return jnp.einsum("bij,bj->bi", matrix, vector, precision=highest)


def compose(earlier, later_part):
    return (mat_mul(later_part[0], earlier[0]), mat_vec(later_part[0], earlier[1]) + later_part[1])


def shards(
    observations, outage_mask, group_length, prior_mean, transition, filter_gain, smoother_gain
):
    capacity = observations.shape[0]
    nblocks = transition.shape[0]
    width = transition.shape[1]
    identity_mat = jnp.eye(width, dtype=jnp.float32)
    identity_all = jnp.broadcast_to(identity_mat, transition.shape)
    updated = mat_mul(identity_mat - filter_gain, transition)
    back_keep = identity_mat - mat_mul(smoother_gain, transition)
    readings = observations.reshape(capacity, nblocks, width)
    length = group_length[0]
    slot_index = jnp.arange(capacity, dtype=jnp.int32)
    alive_slot = slot_index < length
    observed = (outage_mask == 1) & alive_slot[:, None]
    gain_terms = jnp.einsum("bij,tbj->tbi", filter_gain, readings, precision=highest)
    gain_terms = jnp.where(observed[:, :, None], gain_terms, jnp.float32(0.0))
    step_mats = jnp.where(observed[:, :, None, None], updated[None], transition[None])
    step_mats = jnp.where(alive_slot[:, None, None, None], step_mats, identity_mat[None, None])
    start_state = prior_mean.reshape(nblocks, width)
    zero_state = jnp.zeros((nblocks, width), jnp.float32)
    is_last = lax.axis_index("tm") == lax.axis_size("tm") - 1

    def compose_local(carried, inputs):
        step_mat, gain_term = inputs
        offset = mat_vec(step_mat, carried[1]) + gain_term
        return ((mat_mul(step_mat, carried[0]), offset), None)

    (group_map, group_offset), _ = lax.scan(
        compose_local, (identity_all, zero_state), (step_mats, gain_terms)
    )
    before_map, before_offset = carried_in(
        (group_map, group_offset), "tm", compose, (identity_all, zero_state), False
    )
    entry_state = mat_vec(before_map, start_state) + before_offset

    def forward(state, inputs):
        step_mat, gain_term, is_alive = inputs
        moved_state = mat_vec(step_mat, state) + gain_term
        moved_state = jnp.where(is_alive, moved_state, state)
        return (moved_state, moved_state)

    _, filtered = lax.scan(forward, entry_state, (step_mats, gain_terms, alive_slot))
    is_end = is_last & (slot_index == length - 1)

    def backward_run(later_start):

        def backward(later_state, inputs):
            state, is_alive, end_slot = inputs
            recurred = mat_vec(back_keep, state) + mat_vec(smoother_gain, later_state)
            result = jnp.where(end_slot, state, recurred)
            next_state = jnp.where(is_alive, result, later_state)
            return (next_state, jnp.where(is_alive, result, jnp.float32(0.0)))

        return lax.scan(backward, later_start, (filtered, alive_slot, is_end), reverse=True)

    group_back, _ = backward_run(zero_state)
    power_result = identity_all
    power_mat = smoother_gain
    bit_count = capacity.bit_length()
    for bit_index in range(bit_count):
        use_bit = length >> bit_index & 1 == 1
        power_result = jnp.where(use_bit, mat_mul(power_result, power_mat), power_result)
        if bit_index + 1 < bit_count:
            power_mat = mat_mul(power_mat, power_mat)
    back_map = jnp.where(is_last, jnp.float32(0.0), power_result)
    after_map, after_offset = carried_in(
        (back_map, group_back), "tm", compose, (identity_all, zero_state), True
    )
    _, smoothed = backward_run(after_offset)
    return smoothed.reshape(capacity, nblocks * width)


def solution(mesh):
    placed = (
        P(("parts", "tm"), None),
        P(("parts", "tm"), None),
        P(("parts", "tm")),
        P("parts"),
        P(),
        P(),
        P(),
    )
    return jax.shard_map(
        shards, mesh=mesh, in_specs=placed, out_specs=P(("parts", "tm"), None), check_vma=False
    )
```

profile of v0, /device:TPU:0, one launch (start us, length us, event | category | flops | bytes accessed | tf_op | source)
XLA Modules:
  0.0 486.1 jit_solution(12113377193240036252)
XLA Ops:
  8.1 2.9 fusion.27
  11.1 2.7 fusion.28
  13.8 5.2 %select_select_fusion = f32[8,16,128,128]{3,2,1,0:T(8,128)} fusion(f32[128,128]{1,0:T(8,128)S(1)} %fusion.33, f32[16,128,128]{2,1,0:T(8,128)} %param.23, f32[16,128,128]{2,1,0:T(8,128)S(1)} %fusion.28, pred[8]{0:T(512)(128)(4,1)S(1)} %iota_compare_fusion.1, pred[8,16]{1,0:T(8,128)(4,1)S(1)} %compare_and_fusion), kind=kLoop, calls=%fused_computation.39 | loop fusion | flops 4194304 | bytes 10551432 | tf_op jit(solution)/shard_map/jit(_where)/select_n | solution.py:55
  19.1 44.0 %while.86 = (s32[]{:T(128)}, f32[16,128,128]{2,1,0:T(8,128)S(1)}, f32[16,128]{1,0:T(8,128)S(1)}, f32[8,16,128,128]{3,2,1,0:T(8,128)}, f32[8,16,128]{2,1,0:T(8,128)S(1)}, /*index=5*/s32[]{:T(128)}, s32[]{:T(128)}) while((s32[]{:T(128)}, f32[16,128,128]{2,1,0:T(8,128)S(1)}, f32[16,128]{1,0:T(8,128)S(1)}, ...), condition=%wide.region_1.2_spmd.clone, body=%wide.region_0.1_spmd.clone.sunk | while | flops 405803008 | bytes 6349915 | solution.py:65
  19.2 3.0 fusion.130
  22.3 2.4 fusion.129
  24.7 3.0 fusion.130
  27.8 2.4 fusion.129
  30.2 3.0 fusion.130
  33.3 2.4 fusion.129
  35.7 3.0 fusion.130
  38.8 2.4 fusion.129
  41.2 3.0 fusion.130
  44.3 2.4 fusion.129
  46.7 3.0 fusion.130
  49.8 2.4 fusion.129
  52.2 3.0 fusion.130
  55.3 2.4 fusion.129
  57.7 3.0 fusion.130
  60.8 2.4 fusion.129
  71.4 2.2 fusion.26
  73.6 24.4 %all-gather.2 = f32[256,128]{1,0:T(8,128)S(1)} all-gather(f32[16,128]{1,0:T(8,128)S(1)} %get-tuple-element.485), channel_id=4, replica_groups=mesh['parts'=2,'tm'=16] {'tm'}, dimensions={0}, use_global_device_ids=true | all-gather | bytes 139264 | tf_op jit(solution)/shard_map/all_gather | solution.py:13
  99.2 95.8 %all-gather.9.cloned.1.call-done = f32[256,128,128]{2,1,0:T(8,128)} async-done(((f32[16,128,128]{2,1,0:T(8,128)}), f32[256,128,128]{2,1,0:T(8,128)}) %all-gather.9.cloned.1.call-update) | async-done | bytes 16777232 | tf_op jit(solution)/shard_map/all_gather | solution.py:13
  197.5 34.1 %while.83 = (s32[]{:T(128)}, f32[16,128]{1,0:T(8,128)S(1)}, f32[8,16,128]{2,1,0:T(8,128)S(1)}, pred[8]{0:T(512)(128)(4,1)S(1)}, f32[8,16,128,128]{3,2,1,0:T(8,128)}, /*index=5*/f32[8,16,128]{2,1,0:T(8,128)S(1)}, s32[]{:T(128)}) while((s32[]{:T(128)}, f32[16,128]{1,0:T(8,128)S(1)}, f32[8,16,128]{2,1,0:T(8,128)S(1)}, pred[8]{0:T(512)(128)(4,1)S(1)}, ...), condition=%wide.region_5.6_spmd, body=%wide.region_4.5_spmd.sunk | while | flops 3149826 | bytes 1106520 | solution.py:79
  197.6 2.9 fusion.115
  201.8 3.1 fusion.115
  206.2 2.9 fusion.115
  210.4 3.0 fusion.115
  214.6 3.0 fusion.115
  218.9 2.9 fusion.115
  223.1 3.0 fusion.115
  227.4 2.9 fusion.115
  231.6 49.6 %while.87 = (s32[]{:T(128)}, f32[16,128]{1,0:T(8,128)S(1)}, pred[8]{0:T(512)(128)(4,1)S(1)}, pred[8]{0:T(512)(128)(4,1)S(1)}, f32[8,16,128]{2,1,0:T(8,128)S(1)},...) while((s32[]{:T(128)}, f32[16,128]{1,0:T(8,128)S(1)}, ...), condition=%wide.region_7.8_spmd.clone, body=%wide.region_6.7_spmd.clone.sunk | while | flops 6301700 | bytes 2203794 | solution.py:91
  231.7 1.7 fusion.135
  244.1 1.7 fusion.135
  250.3 1.7 fusion.135
  262.7 1.7 fusion.135
  275.1 1.7 fusion.135
  281.2 97.4 %all-gather.3 = f32[256,128]{1,0:T(8,128)S(1)} all-gather(f32[16,128]{1,0:T(8,128)S(1)} %get-tuple-element.489), channel_id=5, replica_groups=mesh['parts'=2,'tm'=16] {'tm'}, dimensions={0}, use_global_device_ids=true | all-gather | bytes 139264 | tf_op jit(solution)/shard_map/all_gather | solution.py:13
  378.6 44.5 %while.84 = (s32[]{:T(128)}, f32[16,128]{1,0:T(8,128)S(1)}, s32[]{:T(128)}, f32[16,16,128,128]{3,2,1,0:T(8,128)}, f32[16,16,128]{2,1,0:T(8,128)S(1)}, /*index=5*/s32[]{:T(128)}, s32[]{:T(128)}, s32[]{:T(128)}, s32[]{:T(128)}) while((s32[]{:T(128)}, f32[16,128]{1,0:T(8,128)S(1)}, s32[]{:T(128)}, f32[16,16,128,128]{3,2,1,0:T(8,128)}, ...), condition=%wide.region_9.10_spmd, body=%wide.region_8.9_spmd.sunk | while | flops 3147782 | bytes 1089683 | solution.py:22
  378.6 2.9 fusion.118
  381.6 3.0 fusion.118
  384.6 3.0 fusion.118
  387.5 3.0 fusion.118
  390.5 3.0 fusion.118
  393.5 3.0 fusion.118
  396.4 3.0 fusion.118
  399.4 3.0 fusion.118
  402.4 3.0 fusion.118
  405.3 3.0 fusion.118
  408.3 3.0 fusion.118
  411.3 3.0 fusion.118
  414.2 3.0 fusion.118
  417.2 3.0 fusion.118
  420.2 3.0 fusion.118
  423.2 55.5 %while.85 = (s32[]{:T(128)}, f32[16,128]{1,0:T(8,128)S(1)}, f32[8,16,128]{2,1,0:T(8,128)S(1)}, pred[8]{0:T(512)(128)(4,1)S(1)}, pred[8]{0:T(512)(128)(4,1)S(1)},...) while((s32[]{:T(128)}, f32[16,128]{1,0:T(8,128)S(1)}, ...), condition=%wide.region_11.12_spmd, body=%wide.region_10.11_spmd.sunk | while | flops 6299651 | bytes 2211976 | solution.py:91
  423.2 1.7 fusion.123
  430.1 1.7 fusion.123
  437.1 1.7 fusion.123
  444.0 1.7 fusion.123
  450.9 1.7 fusion.123
  457.9 1.7 fusion.123
  464.8 1.7 fusion.123
  471.7 1.7 fusion.123
  (194 shorter events, 106.6 us)
Async XLA Ops:
  6.5 1.6 copy-start
  6.5 188.4 %all-gather.9.cloned.1.call-start = ((), (), s32[]{:S(2)}) async-start(), calls=%async_computation.1 | async-start | bytes 17825792 | tf_op jit(solution)/shard_map/all_gather | solution.py:13
  19.1 45.4 %copy-start.1 = (f32[16,128,128]{2,1,0:T(8,128)S(1)}, f32[16,128,128]{2,1,0:T(8,128)}, u32[]{:S(2)}) copy-start(f32[16,128,128]{2,1,0:T(8,128)} %param.25) | copy-start | bytes 3145732
  63.2 1.1 copy-start.2
  64.2 314.4 %all-gather.7.cloned.1.call-start = ((), (), s32[]{:S(2)}) async-start(), calls=%async_computation | async-start | bytes 17825792 | tf_op jit(solution)/shard_map/all_gather | solution.py:13
  66.7 31.4 %copy-start.3 = (f32[16,128,128]{2,1,0:T(8,128)S(1)}, f32[16,128,128]{2,1,0:T(8,128)}, u32[]{:S(2)}) copy-start(f32[16,128,128]{2,1,0:T(8,128)} %param.23) | copy-start | bytes 3145732
  195.1 0.7 copy-start.4
Sparse Core Ops, SparseCore 0:
  64.3 130.5 all-gather.8
  197.1 125.0 all-gather.6
where the time goes:
time: 489 us; the launch traced here: 486 us
  matrix products  184 us (38%)
  blocking collectives  122 us (25%)
  waiting for transfers between devices  95.8 us (20%)
  other arithmetic  39.1 us (8%)
  local copies, waits for them, and re-layouts  29.8 us (6%)
  between operations  14.3 us (3%)
    dot_general x64, matrix products, mat_vec(): return jnp.einsum('bij,bj->bi', matrix, vector, precision=highest)  149 us
    all_gather x2, blocking collectives, carried_in(): gathered = jax.tree.map(lambda a: lax.all_gather(a, axis), part)  122 us
    all_gather x2, waiting for transfers between devices, carried_in(): gathered = jax.tree.map(lambda a: lax.all_gather(a, axis), part)  95.8 us
    dot_general x17, matrix products, mat_mul(): return jnp.einsum('bij,bjk->bik', left, right, precision=highest)  32 us
    dynamic_slice x40, local copies, waits for them, and re-layouts, shards(): lax.scan(forward, entry_state, (step_mats, gain_terms, alive_slot))  26.3 us
    select_n x16, other arithmetic, backward(): next_state = jnp.where(is_alive, result, later_state)  16.5 us
    dynamic_update_slice x16, other arithmetic, shards(): lax.scan(forward, entry_state, (step_mats, gain_terms, alive_slot))  16.3 us
  transfers between devices with their start and end apart: 2, of which 1 were waited for; matrix products, arithmetic and copies ran while one was open for 20% of the time, Pallas kernels for 0%

commit v1 on v0

v1 whole, which is shorter than its diff:
```python
import functools

import jax
import jax.numpy as jnp
from jax import lax
from jax.experimental import pallas as pl
from jax.experimental.pallas import tpu as pltpu
from jax.sharding import PartitionSpec as P

f32 = jnp.float32
bf16 = jnp.bfloat16
LIMIT_P = 2 * 1024 * 1024
LIMIT_A = 8 * 1024 * 1024
LIMIT_B = 8 * 1024 * 1024


def halves(x):
    high = x.astype(bf16)
    return high, (x - high.astype(f32)).astype(bf16)


def left(x):
    high, low = halves(x)
    return jnp.concatenate([high, low, high], axis=1)


def right(w):
    high, low = halves(w)
    return jnp.concatenate([high, high, low], axis=0)


def dot(a, b):
    return jnp.dot(a, b, preferred_element_type=f32)


def mul(x, w):
    return dot(left(x), right(w))


def side(mats):
    return jnp.concatenate(mats, axis=1)


def below(mats):
    return jnp.concatenate(mats, axis=0)


def pick2(wide, seen, width):
    return jnp.where(seen, wide[:, width:], wide[:, :width])


def pick4(wide, first, second, width):
    return jnp.where(
        first,
        pick2(wide[:, 2 * width :], second, width),
        pick2(wide[:, : 2 * width], second, width),
    )


def shift_levels(live):
    levels = []
    unit = 1
    while unit < live:
        levels.append([unit * m for m in (1, 2, 3) if unit * m < live])
        unit *= 4
    return levels


EXCHANGED = 3


def parity(value, bits):
    total = value & 1
    for k in range(1, bits):
        total = total ^ ((value >> k) & 1)
    return total


def held_block(me, bits, rel, top):
    one = ((me >> 1) & 1) ^ ((rel >> 1) & 1)
    two = ((me >> 2) & 1) ^ ((rel >> 2) & 1)
    low = parity(me, bits) ^ (rel & 1) ^ one ^ two ^ parity(top, 8)
    return low + 2 * one + 4 * two + 8 * top


def pack_kernel(bits, x_hbm, mask_hbm, length_hbm, keep_ref, send_ref, x_ref, mask_ref, length_smem, sems):
    cap, nblocks = mask_ref.shape
    width = keep_ref.shape[1]
    tops = nblocks >> EXCHANGED
    copies = [
        pltpu.make_async_copy(src, dst, sems.at[n])
        for n, (src, dst) in enumerate(((x_hbm, x_ref), (mask_hbm, mask_ref), (length_hbm, length_smem)))
    ]
    for c in copies:
        c.start()
    for c in copies:
        c.wait()
    me = lax.axis_index("tm")
    for rel in range(1 << EXCHANGED):
        target = send_ref if rel & 1 else keep_ref
        for top in range(tops):
            row = ((rel >> 1) * tops + top) * cap
            b = held_block(me, bits, rel, top)
            target[row : row + cap] = x_ref[:, pl.ds(pl.multiple_of(b * width, width), width)]
    marks = mask_ref[...].astype(f32)
    wide = jnp.concatenate([marks] * (width // nblocks), axis=1)
    lane = lax.broadcasted_iota(jnp.int32, (cap, width), 1)
    row = lax.broadcasted_iota(jnp.int32, (cap, width), 0)
    line = jnp.sum(jnp.where(lane // nblocks == row, wide, f32(0.0)), axis=0, keepdims=True)
    meta = jnp.where(row == 0, line, jnp.where(row == 1, length_smem[0].astype(f32), f32(0.0)))
    base = 4 * tops * cap
    keep_ref[base:] = meta
    send_ref[base:] = meta


def in_hbm(*arrays):
    return [pltpu.with_memory_space_constraint(a, pltpu.HBM) for a in arrays]


def in_vmem(*arrays):
    return [pltpu.with_memory_space_constraint(a, pltpu.VMEM) for a in arrays]


def pack(bits, observations, outage_mask, group_length, width):
    cap, nblocks = outage_mask.shape
    rows = nblocks * cap // 2 + 8
    vmem = pl.BlockSpec(memory_space=pltpu.VMEM)
    return pl.pallas_call(
        functools.partial(pack_kernel, bits),
        out_shape=[pltpu.VMEM((rows, width), f32)] * 2,
        in_specs=[pl.BlockSpec(memory_space=pltpu.HBM)] * 2 + [pl.BlockSpec(memory_space=pl.ANY)],
        out_specs=[vmem] * 2,
        scratch_shapes=[
            pltpu.VMEM(observations.shape, f32),
            pltpu.VMEM(outage_mask.shape, jnp.int32),
            pltpu.SMEM((1,), jnp.int32),
            pltpu.SemaphoreType.DMA((3,)),
        ],
        compiler_params=pltpu.CompilerParams(vmem_limit_bytes=LIMIT_P),
        name="pack",
    )(*in_hbm(observations, outage_mask), group_length)


def local(kernel, shapes, name, *arrays):
    vmem = pl.BlockSpec(memory_space=pltpu.VMEM)
    return pl.pallas_call(
        kernel,
        out_shape=[pltpu.VMEM(shape, f32) for shape in shapes],
        in_specs=[vmem] * len(arrays),
        out_specs=[vmem] * len(shapes),
        compiler_params=pltpu.CompilerParams(vmem_limit_bytes=LIMIT_P),
        name=name,
    )(*in_vmem(*arrays))


def deal_kernel(keep_ref, other_ref, *outs):
    half = (outs[0].shape[0] - 8) // 2
    near = 4 * half
    for k, out in enumerate(outs):
        out[:half] = keep_ref[k * half : (k + 1) * half]
        out[half : 2 * half] = other_ref[k * half : (k + 1) * half]
        row = lax.broadcasted_iota(jnp.int32, (8, out.shape[1]), 0)
        shifted = pltpu.roll(other_ref[near : near + 8], 2, 0)
        out[2 * half :] = jnp.where(row < 2, keep_ref[near : near + 8], shifted)


def join_kernel(*refs):
    rows = refs[0].shape[0]
    for n, ref in enumerate(refs[:-1]):
        refs[-1][n * rows : (n + 1) * rows] = ref[...]


def split_kernel(stay_ref, came_ref, *outs):
    half = outs[0].shape[0] // 2
    for k, out in enumerate(outs):
        out[:half] = stay_ref[k * half : (k + 1) * half]
        out[half:] = came_ref[k * half : (k + 1) * half]


def place_kernel(bits, *refs):
    out_ref = refs[-1]
    cap = out_ref.shape[0]
    width = refs[0].shape[1]
    tops = refs[0].shape[0] // (2 * cap)
    me = lax.axis_index("tm")
    for rel in range(1 << EXCHANGED):
        for top in range(tops):
            row = ((rel & 1) * tops + top) * cap
            b = held_block(me, bits, rel, top)
            out_ref[:, pl.ds(pl.multiple_of(b * width, width), width)] = refs[rel >> 1][row : row + cap]


def place(bits, shape, *arrays):
    vmem = pl.BlockSpec(memory_space=pltpu.VMEM)
    return pl.pallas_call(
        functools.partial(place_kernel, bits),
        out_shape=jax.ShapeDtypeStruct(shape, f32),
        in_specs=[vmem] * len(arrays),
        out_specs=vmem,
        compiler_params=pltpu.CompilerParams(vmem_limit_bytes=LIMIT_P),
        name="place",
    )(*in_vmem(*arrays))


def model_kernel(
    blocks_of,
    live,
    t_hbm,
    k_hbm,
    s_hbm,
    gain_ref,
    step_ref,
    pair_ref,
    rowprod_ref,
    colprod_ref,
    back_ref,
    power_ref,
    t_ref,
    k_ref,
    s_ref,
    sems,
):
    nb, width = t_ref.shape[0], t_ref.shape[1]
    levels = shift_levels(live)
    copies = []
    for j, b in enumerate(blocks_of()):
        for n, (src, dst) in enumerate(((t_hbm, t_ref), (k_hbm, k_ref), (s_hbm, s_ref))):
            copies.append(pltpu.make_async_copy(src.at[b], dst.at[j], sems.at[j, n]))
    for c in copies:
        c.start()
    for c in copies:
        c.wait()
    eye = (
        lax.broadcasted_iota(jnp.int32, (width, width), 0)
        == lax.broadcasted_iota(jnp.int32, (width, width), 1)
    ).astype(f32)

    for j in range(nb):
        t = t_ref[j]
        k = k_ref[j]
        rt = t.T
        rg = s_ref[j].T
        gain_ref[j] = right(k)
        ru = rt - dot(left(rt), gain_ref[j])
        u = t - mul(k, t)
        step_ref[j] = right(side([rt, ru]))
        row2 = dot(left(below([rt, ru])), step_ref[j])
        row2 = [row2[a * width : (a + 1) * width, b * width : (b + 1) * width] for a in (0, 1) for b in (0, 1)]
        col2 = mul(below([t, u]), side([t, u]))
        col2 = [col2[b * width : (b + 1) * width, a * width : (a + 1) * width] for a in (0, 1) for b in (0, 1)]
        pair_ref[j] = right(side(row2))
        row4 = dot(left(below(row2)), pair_ref[j])
        col4 = mul(below(col2), side(col2))
        for p in range(4):
            for q in range(4):
                rowprod_ref[j, 4 * p + q] = row4[p * width : (p + 1) * width, q * width : (q + 1) * width]
                colprod_ref[j, 4 * p + q] = col4[q * width : (q + 1) * width, p * width : (p + 1) * width]
        back_ref[j] = right(eye - mul(rt, rg))
        power = rg
        for n, level in enumerate(levels):
            rights = [right(power)]
            if len(level) > 1:
                second = dot(left(power), rights[0])
                rights.append(right(second))
                both = dot(left(second), side(rights))
                rights.append(right(both[:, :width]))
                power = both[:, width:]
            for m in range(len(level)):
                power_ref[j, n, m * 3 * width : (m + 1) * 3 * width] = rights[m]


def prepare(blocks_of, nb, live, transition, filter_gain, smoother_gain):
    width = transition.shape[1]
    levels = shift_levels(live)
    hbm = pl.BlockSpec(memory_space=pltpu.HBM)
    vmem = pl.BlockSpec(memory_space=pltpu.VMEM)
    return pl.pallas_call(
        functools.partial(model_kernel, blocks_of, live),
        out_shape=[
            pltpu.VMEM((nb, 3 * width, width), bf16),
            pltpu.VMEM((nb, 3 * width, 2 * width), bf16),
            pltpu.VMEM((nb, 3 * width, 4 * width), bf16),
            pltpu.VMEM((nb, 16, width, width), f32),
            pltpu.VMEM((nb, 16, width, width), f32),
            pltpu.VMEM((nb, 3 * width, width), bf16),
            pltpu.VMEM((nb, len(levels), 9 * width, width), bf16),
        ],
        in_specs=[hbm] * 3,
        out_specs=[vmem] * 7,
        scratch_shapes=[
            pltpu.VMEM((nb, width, width), f32),
            pltpu.VMEM((nb, width, width), f32),
            pltpu.VMEM((nb, width, width), f32),
            pltpu.SemaphoreType.DMA((nb, 3)),
        ],
        compiler_params=pltpu.CompilerParams(vmem_limit_bytes=LIMIT_A),
        cost_estimate=pl.CostEstimate(flops=10**9, bytes_accessed=4 * 10**6, transcendentals=0),
        name="prepare",
    )(*in_hbm(transition, filter_gain, smoother_gain))


def smoother_kernel(
    bits,
    blocks_of,
    live,
    held_ref,
    arrived_ref,
    prior_ref,
    k_ref,
    step_ref,
    pair_ref,
    rowprod_ref,
    colprod_ref,
    back_ref,
    power_ref,
    stay_ref,
    leave_ref,
    gain_ref,
    seen_ref,
    col_ref,
    colgain_ref,
    start_ref,
    filt_ref,
    bits_smem,
    starts_smem,
    y_ref,
    meta_ref,
    meta_smem,
    meta_sem,
):
    nb, width = gain_ref.shape[0], y_ref.shape[2]
    nblocks = prior_ref.shape[0]
    groups = 2 * y_ref.shape[0]
    cap = stay_ref.shape[0] // (4 * nb)
    meta_row = 2 * nb * cap
    nchunks = live // 4
    levels = shift_levels(live)
    blocks = blocks_of()
    me = lax.axis_index("tm")

    count = held_ref.shape[0]
    y_ref[:count] = held_ref[...]
    y_ref[count:] = arrived_ref[...]
    meta_ref[...] = y_ref[:, meta_row:].astype(jnp.int32)
    fetch = pltpu.make_async_copy(meta_ref, meta_smem, meta_sem)
    fetch.start()
    fetch.wait()

    places = [((me ^ g) >> 1, parity(me ^ g, bits)) for g in range(groups)]
    starts = [0]
    for g in range(groups):
        starts_smem[g] = starts[g]
        starts.append(starts[-1] + meta_smem[places[g][0], 2 * places[g][1] + 1, 0])
    for j, b in enumerate(blocks):
        for g in range(groups):
            for s in range(cap):
                bits_smem[j, starts[g] + s] = meta_smem[places[g][0], 2 * places[g][1], s * nblocks + b]

    ones = jnp.ones((width, width), bf16)
    lanes = lax.broadcasted_iota(jnp.int32, (cap, width), 1)
    rows = lax.broadcasted_iota(jnp.int32, (cap, width), 0)
    for j, b in enumerate(blocks):
        readings = below(
            [y_ref[pk, pl.ds(pl.multiple_of((near * nb + j) * cap, cap), cap), :] for pk, near in places]
        )
        gains = dot(left(readings), k_ref[j])
        chosen = lanes == rows * nblocks + b
        marks = below(
            [
                jnp.where(
                    chosen,
                    jnp.broadcast_to(y_ref[pk, pl.ds(meta_row + 2 * near, 1), :], (cap, width)),
                    f32(0.0),
                )
                for pk, near in places
            ]
        )
        seen = dot(marks.astype(bf16), ones)
        gains = jnp.where(seen > 0.5, gains, f32(0.0))
        for g in range(groups):
            gain_ref[j, pl.ds(starts[g], cap), :] = gains[g * cap : (g + 1) * cap]
            seen_ref[j, pl.ds(starts[g], cap), :] = seen[g * cap : (g + 1) * cap]

    gain = [[gain_ref[j, pl.ds(s, nchunks, stride=4), :] for s in range(4)] for j in range(nb)]
    seen = [[seen_ref[j, pl.ds(s, nchunks, stride=4), :] > 0.5 for s in range(4)] for j in range(nb)]
    twos = []
    for j in range(nb):
        first = pick2(dot(left(gain[j][0]), step_ref[j]), seen[j][1], width) + gain[j][1]
        last = pick2(dot(left(gain[j][2]), step_ref[j]), seen[j][3], width) + gain[j][3]
        four = pick4(dot(left(first), pair_ref[j]), seen[j][2], seen[j][3], width) + last
        twos.append(first)
        filt_ref[j, :nchunks] = four
        pad = -nchunks % width
        padded = below([four, jnp.zeros((pad, width), f32)]) if pad else four
        for n in range(padded.shape[0] // width):
            colgain_ref[j, n] = padded[n * width : (n + 1) * width].T
        start_ref[j, pl.ds(0, 1), :] = prior_ref[pl.ds(blocks[j], 1), :]

    lane_full = lax.broadcasted_iota(jnp.int32, (width, width), 1)

    def pattern(j, c):
        o = [bits_smem[j, 4 * c + s] for s in range(4)]
        return ((o[0] * 2 + o[1]) * 2 + o[2]) * 2 + o[3]

    def two_steps(i, state):
        moved = []
        c = 2 * i
        part = c // width
        lane = c - part * width
        here = lane_full == lane
        for j in range(nb):
            prod = colprod_ref[j, pattern(j, c)] * state[j]
            prod = prod + jnp.where(here, colgain_ref[j, part], f32(0.0))
            column = jnp.broadcast_to(jnp.sum(prod, axis=1, keepdims=True), (width, width))
            pltpu.store(col_ref.at[j, part], column, mask=here)
            row = jnp.sum(rowprod_ref[j, pattern(j, c + 1)] * column, axis=0, keepdims=True)
            row = row + filt_ref[j, pl.ds(c + 1, 1), :]
            start_ref[j, pl.ds(c + 2, 1), :] = row
            moved.append(row)
        return tuple(moved)

    lax.fori_loop(0, nchunks // 2, two_steps, tuple(prior_ref[pl.ds(b, 1), :] for b in blocks))

    for j in range(nb):
        for n in range(col_ref.shape[1]):
            count = min(width, nchunks - n * width) // 2
            flipped = col_ref[j, n].T
            col_ref[j, n] = flipped
            start_ref[j, pl.ds(n * width + 1, count, stride=2), :] = col_ref[j, n, pl.ds(0, count, stride=2), :]
        begin = start_ref[j, :nchunks]
        lefts = left(begin)
        one = pick2(dot(lefts, step_ref[j]), seen[j][0], width) + gain[j][0]
        two = pick4(dot(lefts, pair_ref[j]), seen[j][0], seen[j][1], width) + twos[j]
        three = pick2(dot(left(two), step_ref[j]), seen[j][2], width) + gain[j][2]
        four = start_ref[j, 1 : nchunks + 1]
        for s, value in enumerate((one, two, three, four)):
            filt_ref[j, pl.ds(s, nchunks, stride=4), :] = value
    for j in range(nb):
        tail = filt_ref.shape[1] - live
        filtered = filt_ref[j, :live]
        smoothed = dot(left(filtered), back_ref[j])
        is_last = lax.broadcasted_iota(jnp.int32, (live, width), 0) == live - 1
        smoothed = jnp.where(is_last, filtered, smoothed)
        filt_ref[j, live:] = jnp.zeros((tail, width), f32)
        for n, level in enumerate(levels):
            filt_ref[j, :live] = smoothed
            moved = side([left(filt_ref[j, sh : sh + live]) for sh in level])
            smoothed = smoothed + dot(moved, power_ref[j, n, : 3 * width * len(level)])
        filt_ref[j, :live] = smoothed
        for d in range(1 << EXCHANGED):
            near = parity(d, EXCHANGED)
            value = filt_ref[j, pl.ds(starts_smem[me ^ d], cap), :]
            value = jnp.where(rows < meta_smem[d >> 1, 2 * near + 1, 0], value, f32(0.0))
            row = ((d >> 1) * nb + j) * cap
            (leave_ref if near else stay_ref)[row : row + cap] = value


def smooth(bits, blocks_of, nb, cap, live, held, arrived, prior, model):
    packages = 2 * held.shape[0]
    rows, width = held.shape[1:]
    nchunks = live // 4
    levels = shift_levels(live)
    parts = -(-nchunks // width)
    vmem = pl.BlockSpec(memory_space=pltpu.VMEM)
    tail = max(max(level) for level in levels) + cap
    return pl.pallas_call(
        functools.partial(smoother_kernel, bits, blocks_of, live),
        out_shape=[pltpu.VMEM((4 * nb * cap, width), f32)] * 2,
        in_specs=[vmem] * 10,
        out_specs=[vmem] * 2,
        scratch_shapes=[
            pltpu.VMEM((nb, live + cap, width), f32),
            pltpu.VMEM((nb, live + cap, width), f32),
            pltpu.VMEM((nb, parts, width, width), f32),
            pltpu.VMEM((nb, parts, width, width), f32),
            pltpu.VMEM((nb, nchunks + cap, width), f32),
            pltpu.VMEM((nb, live + tail, width), f32),
            pltpu.SMEM((nb, live + cap), jnp.int32),
            pltpu.SMEM((2 * packages,), jnp.int32),
            pltpu.VMEM((packages, rows, width), f32),
            pltpu.VMEM((packages, 8, width), jnp.int32),
            pltpu.SMEM((packages, 8, width), jnp.int32),
            pltpu.SemaphoreType.DMA,
        ],
        compiler_params=pltpu.CompilerParams(vmem_limit_bytes=LIMIT_B),
        name="smooth",
    )(*in_vmem(held, arrived), prior, *in_vmem(*model))


def permuted(x, mask):
    count = lax.axis_size("tm")
    return lax.ppermute(x, "tm", [(i, i ^ mask) for i in range(count)])


def shards(observations, outage_mask, group_length, prior_mean, transition, filter_gain, smoother_gain):
    cap = observations.shape[0]
    nblocks, width = transition.shape[0], transition.shape[1]
    bits = lax.axis_size("tm").bit_length() - 1
    nb = nblocks >> EXCHANGED
    live = (cap << bits) * 3 // 4
    half = nb * cap

    def blocks_of():
        return [held_block(lax.axis_index("tm"), bits, 0, top) for top in range(nb)]

    masks = (3, 5, 6)
    model = prepare(blocks_of, nb, live, transition, filter_gain, smoother_gain)
    keep, send = pack(bits, observations, outage_mask, group_length, width)
    package = (2 * half + 8, width)
    dealt = local(deal_kernel, [package] * 4, "deal", keep, permuted(send, 1))
    crossed = [permuted(p, mask) for p, mask in zip(dealt[1:], masks)]
    (held,) = local(join_kernel, [(4 * package[0], width)], "join", dealt[0], *crossed)
    held = held.reshape(4, *package)
    arrived = permuted(held, (1 << EXCHANGED) | 1)
    for k in range(EXCHANGED + 1, bits):
        held = jnp.concatenate([held, arrived])
        arrived = permuted(held, (1 << k) | 1)
    stay, leave = smooth(bits, blocks_of, nb, cap, live, held, arrived, prior_mean.reshape(nblocks, width), model)
    split = local(split_kernel, [(2 * half, width)] * 4, "split", stay, permuted(leave, 1))
    crossed = [permuted(p, mask) for p, mask in zip(split[1:], masks)]
    return place(bits, observations.shape, split[0], *crossed)


def solution(mesh):
    placed = (
        P(("parts", "tm"), None),
        P(("parts", "tm"), None),
        P(("parts", "tm")),
        P("parts"),
        P(),
        P(),
        P(),
    )
    return jax.shard_map(
        shards, mesh=mesh, in_specs=placed, out_specs=P(("parts", "tm"), None), check_vma=False
    )
```

time: 489 us -> 33.3 us (0.07)
  matrix products: 184 us -> 0 us
  blocking collectives: 122 us -> 0 us
  waiting for transfers between devices: 95.8 us -> 9.53 us
  other arithmetic: 39.1 us -> 0 us
  local copies, waits for them, and re-layouts: 29.8 us -> 0.01 us
  between operations: 14.3 us -> 0.7 us
  Pallas kernels: 0 us -> 13.1 us
  starting transfers between devices: 0.22 us -> 9.73 us
    dot_general x82 -> x0, matrix products: 184 us -> none  [the longest x64 149 us: mat_vec(): return jnp.einsum('bij,bj->bi', matrix, vector, precision=highest)]
    all_gather x2 -> x0, blocking collectives: 122 us -> none  [carried_in(): gathered = jax.tree.map(lambda a: lax.all_gather(a, axis), part)]
    all_gather x2 -> x0, waiting for transfers between devices: 95.8 us -> none  [carried_in(): gathered = jax.tree.map(lambda a: lax.all_gather(a, axis), part)]
    dynamic_slice x56 -> x0, local copies, waits for them, and re-layouts: 26.4 us -> none  [the longest x40 26.3 us: shards(): lax.scan(forward, entry_state, (step_mats, gain_terms, alive_slot))]
    select_n x17 -> x0, other arithmetic: 21.8 us -> none  [the longest x16 16.5 us: backward(): next_state = jnp.where(is_alive, result, later_state)]
    dynamic_update_slice x16 -> x0, other arithmetic: 16.3 us -> none  [shards(): lax.scan(forward, entry_state, (step_mats, gain_terms, alive_slot))]
    pallas_call x0 -> x7, Pallas kernels: none -> 13.1 us  [the longest x1 6.37 us: smooth(): pl.pallas_call(functools.partial(smoother_kernel, bits, blocks_of, live),...]
    ppermute x0 -> x9, starting transfers between devices: none -> 9.73 us  [permuted(): return lax.ppermute(x, 'tm', [(i, i ^ mask) for i in range(count)])]
  transfers between devices with their start and end apart: 2 -> 9, of which waited for: 1 -> 7; matrix products, arithmetic and copies ran while one was open for 20% -> 0% of each run, Pallas kernels for 0% -> 15%
where the time goes in v1:
time: 33.3 us; the launch traced here: 33 us
  Pallas kernels  13.1 us (39%)
  starting transfers between devices  9.73 us (29%)
  waiting for transfers between devices  9.53 us (29%)
  between operations  0.7 us (2%)
    ppermute x9, starting transfers between devices, permuted(): return lax.ppermute(x, 'tm', [(i, i ^ mask) for i in range(count)])  9.73 us
    ppermute x9, waiting for transfers between devices, permuted(): return lax.ppermute(x, 'tm', [(i, i ^ mask) for i in range(count)])  9.53 us
    pallas_call x1, Pallas kernels, smooth(): pl.pallas_call(functools.partial(smoother_kernel, bits, blocks_of, live),...  6.37 us
    pallas_call x1, Pallas kernels, prepare(): pl.pallas_call(functools.partial(model_kernel, blocks_of, live), out_shap...  5.06 us
    pallas_call x1, Pallas kernels, pack(): pl.pallas_call(functools.partial(pack_kernel, bits), out_shape=[pltpu.VME...  0.96 us
  transfers between devices with their start and end apart: 9, of which 7 were waited for; matrix products, arithmetic and copies ran while one was open for 0% of the time, Pallas kernels for 15%

profile of v1, /device:TPU:0, one launch (start us, length us, event | category | flops | bytes accessed | tf_op | source)
XLA Modules:
  0.0 33.0 jit_solution(4936494867062082718)
XLA Ops:
  0.0 0.0 copy-start
  0.7 1.0 %pack.1 = (f32[72,128]{1,0:T(8,128)S(1)}, f32[72,128]{1,0:T(8,128)S(1)}) custom-call(f32[8,2048]{1,0:T(8,128)} %x_hbm.1, s32[8,16]{1,0:T(8,128)} %mask_hbm.1, s32[1]{0:T(128)S(6)} %copy.8.length_hbm), custom_call_target="tpu_custom_call" | custom-call | tf_op jit(solution)/shard_map/pack/pallas_call | solution.py:128
  1.6 0.5 %collective-permute-start = (f32[72,128]{1,0:T(8,128)S(1)}, f32[72,128]{1,0:T(8,128)S(1)}, u32[]{:S(2)}, u32[]{:S(2)}) collective-permute-start(f32[72,128]{1,0:T(8,128)S(1)} %get-tuple-element.25), channel_id=1, source_target_pairs={{0,1},{1,0},{2,3},{3,2},{4,5},{5,4},{6,7},{7,6},{8,9},{9,8},{10,11... | collective-permute-start | bytes 110600 | tf_op jit(solution)/shard_map/ppermute | solution.py:492
  2.2 0.9 %collective-permute-done.other_ref = f32[72,128]{1,0:T(8,128)S(1)} collective-permute-done((f32[72,128]{1,0:T(8,128)S(1)}, f32[72,128]{1,0:T(8,128)S(1)}, u32[]{:S(2)}, u32[]{:S(2)}) %collective-permute-start) | collective-permute-done | bytes 36896 | tf_op jit(solution)/shard_map/ppermute | solution.py:492
  3.0 2.6 %collective-permute-start.1 = (f32[40,128]{1,0:T(8,128)S(1)}, f32[40,128]{1,0:T(8,128)S(1)}, u32[]{:S(2)}, u32[]{:S(2)}) collective-permute-start(f32[40,128]{1,0:T(8,128)S(1)} %get-tuple-element.27), channel_id=1, source_target_pairs={{0,3},{1,2},{2,1},{3,0},{4,7},{5,6},{6,5},{7,4},{8,11},{9,10},{10,... | collective-permute-start | bytes 61448 | tf_op jit(solution)/shard_map/ppermute | solution.py:492
  5.7 1.6 %collective-permute-start.2 = (f32[40,128]{1,0:T(8,128)S(1)}, f32[40,128]{1,0:T(8,128)S(1)}, u32[]{:S(2)}, u32[]{:S(2)}) collective-permute-start(f32[40,128]{1,0:T(8,128)S(1)} %get-tuple-element.28), channel_id=1, source_target_pairs={{0,5},{1,4},{2,7},{3,6},{4,1},{5,0},{6,3},{7,2},{8,13},{9,12},{10,... | collective-permute-start | bytes 61448 | tf_op jit(solution)/shard_map/ppermute | solution.py:492
  7.3 0.0 collective-permute-start.3
  7.3 0.0 collective-permute-done.1.refs_1_
  7.3 1.7 %collective-permute-done.2.refs_2_ = f32[40,128]{1,0:T(8,128)S(1)} collective-permute-done((f32[40,128]{1,0:T(8,128)S(1)}, f32[40,128]{1,0:T(8,128)S(1)}, u32[]{:S(2)}, u32[]{:S(2)}) %collective-permute-start.2) | collective-permute-done | bytes 20512 | tf_op jit(solution)/shard_map/ppermute | solution.py:492
  8.9 3.0 %collective-permute-done.3.refs_3_ = f32[40,128]{1,0:T(8,128)S(1)} collective-permute-done((f32[40,128]{1,0:T(8,128)S(1)}, f32[40,128]{1,0:T(8,128)S(1)}, u32[]{:S(2)}, u32[]{:S(2)}) %collective-permute-start.3) | collective-permute-done | bytes 20512 | tf_op jit(solution)/shard_map/ppermute | solution.py:492
  11.9 1.2 %collective-permute-start.4 = (f32[4,40,128]{2,1,0:T(8,128)S(1)}, f32[4,40,128]{2,1,0:T(8,128)S(1)}, u32[]{:S(2)}, u32[]{:S(2)}) collective-permute-start(f32[4,40,128]{2,1,0:T(8,128)S(1)} %bitcast.2), channel_id=1, source_target_pairs={{0,9},{1,8},{2,11},{3,10},{4,13},{5,12},{6,15},{7,14},{8,1},{9,0},... | collective-permute-start | bytes 245768 | tf_op jit(solution)/shard_map/ppermute | solution.py:492
  13.1 5.1 %prepare.1 = (bf16[2,384,128]{2,1,0:T(8,128)(2,1)S(1)}, bf16[2,384,256]{2,1,0:T(8,128)(2,1)S(1)}, bf16[2,384,512]{2,1,0:T(8,128)(2,1)S(1)}, f32[2,16,128,128]{3,...) custom-call(f32[16,128,128]{2,1,0:T(8,128)} %t_hbm.1, ...), custom_call_target="tpu_custom_call" | custom-call | flops 1000000000 | bytes 4000000 | tf_op jit(solution)/shard_map/prepare/pallas_call | solution.py:277
  18.2 1.0 %collective-permute-done.4.arrived_ref = f32[4,40,128]{2,1,0:T(8,128)S(1)} collective-permute-done((f32[4,40,128]{2,1,0:T(8,128)S(1)}, f32[4,40,128]{2,1,0:T(8,128)S(1)}, u32[]{:S(2)}, u32[]{:S(2)}) %collective-permute-start.4) | collective-permute-done | bytes 81952 | tf_op jit(solution)/shard_map/ppermute | solution.py:492
  19.2 0.0 copy-done
  19.2 6.4 %smooth.1 = (f32[64,128]{1,0:T(8,128)S(1)}, f32[64,128]{1,0:T(8,128)S(1)}) custom-call(f32[4,40,128]{2,1,0:T(8,128)S(1)} %bitcast.3, f32[4,40,128]{2,1,0:T(8,128)S(1)} %collective-permute-done.4.arrived_ref, f32[16,128]{1,0:T(8,128)S(1)} %bitcast.4, bf16[2,384,128]{2,1,0:T(8,128)(2,1)S(1)} %get-tuple-element.30.k_ref, ...), custom_call_target="tpu_custom_call" | custom-call | tf_op jit(solution)/shard_map/smooth/pallas_call | solution.py:466
  25.6 0.6 %collective-permute-start.5 = (f32[64,128]{1,0:T(8,128)S(1)}, f32[64,128]{1,0:T(8,128)S(1)}, u32[]{:S(2)}, u32[]{:S(2)}) collective-permute-start(f32[64,128]{1,0:T(8,128)S(1)} %get-tuple-element.38), channel_id=1, source_target_pairs={{0,1},{1,0},{2,3},{3,2},{4,5},{5,4},{6,7},{7,6},{8,9},{9,8},{10,11... | collective-permute-start | bytes 98312 | tf_op jit(solution)/shard_map/ppermute | solution.py:492
  26.2 0.9 %collective-permute-done.5.came_ref = f32[64,128]{1,0:T(8,128)S(1)} collective-permute-done((f32[64,128]{1,0:T(8,128)S(1)}, f32[64,128]{1,0:T(8,128)S(1)}, u32[]{:S(2)}, u32[]{:S(2)}) %collective-permute-start.5) | collective-permute-done | bytes 32800 | tf_op jit(solution)/shard_map/ppermute | solution.py:492
  27.0 0.5 %collective-permute-start.6 = (f32[32,128]{1,0:T(8,128)S(1)}, f32[32,128]{1,0:T(8,128)S(1)}, u32[]{:S(2)}, u32[]{:S(2)}) collective-permute-start(f32[32,128]{1,0:T(8,128)S(1)} %get-tuple-element.40), channel_id=1, source_target_pairs={{0,3},{1,2},{2,1},{3,0},{4,7},{5,6},{6,5},{7,4},{8,11},{9,10},{10,... | collective-permute-start | bytes 49160 | tf_op jit(solution)/shard_map/ppermute | solution.py:492
  27.5 0.2 collective-permute-start.7
  27.7 2.5 %collective-permute-start.8 = (f32[32,128]{1,0:T(8,128)S(1)}, f32[32,128]{1,0:T(8,128)S(1)}, u32[]{:S(2)}, u32[]{:S(2)}) collective-permute-start(f32[32,128]{1,0:T(8,128)S(1)} %get-tuple-element.42), channel_id=1, source_target_pairs={{0,6},{1,7},{2,4},{3,5},{4,2},{5,3},{6,0},{7,1},{8,14},{9,15},{10,... | collective-permute-start | bytes 49160 | tf_op jit(solution)/shard_map/ppermute | solution.py:492
  30.3 0.0 collective-permute-done.6.refs_1_
  30.3 0.4 %collective-permute-done.7.refs_2_ = f32[32,128]{1,0:T(8,128)S(1)} collective-permute-done((f32[32,128]{1,0:T(8,128)S(1)}, f32[32,128]{1,0:T(8,128)S(1)}, u32[]{:S(2)}, u32[]{:S(2)}) %collective-permute-start.7) | collective-permute-done | bytes 16416 | tf_op jit(solution)/shard_map/ppermute | solution.py:492
  30.7 1.7 %collective-permute-done.8.refs_3_ = f32[32,128]{1,0:T(8,128)S(1)} collective-permute-done((f32[32,128]{1,0:T(8,128)S(1)}, f32[32,128]{1,0:T(8,128)S(1)}, u32[]{:S(2)}, u32[]{:S(2)}) %collective-permute-start.8) | collective-permute-done | bytes 16416 | tf_op jit(solution)/shard_map/ppermute | solution.py:492
  32.4 0.6 %place.1 = f32[8,2048]{1,0:T(8,128)} custom-call(f32[32,128]{1,0:T(8,128)S(1)} %get-tuple-element.39.refs_0_, f32[32,128]{1,0:T(8,128)S(1)} %collective-permute-done.6.refs_1_, f32[32,128]{1,0:T(8,128)S(1)} %collective-permute-done.7.refs_2_, f32[32,128]{1,0:T(8,128)S(1)} %collective-permute-done.8.refs_3_), custom_call_target="tpu_custom_call" | custom-call | tf_op jit(solution)/shard_map/place/pallas_call | solution.py:195
  (3 shorter events, 0.0 us)
Async XLA Ops:
  0.0 19.2 %copy-start = (f32[2048]{0:T(1024)S(1)}, f32[2048]{0:T(1024)}, u32[]{:S(2)}) copy-start(f32[2048]{0:T(1024)} %param.10) | copy-start | bytes 24580
  1.6 1.4 %collective-permute-start = (f32[72,128]{1,0:T(8,128)S(1)}, f32[72,128]{1,0:T(8,128)S(1)}, u32[]{:S(2)}, u32[]{:S(2)}) collective-permute-start(f32[72,128]{1,0:T(8,128)S(1)} %get-tuple-element.25), channel_id=1, source_target_pairs={{0,1},{1,0},{2,3},{3,2},{4,5},{5,4},{6,7},{7,6},{8,9},{9,8},{10,11... | collective-permute-start | bytes 110600 | tf_op jit(solution)/shard_map/ppermute | solution.py:492
  3.0 4.2 %collective-permute-start.1 = (f32[40,128]{1,0:T(8,128)S(1)}, f32[40,128]{1,0:T(8,128)S(1)}, u32[]{:S(2)}, u32[]{:S(2)}) collective-permute-start(f32[40,128]{1,0:T(8,128)S(1)} %get-tuple-element.27), channel_id=1, source_target_pairs={{0,3},{1,2},{2,1},{3,0},{4,7},{5,6},{6,5},{7,4},{8,11},{9,10},{10,... | collective-permute-start | bytes 61448 | tf_op jit(solution)/shard_map/ppermute | solution.py:492
  5.7 3.2 %collective-permute-start.2 = (f32[40,128]{1,0:T(8,128)S(1)}, f32[40,128]{1,0:T(8,128)S(1)}, u32[]{:S(2)}, u32[]{:S(2)}) collective-permute-start(f32[40,128]{1,0:T(8,128)S(1)} %get-tuple-element.28), channel_id=1, source_target_pairs={{0,5},{1,4},{2,7},{3,6},{4,1},{5,0},{6,3},{7,2},{8,13},{9,12},{10,... | collective-permute-start | bytes 61448 | tf_op jit(solution)/shard_map/ppermute | solution.py:492
  7.3 4.7 %collective-permute-start.3 = (f32[40,128]{1,0:T(8,128)S(1)}, f32[40,128]{1,0:T(8,128)S(1)}, u32[]{:S(2)}, u32[]{:S(2)}) collective-permute-start(f32[40,128]{1,0:T(8,128)S(1)} %get-tuple-element.29), channel_id=1, source_target_pairs={{0,6},{1,7},{2,4},{3,5},{4,2},{5,3},{6,0},{7,1},{8,14},{9,15},{10,... | collective-permute-start | bytes 61448 | tf_op jit(solution)/shard_map/ppermute | solution.py:492
  11.9 7.3 %collective-permute-start.4 = (f32[4,40,128]{2,1,0:T(8,128)S(1)}, f32[4,40,128]{2,1,0:T(8,128)S(1)}, u32[]{:S(2)}, u32[]{:S(2)}) collective-permute-start(f32[4,40,128]{2,1,0:T(8,128)S(1)} %bitcast.2), channel_id=1, source_target_pairs={{0,9},{1,8},{2,11},{3,10},{4,13},{5,12},{6,15},{7,14},{8,1},{9,0},... | collective-permute-start | bytes 245768 | tf_op jit(solution)/shard_map/ppermute | solution.py:492
  25.6 1.4 %collective-permute-start.5 = (f32[64,128]{1,0:T(8,128)S(1)}, f32[64,128]{1,0:T(8,128)S(1)}, u32[]{:S(2)}, u32[]{:S(2)}) collective-permute-start(f32[64,128]{1,0:T(8,128)S(1)} %get-tuple-element.38), channel_id=1, source_target_pairs={{0,1},{1,0},{2,3},{3,2},{4,5},{5,4},{6,7},{7,6},{8,9},{9,8},{10,11... | collective-permute-start | bytes 98312 | tf_op jit(solution)/shard_map/ppermute | solution.py:492
  27.0 3.2 %collective-permute-start.6 = (f32[32,128]{1,0:T(8,128)S(1)}, f32[32,128]{1,0:T(8,128)S(1)}, u32[]{:S(2)}, u32[]{:S(2)}) collective-permute-start(f32[32,128]{1,0:T(8,128)S(1)} %get-tuple-element.40), channel_id=1, source_target_pairs={{0,3},{1,2},{2,1},{3,0},{4,7},{5,6},{6,5},{7,4},{8,11},{9,10},{10,... | collective-permute-start | bytes 49160 | tf_op jit(solution)/shard_map/ppermute | solution.py:492
  27.5 3.2 %collective-permute-start.7 = (f32[32,128]{1,0:T(8,128)S(1)}, f32[32,128]{1,0:T(8,128)S(1)}, u32[]{:S(2)}, u32[]{:S(2)}) collective-permute-start(f32[32,128]{1,0:T(8,128)S(1)} %get-tuple-element.41), channel_id=1, source_target_pairs={{0,5},{1,4},{2,7},{3,6},{4,1},{5,0},{6,3},{7,2},{8,13},{9,12},{10,... | collective-permute-start | bytes 49160 | tf_op jit(solution)/shard_map/ppermute | solution.py:492
  27.7 4.6 %collective-permute-start.8 = (f32[32,128]{1,0:T(8,128)S(1)}, f32[32,128]{1,0:T(8,128)S(1)}, u32[]{:S(2)}, u32[]{:S(2)}) collective-permute-start(f32[32,128]{1,0:T(8,128)S(1)} %get-tuple-element.42), channel_id=1, source_target_pairs={{0,6},{1,7},{2,4},{3,5},{4,2},{5,3},{6,0},{7,1},{8,14},{9,15},{10,... | collective-permute-start | bytes 49160 | tf_op jit(solution)/shard_map/ppermute | solution.py:492

commit v2 on v1

--- a/solution.py
+++ b/solution.py
@@ -146,7 +146,7 @@
     return pl.pallas_call(
         kernel,
         out_shape=[pltpu.VMEM(shape, f32) for shape in shapes],
-        in_specs=[vmem] * len(arrays),
+        in_specs=[vmem if a.dtype == f32 else pl.BlockSpec(memory_space=pl.ANY) for a in arrays],
         out_specs=[vmem] * len(shapes),
         compiler_params=pltpu.CompilerParams(vmem_limit_bytes=LIMIT_P),
         name=name,
@@ -164,10 +164,12 @@
         out[2 * half :] = jnp.where(row < 2, keep_ref[near : near + 8], shifted)
 
 
-def join_kernel(*refs):
-    rows = refs[0].shape[0]
-    for n, ref in enumerate(refs[:-1]):
-        refs[-1][n * rows : (n + 1) * rows] = ref[...]
+def join_kernel(_, *refs):
+    out_ref = refs[-1]
+    rows = refs[0].shape[0] - 8
+    for k, ref in enumerate(refs[:-1]):
+        out_ref[k * rows : (k + 1) * rows] = ref[:rows]
+        out_ref[4 * rows + 4 * k : 4 * rows + 4 * k + 4] = ref[rows : rows + 4]
 
 
 def split_kernel(stay_ref, came_ref, *outs):
@@ -204,16 +206,16 @@
 
 def model_kernel(
     blocks_of,
-    live,
     t_hbm,
     k_hbm,
     s_hbm,
+    after_ref,
     gain_ref,
     step_ref,
     pair_ref,
-    rowprod_ref,
-    colprod_ref,
     back_ref,
+    row_ref,
+    col_ref,
     power_ref,
     t_ref,
     k_ref,
@@ -221,7 +223,6 @@
     sems,
 ):
     nb, width = t_ref.shape[0], t_ref.shape[1]
-    levels = shift_levels(live)
     copies = []
     for j, b in enumerate(blocks_of()):
         for n, (src, dst) in enumerate(((t_hbm, t_ref), (k_hbm, k_ref), (s_hbm, s_ref))):
@@ -234,58 +235,70 @@
         lax.broadcasted_iota(jnp.int32, (width, width), 0)
         == lax.broadcasted_iota(jnp.int32, (width, width), 1)
     ).astype(f32)
-
-    for j in range(nb):
-        t = t_ref[j]
-        k = k_ref[j]
-        rt = t.T
-        rg = s_ref[j].T
-        gain_ref[j] = right(k)
-        ru = rt - dot(left(rt), gain_ref[j])
-        u = t - mul(k, t)
-        step_ref[j] = right(side([rt, ru]))
-        row2 = dot(left(below([rt, ru])), step_ref[j])
-        row2 = [row2[a * width : (a + 1) * width, b * width : (b + 1) * width] for a in (0, 1) for b in (0, 1)]
-        col2 = mul(below([t, u]), side([t, u]))
-        col2 = [col2[b * width : (b + 1) * width, a * width : (a + 1) * width] for a in (0, 1) for b in (0, 1)]
-        pair_ref[j] = right(side(row2))
-        row4 = dot(left(below(row2)), pair_ref[j])
-        col4 = mul(below(col2), side(col2))
+    both = range(nb)
+    rt = [t_ref[j].T for j in both]
+    for j in both:
+        power_ref[j] = s_ref[j].T
+        gain_ref[j] = right(k_ref[j])
+    ru = [rt[j] - dot(left(rt[j]), gain_ref[j]) for j in both]
+    u = [t_ref[j] - mul(k_ref[j], t_ref[j]) for j in both]
+    for j in both:
+        step_ref[j] = right(side([rt[j], ru[j]]))
+    row2 = [dot(left(below([rt[j], ru[j]])), step_ref[j]) for j in both]
+    col2 = [mul(below([t_ref[j], u[j]]), side([t_ref[j], u[j]])) for j in both]
+    for j in both:
+        back_ref[j] = right(eye - mul(rt[j], power_ref[j]))
+        for a in (0, 1):
+            for b in (0, 1):
+                one, two = slice(a * width, (a + 1) * width), slice(b * width, (b + 1) * width)
+                row_ref[j, (2 * a + b) * width : (2 * a + b + 1) * width] = row2[j][one, two]
+                col_ref[j, (2 * a + b) * width : (2 * a + b + 1) * width] = col2[j][two, one]
+        pair_ref[j] = right(side([row_ref[j, n * width : (n + 1) * width] for n in range(4)]))
+
+
+def product_kernel(live, pair_ref, row_ref, col_ref, gain_ref, after_ref, rowprod_ref, colprod_ref, power_ref):
+    nb, _, width = row_ref.shape
+    levels = shift_levels(live)
+    both = range(nb)
+    power = [gain_ref[j] for j in both]
+    for j in both:
+        row4 = dot(left(row_ref[j]), pair_ref[j])
+        col4 = mul(col_ref[j], side([col_ref[j, n * width : (n + 1) * width] for n in range(4)]))
         for p in range(4):
             for q in range(4):
                 rowprod_ref[j, 4 * p + q] = row4[p * width : (p + 1) * width, q * width : (q + 1) * width]
                 colprod_ref[j, 4 * p + q] = col4[q * width : (q + 1) * width, p * width : (p + 1) * width]
-        back_ref[j] = right(eye - mul(rt, rg))
-        power = rg
-        for n, level in enumerate(levels):
-            rights = [right(power)]
-            if len(level) > 1:
-                second = dot(left(power), rights[0])
-                rights.append(right(second))
-                both = dot(left(second), side(rights))
-                rights.append(right(both[:, :width]))
-                power = both[:, width:]
+    for n, level in enumerate(levels):
+        rights = [[right(power[j])] for j in both]
+        if len(level) > 1:
+            second = [dot(left(power[j]), rights[j][0]) for j in both]
+            for j in both:
+                rights[j].append(right(second[j]))
+            double = [dot(left(second[j]), side(rights[j])) for j in both]
+            for j in both:
+                rights[j].append(right(double[j][:, :width]))
+                power[j] = double[j][:, width:]
+        for j in both:
             for m in range(len(level)):
-                power_ref[j, n, m * 3 * width : (m + 1) * 3 * width] = rights[m]
-
-
-def prepare(blocks_of, nb, live, transition, filter_gain, smoother_gain):
+                power_ref[j, n, m * 3 * width : (m + 1) * 3 * width] = rights[j][m]
+
+
+def prepare(blocks_of, nb, transition, filter_gain, smoother_gain, after):
     width = transition.shape[1]
-    levels = shift_levels(live)
     hbm = pl.BlockSpec(memory_space=pltpu.HBM)
     vmem = pl.BlockSpec(memory_space=pltpu.VMEM)
     return pl.pallas_call(
-        functools.partial(model_kernel, blocks_of, live),
+        functools.partial(model_kernel, blocks_of),
         out_shape=[
             pltpu.VMEM((nb, 3 * width, width), bf16),
             pltpu.VMEM((nb, 3 * width, 2 * width), bf16),
             pltpu.VMEM((nb, 3 * width, 4 * width), bf16),
-            pltpu.VMEM((nb, 16, width, width), f32),
-            pltpu.VMEM((nb, 16, width, width), f32),
             pltpu.VMEM((nb, 3 * width, width), bf16),
-            pltpu.VMEM((nb, len(levels), 9 * width, width), bf16),
+            pltpu.VMEM((nb, 4 * width, width), f32),
+            pltpu.VMEM((nb, 4 * width, width), f32),
+            pltpu.VMEM((nb, width, width), f32),
         ],
-        in_specs=[hbm] * 3,
+        in_specs=[hbm] * 3 + [pl.BlockSpec(memory_space=pl.ANY)],
         out_specs=[vmem] * 7,
         scratch_shapes=[
             pltpu.VMEM((nb, width, width), f32),
@@ -296,7 +309,26 @@
         compiler_params=pltpu.CompilerParams(vmem_limit_bytes=LIMIT_A),
         cost_estimate=pl.CostEstimate(flops=10**9, bytes_accessed=4 * 10**6, transcendentals=0),
         name="prepare",
-    )(*in_hbm(transition, filter_gain, smoother_gain))
+    )(*in_hbm(transition, filter_gain, smoother_gain), after)
+
+
+def products(live, pair, row2, col2, gain, after):
+    nb, _, width = row2.shape
+    levels = shift_levels(live)
+    vmem = pl.BlockSpec(memory_space=pltpu.VMEM)
+    return pl.pallas_call(
+        functools.partial(product_kernel, live),
+        out_shape=[
+            pltpu.VMEM((nb, 16, width, width), f32),
+            pltpu.VMEM((nb, 16, width, width), f32),
+            pltpu.VMEM((nb, len(levels), 9 * width, width), bf16),
+        ],
+        in_specs=[vmem] * 4 + [pl.BlockSpec(memory_space=pl.ANY)],
+        out_specs=[vmem] * 3,
+        compiler_params=pltpu.CompilerParams(vmem_limit_bytes=LIMIT_A),
+        cost_estimate=pl.CostEstimate(flops=10**9, bytes_accessed=4 * 10**6, transcendentals=0),
+        name="products",
+    )(*in_vmem(pair, row2, col2, gain), after)
 
 
 def smoother_kernel(
@@ -321,47 +353,47 @@
     colgain_ref,
     start_ref,
     filt_ref,
-    bits_smem,
     starts_smem,
     y_ref,
     meta_ref,
     meta_smem,
-    meta_sem,
+    order_ref,
+    order_smem,
+    sems,
 ):
     nb, width = gain_ref.shape[0], y_ref.shape[2]
     nblocks = prior_ref.shape[0]
-    groups = 2 * y_ref.shape[0]
+    groups = 8 * y_ref.shape[0]
     cap = stay_ref.shape[0] // (4 * nb)
-    meta_row = 2 * nb * cap
+    meta_row = 8 * nb * cap
     nchunks = live // 4
     levels = shift_levels(live)
     blocks = blocks_of()
     me = lax.axis_index("tm")
+    odd = parity(me, bits)
 
     count = held_ref.shape[0]
+    meta_ref[:count] = held_ref[:, meta_row:].astype(jnp.int32)
+    meta_ref[count:] = arrived_ref[:, meta_row:].astype(jnp.int32)
+    fetch = pltpu.make_async_copy(meta_ref, meta_smem, sems.at[0])
+    fetch.start()
     y_ref[:count] = held_ref[...]
     y_ref[count:] = arrived_ref[...]
-    meta_ref[...] = y_ref[:, meta_row:].astype(jnp.int32)
-    fetch = pltpu.make_async_copy(meta_ref, meta_smem, meta_sem)
-    fetch.start()
-    fetch.wait()
-
-    places = [((me ^ g) >> 1, parity(me ^ g, bits)) for g in range(groups)]
-    starts = [0]
+    places = []
     for g in range(groups):
-        starts_smem[g] = starts[g]
-        starts.append(starts[-1] + meta_smem[places[g][0], 2 * places[g][1] + 1, 0])
-    for j, b in enumerate(blocks):
-        for g in range(groups):
-            for s in range(cap):
-                bits_smem[j, starts[g] + s] = meta_smem[places[g][0], 2 * places[g][1], s * nblocks + b]
+        d = me ^ g
+        places.append((d >> 3, (d >> 1) & 3, odd ^ parity(g, bits)))
 
     ones = jnp.ones((width, width), bf16)
     lanes = lax.broadcasted_iota(jnp.int32, (cap, width), 1)
     rows = lax.broadcasted_iota(jnp.int32, (cap, width), 0)
+    packed = []
     for j, b in enumerate(blocks):
         readings = below(
-            [y_ref[pk, pl.ds(pl.multiple_of((near * nb + j) * cap, cap), cap), :] for pk, near in places]
+            [
+                y_ref[top, pl.ds(pl.multiple_of(((k * 2 + near) * nb + j) * cap, cap), cap), :]
+                for top, k, near in places
+            ]
         )
         gains = dot(left(readings), k_ref[j])
         chosen = lanes == rows * nblocks + b
@@ -369,38 +401,56 @@
             [
                 jnp.where(
                     chosen,
-                    jnp.broadcast_to(y_ref[pk, pl.ds(meta_row + 2 * near, 1), :], (cap, width)),
+                    jnp.broadcast_to(y_ref[top, pl.ds(meta_row + 4 * k + 2 * near, 1), :], (cap, width)),
                     f32(0.0),
                 )
-                for pk, near in places
+                for top, k, near in places
             ]
         )
         seen = dot(marks.astype(bf16), ones)
         gains = jnp.where(seen > 0.5, gains, f32(0.0))
+        packed.append((gains, seen))
+    fetch.wait()
+    starts = [0]
+    for g in range(groups):
+        top, k, near = places[g]
+        starts_smem[g] = starts[g]
+        starts.append(starts[-1] + meta_smem[top, 4 * k + 2 * near + 1, 0])
+    for j, (gains, seen) in enumerate(packed):
         for g in range(groups):
             gain_ref[j, pl.ds(starts[g], cap), :] = gains[g * cap : (g + 1) * cap]
             seen_ref[j, pl.ds(starts[g], cap), :] = seen[g * cap : (g + 1) * cap]
 
     gain = [[gain_ref[j, pl.ds(s, nchunks, stride=4), :] for s in range(4)] for j in range(nb)]
-    seen = [[seen_ref[j, pl.ds(s, nchunks, stride=4), :] > 0.5 for s in range(4)] for j in range(nb)]
-    twos = []
-    for j in range(nb):
-        first = pick2(dot(left(gain[j][0]), step_ref[j]), seen[j][1], width) + gain[j][1]
-        last = pick2(dot(left(gain[j][2]), step_ref[j]), seen[j][3], width) + gain[j][3]
-        four = pick4(dot(left(first), pair_ref[j]), seen[j][2], seen[j][3], width) + last
-        twos.append(first)
+    marks = [[seen_ref[j, pl.ds(s, nchunks, stride=4), :] for s in range(4)] for j in range(nb)]
+    for j in range(nb):
+        order = ((marks[j][0] * 2.0 + marks[j][1]) * 2.0 + marks[j][2]) * 2.0 + marks[j][3]
+        order_ref[j] = order.astype(jnp.int32)
+    fetch = pltpu.make_async_copy(order_ref, order_smem, sems.at[1])
+    fetch.start()
+    seen = [[m > 0.5 for m in marks[j]] for j in range(nb)]
+    begun = [
+        dot(left(below([gain[j][0], gain[j][2]])), step_ref[j]) for j in range(nb)
+    ]
+    twos, lasts, fours = [], [], []
+    for j in range(nb):
+        twos.append(pick2(begun[j][:nchunks], seen[j][1], width) + gain[j][1])
+        lasts.append(pick2(begun[j][nchunks:], seen[j][3], width) + gain[j][3])
+    wide = [dot(left(twos[j]), pair_ref[j]) for j in range(nb)]
+    for j in range(nb):
+        four = pick4(wide[j], seen[j][2], seen[j][3], width) + lasts[j]
         filt_ref[j, :nchunks] = four
         pad = -nchunks % width
         padded = below([four, jnp.zeros((pad, width), f32)]) if pad else four
         for n in range(padded.shape[0] // width):
             colgain_ref[j, n] = padded[n * width : (n + 1) * width].T
         start_ref[j, pl.ds(0, 1), :] = prior_ref[pl.ds(blocks[j], 1), :]
+    fetch.wait()
 
     lane_full = lax.broadcasted_iota(jnp.int32, (width, width), 1)
 
     def pattern(j, c):
-        o = [bits_smem[j, 4 * c + s] for s in range(4)]
-        return ((o[0] * 2 + o[1]) * 2 + o[2]) * 2 + o[3]
+        return order_smem[j, c, 0]
 
     def two_steps(i, state):
         moved = []
@@ -427,36 +477,42 @@
             flipped = col_ref[j, n].T
             col_ref[j, n] = flipped
             start_ref[j, pl.ds(n * width + 1, count, stride=2), :] = col_ref[j, n, pl.ds(0, count, stride=2), :]
-        begin = start_ref[j, :nchunks]
-        lefts = left(begin)
-        one = pick2(dot(lefts, step_ref[j]), seen[j][0], width) + gain[j][0]
-        two = pick4(dot(lefts, pair_ref[j]), seen[j][0], seen[j][1], width) + twos[j]
-        three = pick2(dot(left(two), step_ref[j]), seen[j][2], width) + gain[j][2]
+    lefts = [left(start_ref[j, :nchunks]) for j in range(nb)]
+    ones = [dot(lefts[j], step_ref[j]) for j in range(nb)]
+    pairs = [dot(lefts[j], pair_ref[j]) for j in range(nb)]
+    pairs = [pick4(pairs[j], seen[j][0], seen[j][1], width) + twos[j] for j in range(nb)]
+    threes = [dot(left(pairs[j]), step_ref[j]) for j in range(nb)]
+    for j in range(nb):
+        one = pick2(ones[j], seen[j][0], width) + gain[j][0]
+        three = pick2(threes[j], seen[j][2], width) + gain[j][2]
         four = start_ref[j, 1 : nchunks + 1]
-        for s, value in enumerate((one, two, three, four)):
+        for s, value in enumerate((one, pairs[j], three, four)):
             filt_ref[j, pl.ds(s, nchunks, stride=4), :] = value
-    for j in range(nb):
-        tail = filt_ref.shape[1] - live
-        filtered = filt_ref[j, :live]
-        smoothed = dot(left(filtered), back_ref[j])
-        is_last = lax.broadcasted_iota(jnp.int32, (live, width), 0) == live - 1
-        smoothed = jnp.where(is_last, filtered, smoothed)
+    is_last = lax.broadcasted_iota(jnp.int32, (live, width), 0) == live - 1
+    tail = filt_ref.shape[1] - live
+    filtered = [filt_ref[j, :live] for j in range(nb)]
+    smoothed = [jnp.where(is_last, x, dot(left(x), back_ref[j])) for j, x in enumerate(filtered)]
+    for j in range(nb):
         filt_ref[j, live:] = jnp.zeros((tail, width), f32)
-        for n, level in enumerate(levels):
-            filt_ref[j, :live] = smoothed
+    for n, level in enumerate(levels):
+        for j in range(nb):
+            filt_ref[j, :live] = smoothed[j]
+        for j in range(nb):
             moved = side([left(filt_ref[j, sh : sh + live]) for sh in level])
-            smoothed = smoothed + dot(moved, power_ref[j, n, : 3 * width * len(level)])
-        filt_ref[j, :live] = smoothed
+            smoothed[j] = smoothed[j] + dot(moved, power_ref[j, n, : 3 * width * len(level)])
+    for j in range(nb):
+        filt_ref[j, :live] = smoothed[j]
+    for j in range(nb):
         for d in range(1 << EXCHANGED):
             near = parity(d, EXCHANGED)
             value = filt_ref[j, pl.ds(starts_smem[me ^ d], cap), :]
-            value = jnp.where(rows < meta_smem[d >> 1, 2 * near + 1, 0], value, f32(0.0))
+            value = jnp.where(rows < meta_smem[0, 4 * (d >> 1) + 2 * near + 1, 0], value, f32(0.0))
             row = ((d >> 1) * nb + j) * cap
             (leave_ref if near else stay_ref)[row : row + cap] = value
 
 
 def smooth(bits, blocks_of, nb, cap, live, held, arrived, prior, model):
-    packages = 2 * held.shape[0]
+    tops = 2 * held.shape[0]
     rows, width = held.shape[1:]
     nchunks = live // 4
     levels = shift_levels(live)
@@ -475,12 +531,13 @@
             pltpu.VMEM((nb, parts, width, width), f32),
             pltpu.VMEM((nb, nchunks + cap, width), f32),
             pltpu.VMEM((nb, live + tail, width), f32),
-            pltpu.SMEM((nb, live + cap), jnp.int32),
-            pltpu.SMEM((2 * packages,), jnp.int32),
-            pltpu.VMEM((packages, rows, width), f32),
-            pltpu.VMEM((packages, 8, width), jnp.int32),
-            pltpu.SMEM((packages, 8, width), jnp.int32),
-            pltpu.SemaphoreType.DMA,
+            pltpu.SMEM((8 * tops,), jnp.int32),
+            pltpu.VMEM((tops, rows, width), f32),
+            pltpu.VMEM((tops, 16, width), jnp.int32),
+            pltpu.SMEM((tops, 16, width), jnp.int32),
+            pltpu.VMEM((nb, nchunks, width), jnp.int32),
+            pltpu.SMEM((nb, nchunks, width), jnp.int32),
+            pltpu.SemaphoreType.DMA((2,)),
         ],
         compiler_params=pltpu.CompilerParams(vmem_limit_bytes=LIMIT_B),
         name="smooth",
@@ -504,17 +561,22 @@
         return [held_block(lax.axis_index("tm"), bits, 0, top) for top in range(nb)]
 
     masks = (3, 5, 6)
-    model = prepare(blocks_of, nb, live, transition, filter_gain, smoother_gain)
     keep, send = pack(bits, observations, outage_mask, group_length, width)
     package = (2 * half + 8, width)
     dealt = local(deal_kernel, [package] * 4, "deal", keep, permuted(send, 1))
     crossed = [permuted(p, mask) for p, mask in zip(dealt[1:], masks)]
-    (held,) = local(join_kernel, [(4 * package[0], width)], "join", dealt[0], *crossed)
-    held = held.reshape(4, *package)
+    joined = (8 * half + 16, width)
+    gain, step, pair, back, row2, col2, power = prepare(
+        blocks_of, nb, transition, filter_gain, smoother_gain, dealt[0]
+    )
+    (held,) = local(join_kernel, [joined], "join", gain, dealt[0], *crossed)
+    held = held.reshape(1, *joined)
     arrived = permuted(held, (1 << EXCHANGED) | 1)
     for k in range(EXCHANGED + 1, bits):
         held = jnp.concatenate([held, arrived])
         arrived = permuted(held, (1 << k) | 1)
+    rowprod, colprod, powers = products(live, pair, row2, col2, power, held)
+    model = [gain, step, pair, rowprod, colprod, back, powers]
     stay, leave = smooth(bits, blocks_of, nb, cap, live, held, arrived, prior_mean.reshape(nblocks, width), model)
     split = local(split_kernel, [(2 * half, width)] * 4, "split", stay, permuted(leave, 1))
     crossed = [permuted(p, mask) for p, mask in zip(split[1:], masks)]

time: 33.3 us -> 31.2 us (0.937)
  Pallas kernels: 13.1 us -> 10.8 us
  waiting for transfers between devices: 9.53 us -> 10.1 us
  starting transfers between devices: 9.73 us -> 9.33 us
    pallas_call x1, Pallas kernels: 6.37 us -> 5.11 us  [smooth(): pl.pallas_call(functools.partial(smoother_kernel, bits, blocks_of, live),...]
    pallas_call x1 -> x2, Pallas kernels: 5.06 us -> 4.09 us  [the longest x1 2.28 us: products(): pl.pallas_call(functools.partial(product_kernel, live), out_shape=[pltpu....]
    ppermute x9, waiting for transfers between devices: 9.53 us -> 10.1 us  [permuted(): return lax.ppermute(x, 'tm', [(i, i ^ mask) for i in range(count)])]
    ppermute x9, starting transfers between devices: 9.73 us -> 9.33 us  [permuted(): return lax.ppermute(x, 'tm', [(i, i ^ mask) for i in range(count)])]
  transfers between devices with their start and end apart: 9 -> 9, of which waited for: 7 -> 6; matrix products, arithmetic and copies ran while one was open for 0% -> 0% of each run, Pallas kernels for 15% -> 13%
where the time goes in v2:
time: 31.2 us; the launch traced here: 31 us
  Pallas kernels  10.8 us (35%)
  waiting for transfers between devices  10.1 us (32%)
  starting transfers between devices  9.33 us (30%)
  between operations  0.72 us (2%)
    ppermute x9, waiting for transfers between devices, permuted(): return lax.ppermute(x, 'tm', [(i, i ^ mask) for i in range(count)])  10.1 us
    ppermute x9, starting transfers between devices, permuted(): return lax.ppermute(x, 'tm', [(i, i ^ mask) for i in range(count)])  9.33 us
    pallas_call x1, Pallas kernels, smooth(): pl.pallas_call(functools.partial(smoother_kernel, bits, blocks_of, live),...  5.11 us
    pallas_call x1, Pallas kernels, products(): pl.pallas_call(functools.partial(product_kernel, live), out_shape=[pltpu....  2.28 us
    pallas_call x1, Pallas kernels, prepare(): pl.pallas_call(functools.partial(model_kernel, blocks_of), out_shape=[plt...  1.82 us
    pallas_call x1, Pallas kernels, pack(): pl.pallas_call(functools.partial(pack_kernel, bits), out_shape=[pltpu.VME...  0.96 us
    pallas_call x1, Pallas kernels, place(): pl.pallas_call(functools.partial(place_kernel, bits), out_shape=jax.Shape...  0.64 us
  transfers between devices with their start and end apart: 9, of which 6 were waited for; matrix products, arithmetic and copies ran while one was open for 0% of the time, Pallas kernels for 13%

profile of v2, /device:TPU:0, one launch (start us, length us, event | category | flops | bytes accessed | tf_op | source)
XLA Modules:
  0.0 31.0 jit_solution(16809597351814611694)
XLA Ops:
  0.7 1.0 %pack.1 = (f32[72,128]{1,0:T(8,128)S(1)}, f32[72,128]{1,0:T(8,128)S(1)}) custom-call(f32[8,2048]{1,0:T(8,128)} %x_hbm.1, s32[8,16]{1,0:T(8,128)} %mask_hbm.1, s32[1]{0:T(128)S(6)} %copy.8.length_hbm), custom_call_target="tpu_custom_call" | custom-call | tf_op jit(solution)/shard_map/pack/pallas_call | solution.py:128
  1.6 0.5 %collective-permute-start = (f32[72,128]{1,0:T(8,128)S(1)}, f32[72,128]{1,0:T(8,128)S(1)}, u32[]{:S(2)}, u32[]{:S(2)}) collective-permute-start(f32[72,128]{1,0:T(8,128)S(1)} %get-tuple-element.28), channel_id=1, source_target_pairs={{0,1},{1,0},{2,3},{3,2},{4,5},{5,4},{6,7},{7,6},{8,9},{9,8},{10,11... | collective-permute-start | bytes 110600 | tf_op jit(solution)/shard_map/ppermute | solution.py:549
  2.1 0.9 %collective-permute-done.other_ref = f32[72,128]{1,0:T(8,128)S(1)} collective-permute-done((f32[72,128]{1,0:T(8,128)S(1)}, f32[72,128]{1,0:T(8,128)S(1)}, u32[]{:S(2)}, u32[]{:S(2)}) %collective-permute-start) | collective-permute-done | bytes 36896 | tf_op jit(solution)/shard_map/ppermute | solution.py:549
  3.0 2.6 %collective-permute-start.1 = (f32[40,128]{1,0:T(8,128)S(1)}, f32[40,128]{1,0:T(8,128)S(1)}, u32[]{:S(2)}, u32[]{:S(2)}) collective-permute-start(f32[40,128]{1,0:T(8,128)S(1)} %get-tuple-element.31), channel_id=1, source_target_pairs={{0,3},{1,2},{2,1},{3,0},{4,7},{5,6},{6,5},{7,4},{8,11},{9,10},{10,... | collective-permute-start | bytes 61448 | tf_op jit(solution)/shard_map/ppermute | solution.py:549
  5.7 1.6 %collective-permute-start.2 = (f32[40,128]{1,0:T(8,128)S(1)}, f32[40,128]{1,0:T(8,128)S(1)}, u32[]{:S(2)}, u32[]{:S(2)}) collective-permute-start(f32[40,128]{1,0:T(8,128)S(1)} %get-tuple-element.32), channel_id=1, source_target_pairs={{0,5},{1,4},{2,7},{3,6},{4,1},{5,0},{6,3},{7,2},{8,13},{9,12},{10,... | collective-permute-start | bytes 61448 | tf_op jit(solution)/shard_map/ppermute | solution.py:549
  7.2 0.0 collective-permute-start.3
  7.2 1.8 %prepare.1 = (bf16[2,384,128]{2,1,0:T(8,128)(2,1)S(1)}, bf16[2,384,256]{2,1,0:T(8,128)(2,1)S(1)}, bf16[2,384,512]{2,1,0:T(8,128)(2,1)S(1)}, bf16[2,384,128]{2,1,...) custom-call(f32[16,128,128]{2,1,0:T(8,128)} %t_hbm.1, ...), custom_call_target="tpu_custom_call" | custom-call | flops 1000000000 | bytes 4000000 | tf_op jit(solution)/shard_map/prepare/pallas_call | solution.py:290
  9.1 0.0 copy-start
  9.1 0.0 collective-permute-done.1.refs_1_
  9.1 0.0 collective-permute-done.2.refs_2_
  9.1 2.8 %collective-permute-done.3.refs_3_ = f32[40,128]{1,0:T(8,128)S(1)} collective-permute-done((f32[40,128]{1,0:T(8,128)S(1)}, f32[40,128]{1,0:T(8,128)S(1)}, u32[]{:S(2)}, u32[]{:S(2)}) %collective-permute-start.3) | collective-permute-done | bytes 20512 | tf_op jit(solution)/shard_map/ppermute | solution.py:549
  11.9 1.2 %collective-permute-start.4 = (f32[1,144,128]{2,1,0:T(8,128)S(1)}, f32[1,144,128]{2,1,0:T(8,128)S(1)}, u32[]{:S(2)}, u32[]{:S(2)}) collective-permute-start(f32[1,144,128]{2,1,0:T(8,128)S(1)} %bitcast.2), channel_id=1, source_target_pairs={{0,9},{1,8},{2,11},{3,10},{4,13},{5,12},{6,15},{7,14},{8,1},{9,0},... | collective-permute-start | bytes 221192 | tf_op jit(solution)/shard_map/ppermute | solution.py:549
  13.1 2.3 %products.1 = (f32[2,16,128,128]{3,2,1,0:T(8,128)S(1)}, f32[2,16,128,128]{3,2,1,0:T(8,128)S(1)}, bf16[2,4,1152,128]{3,2,1,0:T(8,128)(2,1)S(1)}) custom-call(bf16[2,384,512]{2,1,0:T(8,128)(2,1)S(1)} %get-tuple-element.35.pair_ref, f32[2,512,128]{2,1,0:T(8,128)S(1)} %get-tuple-element.36.row_ref, f32[2,512,128]{2,1,0:T(8,128)S(1)} %get-tuple-element.37.col_ref, ...), custom_call_target="tpu_custom_call" | custom-call | flops 1000000000 | bytes 4000000 | tf_op jit(solution)/shard_map/products/pallas_call | solution.py:319
  15.4 3.4 %collective-permute-done.4.arrived_ref = f32[1,144,128]{2,1,0:T(8,128)S(1)} collective-permute-done((f32[1,144,128]{2,1,0:T(8,128)S(1)}, f32[1,144,128]{2,1,0:T(8,128)S(1)}, u32[]{:S(2)}, u32[]{:S(2)}) %collective-permute-start.4) | collective-permute-done | bytes 73760 | tf_op jit(solution)/shard_map/ppermute | solution.py:549
  18.8 0.0 copy-done
  18.8 5.1 %smooth.1 = (f32[64,128]{1,0:T(8,128)S(1)}, f32[64,128]{1,0:T(8,128)S(1)}) custom-call(f32[1,144,128]{2,1,0:T(8,128)S(1)} %bitcast.4, f32[1,144,128]{2,1,0:T(8,128)S(1)} %collective-permute-done.4.arrived_ref, f32[16,128]{1,0:T(8,128)S(1)} %bitcast.5, bf16[2,384,128]{2,1,0:T(8,128)(2,1)S(1)} %get-tuple-element.30._.k_ref, ...), custom_call_target="tpu_custom_call" | custom-call | tf_op jit(solution)/shard_map/smooth/pallas_call | solution.py:522
  24.0 0.2 collective-permute-start.5
  24.1 1.1 %collective-permute-done.5.came_ref = f32[64,128]{1,0:T(8,128)S(1)} collective-permute-done((f32[64,128]{1,0:T(8,128)S(1)}, f32[64,128]{1,0:T(8,128)S(1)}, u32[]{:S(2)}, u32[]{:S(2)}) %collective-permute-start.5) | collective-permute-done | bytes 32800 | tf_op jit(solution)/shard_map/ppermute | solution.py:549
  25.2 0.1 collective-permute-start.6
  25.4 0.0 collective-permute-start.7
  25.4 3.1 %collective-permute-start.8 = (f32[32,128]{1,0:T(8,128)S(1)}, f32[32,128]{1,0:T(8,128)S(1)}, u32[]{:S(2)}, u32[]{:S(2)}) collective-permute-start(f32[32,128]{1,0:T(8,128)S(1)} %get-tuple-element.48), channel_id=1, source_target_pairs={{0,6},{1,7},{2,4},{3,5},{4,2},{5,3},{6,0},{7,1},{8,14},{9,15},{10,... | collective-permute-start | bytes 49160 | tf_op jit(solution)/shard_map/ppermute | solution.py:549
  28.5 0.0 collective-permute-done.6.refs_1_
  28.5 0.1 collective-permute-done.7.refs_2_
  28.5 1.8 %collective-permute-done.8.refs_3_ = f32[32,128]{1,0:T(8,128)S(1)} collective-permute-done((f32[32,128]{1,0:T(8,128)S(1)}, f32[32,128]{1,0:T(8,128)S(1)}, u32[]{:S(2)}, u32[]{:S(2)}) %collective-permute-start.8) | collective-permute-done | bytes 16416 | tf_op jit(solution)/shard_map/ppermute | solution.py:549
  30.3 0.6 %place.1 = f32[8,2048]{1,0:T(8,128)} custom-call(f32[32,128]{1,0:T(8,128)S(1)} %get-tuple-element.45.refs_0_, f32[32,128]{1,0:T(8,128)S(1)} %collective-permute-done.6.refs_1_, f32[32,128]{1,0:T(8,128)S(1)} %collective-permute-done.7.refs_2_, f32[32,128]{1,0:T(8,128)S(1)} %collective-permute-done.8.refs_3_), custom_call_target="tpu_custom_call" | custom-call | tf_op jit(solution)/shard_map/place/pallas_call | solution.py:197
  (3 shorter events, 0.0 us)
Async XLA Ops:
  1.6 1.4 %collective-permute-start = (f32[72,128]{1,0:T(8,128)S(1)}, f32[72,128]{1,0:T(8,128)S(1)}, u32[]{:S(2)}, u32[]{:S(2)}) collective-permute-start(f32[72,128]{1,0:T(8,128)S(1)} %get-tuple-element.28), channel_id=1, source_target_pairs={{0,1},{1,0},{2,3},{3,2},{4,5},{5,4},{6,7},{7,6},{8,9},{9,8},{10,11... | collective-permute-start | bytes 110600 | tf_op jit(solution)/shard_map/ppermute | solution.py:549
  3.0 6.1 %collective-permute-start.1 = (f32[40,128]{1,0:T(8,128)S(1)}, f32[40,128]{1,0:T(8,128)S(1)}, u32[]{:S(2)}, u32[]{:S(2)}) collective-permute-start(f32[40,128]{1,0:T(8,128)S(1)} %get-tuple-element.31), channel_id=1, source_target_pairs={{0,3},{1,2},{2,1},{3,0},{4,7},{5,6},{6,5},{7,4},{8,11},{9,10},{10,... | collective-permute-start | bytes 61448 | tf_op jit(solution)/shard_map/ppermute | solution.py:549
  5.7 3.4 %collective-permute-start.2 = (f32[40,128]{1,0:T(8,128)S(1)}, f32[40,128]{1,0:T(8,128)S(1)}, u32[]{:S(2)}, u32[]{:S(2)}) collective-permute-start(f32[40,128]{1,0:T(8,128)S(1)} %get-tuple-element.32), channel_id=1, source_target_pairs={{0,5},{1,4},{2,7},{3,6},{4,1},{5,0},{6,3},{7,2},{8,13},{9,12},{10,... | collective-permute-start | bytes 61448 | tf_op jit(solution)/shard_map/ppermute | solution.py:549
  7.2 4.7 %collective-permute-start.3 = (f32[40,128]{1,0:T(8,128)S(1)}, f32[40,128]{1,0:T(8,128)S(1)}, u32[]{:S(2)}, u32[]{:S(2)}) collective-permute-start(f32[40,128]{1,0:T(8,128)S(1)} %get-tuple-element.33), channel_id=1, source_target_pairs={{0,6},{1,7},{2,4},{3,5},{4,2},{5,3},{6,0},{7,1},{8,14},{9,15},{10,... | collective-permute-start | bytes 61448 | tf_op jit(solution)/shard_map/ppermute | solution.py:549
  9.1 9.8 %copy-start = (f32[2048]{0:T(1024)S(1)}, f32[2048]{0:T(1024)}, u32[]{:S(2)}) copy-start(f32[2048]{0:T(1024)} %param.10) | copy-start | bytes 24580
  11.9 6.9 %collective-permute-start.4 = (f32[1,144,128]{2,1,0:T(8,128)S(1)}, f32[1,144,128]{2,1,0:T(8,128)S(1)}, u32[]{:S(2)}, u32[]{:S(2)}) collective-permute-start(f32[1,144,128]{2,1,0:T(8,128)S(1)} %bitcast.2), channel_id=1, source_target_pairs={{0,9},{1,8},{2,11},{3,10},{4,13},{5,12},{6,15},{7,14},{8,1},{9,0},... | collective-permute-start | bytes 221192 | tf_op jit(solution)/shard_map/ppermute | solution.py:549
  24.0 1.3 %collective-permute-start.5 = (f32[64,128]{1,0:T(8,128)S(1)}, f32[64,128]{1,0:T(8,128)S(1)}, u32[]{:S(2)}, u32[]{:S(2)}) collective-permute-start(f32[64,128]{1,0:T(8,128)S(1)} %get-tuple-element.44), channel_id=1, source_target_pairs={{0,1},{1,0},{2,3},{3,2},{4,5},{5,4},{6,7},{7,6},{8,9},{9,8},{10,11... | collective-permute-start | bytes 98312 | tf_op jit(solution)/shard_map/ppermute | solution.py:549
  25.2 3.2 %collective-permute-start.6 = (f32[32,128]{1,0:T(8,128)S(1)}, f32[32,128]{1,0:T(8,128)S(1)}, u32[]{:S(2)}, u32[]{:S(2)}) collective-permute-start(f32[32,128]{1,0:T(8,128)S(1)} %get-tuple-element.46), channel_id=1, source_target_pairs={{0,3},{1,2},{2,1},{3,0},{4,7},{5,6},{6,5},{7,4},{8,11},{9,10},{10,... | collective-permute-start | bytes 49160 | tf_op jit(solution)/shard_map/ppermute | solution.py:549
  25.4 3.2 %collective-permute-start.7 = (f32[32,128]{1,0:T(8,128)S(1)}, f32[32,128]{1,0:T(8,128)S(1)}, u32[]{:S(2)}, u32[]{:S(2)}) collective-permute-start(f32[32,128]{1,0:T(8,128)S(1)} %get-tuple-element.47), channel_id=1, source_target_pairs={{0,5},{1,4},{2,7},{3,6},{4,1},{5,0},{6,3},{7,2},{8,13},{9,12},{10,... | collective-permute-start | bytes 49160 | tf_op jit(solution)/shard_map/ppermute | solution.py:549
  25.4 5.0 %collective-permute-start.8 = (f32[32,128]{1,0:T(8,128)S(1)}, f32[32,128]{1,0:T(8,128)S(1)}, u32[]{:S(2)}, u32[]{:S(2)}) collective-permute-start(f32[32,128]{1,0:T(8,128)S(1)} %get-tuple-element.48), channel_id=1, source_target_pairs={{0,6},{1,7},{2,4},{3,5},{4,2},{5,3},{6,0},{7,1},{8,14},{9,15},{10,... | collective-permute-start | bytes 49160 | tf_op jit(solution)/shard_map/ppermute | solution.py:549

commit v3 on v2

--- a/solution.py
+++ b/solution.py
@@ -20,17 +20,19 @@
 
 
 def left(x):
-    high, low = halves(x)
-    return jnp.concatenate([high, low, high], axis=1)
+    high = x.astype(bf16).astype(f32)
+    both = jnp.concatenate([high, x - high], axis=0).astype(bf16)
+    return jnp.concatenate([both, both], axis=1)
 
 
 def right(w):
-    high, low = halves(w)
-    return jnp.concatenate([high, high, low], axis=0)
+    return jnp.concatenate(halves(w), axis=0)
 
 
 def dot(a, b):
-    return jnp.dot(a, b, preferred_element_type=f32)
+    both = jnp.dot(a, b, preferred_element_type=f32)
+    half = both.shape[0] // 2
+    return both[:half] + both[half:]
 
 
 def mul(x, w):
@@ -67,6 +69,7 @@
 
 
 EXCHANGED = 3
+PLACED = (0, 2, 3, 1)
 
 
 def parity(value, bits):
@@ -83,85 +86,70 @@
     return low + 2 * one + 4 * two + 8 * top
 
 
-def pack_kernel(bits, x_hbm, mask_hbm, length_hbm, keep_ref, send_ref, x_ref, mask_ref, length_smem, sems):
-    cap, nblocks = mask_ref.shape
-    width = keep_ref.shape[1]
-    tops = nblocks >> EXCHANGED
+def in_hbm(*arrays):
+    return [pltpu.with_memory_space_constraint(a, pltpu.HBM) for a in arrays]
+
+
+def in_vmem(*arrays):
+    return [pltpu.with_memory_space_constraint(a, pltpu.VMEM) for a in arrays]
+
+
+def local(kernel, shapes, name, *arrays):
+    vmem = pl.BlockSpec(memory_space=pltpu.VMEM)
+    return pl.pallas_call(
+        kernel,
+        out_shape=[pltpu.VMEM(shape, f32) for shape in shapes],
+        in_specs=[vmem if a.dtype != bf16 else pl.BlockSpec(memory_space=pl.ANY) for a in arrays],
+        out_specs=[vmem] * len(shapes),
+        compiler_params=pltpu.CompilerParams(vmem_limit_bytes=LIMIT_P),
+        name=name,
+    )(*in_vmem(*arrays))
+
+
+def fetch_kernel(x_hbm, mask_hbm, x_ref, mask_ref, sems):
     copies = [
-        pltpu.make_async_copy(src, dst, sems.at[n])
-        for n, (src, dst) in enumerate(((x_hbm, x_ref), (mask_hbm, mask_ref), (length_hbm, length_smem)))
+        pltpu.make_async_copy(x_hbm, x_ref, sems.at[0]),
+        pltpu.make_async_copy(mask_hbm, mask_ref, sems.at[1]),
     ]
     for c in copies:
         c.start()
     for c in copies:
         c.wait()
+
+
+def fetch(observations, outage_mask):
+    return pl.pallas_call(
+        fetch_kernel,
+        out_shape=[pltpu.VMEM(observations.shape, f32), pltpu.VMEM(outage_mask.shape, jnp.int32)],
+        in_specs=[pl.BlockSpec(memory_space=pltpu.HBM)] * 2,
+        out_specs=[pl.BlockSpec(memory_space=pltpu.VMEM)] * 2,
+        scratch_shapes=[pltpu.SemaphoreType.DMA((2,))],
+        compiler_params=pltpu.CompilerParams(vmem_limit_bytes=LIMIT_P),
+        cost_estimate=pl.CostEstimate(flops=0, bytes_accessed=10**6, transcendentals=0),
+        name="fetch",
+    )(*in_hbm(observations, outage_mask))
+
+
+def deal_kernel(bits, x_ref, other_ref, length_ref, other_length_ref, mask_ref, other_mask_ref, *outs):
+    cap, nblocks = mask_ref.shape
+    width = length_ref.shape[1]
+    half = (outs[0].shape[0] - 8) // 2
     me = lax.axis_index("tm")
-    for rel in range(1 << EXCHANGED):
-        target = send_ref if rel & 1 else keep_ref
-        for top in range(tops):
-            row = ((rel >> 1) * tops + top) * cap
-            b = held_block(me, bits, rel, top)
-            target[row : row + cap] = x_ref[:, pl.ds(pl.multiple_of(b * width, width), width)]
-    marks = mask_ref[...].astype(f32)
-    wide = jnp.concatenate([marks] * (width // nblocks), axis=1)
     lane = lax.broadcasted_iota(jnp.int32, (cap, width), 1)
     row = lax.broadcasted_iota(jnp.int32, (cap, width), 0)
-    line = jnp.sum(jnp.where(lane // nblocks == row, wide, f32(0.0)), axis=0, keepdims=True)
-    meta = jnp.where(row == 0, line, jnp.where(row == 1, length_smem[0].astype(f32), f32(0.0)))
-    base = 4 * tops * cap
-    keep_ref[base:] = meta
-    send_ref[base:] = meta
-
-
-def in_hbm(*arrays):
-    return [pltpu.with_memory_space_constraint(a, pltpu.HBM) for a in arrays]
-
-
-def in_vmem(*arrays):
-    return [pltpu.with_memory_space_constraint(a, pltpu.VMEM) for a in arrays]
-
-
-def pack(bits, observations, outage_mask, group_length, width):
-    cap, nblocks = outage_mask.shape
-    rows = nblocks * cap // 2 + 8
-    vmem = pl.BlockSpec(memory_space=pltpu.VMEM)
-    return pl.pallas_call(
-        functools.partial(pack_kernel, bits),
-        out_shape=[pltpu.VMEM((rows, width), f32)] * 2,
-        in_specs=[pl.BlockSpec(memory_space=pltpu.HBM)] * 2 + [pl.BlockSpec(memory_space=pl.ANY)],
-        out_specs=[vmem] * 2,
-        scratch_shapes=[
-            pltpu.VMEM(observations.shape, f32),
-            pltpu.VMEM(outage_mask.shape, jnp.int32),
-            pltpu.SMEM((1,), jnp.int32),
-            pltpu.SemaphoreType.DMA((3,)),
-        ],
-        compiler_params=pltpu.CompilerParams(vmem_limit_bytes=LIMIT_P),
-        name="pack",
-    )(*in_hbm(observations, outage_mask), group_length)
-
-
-def local(kernel, shapes, name, *arrays):
-    vmem = pl.BlockSpec(memory_space=pltpu.VMEM)
-    return pl.pallas_call(
-        kernel,
-        out_shape=[pltpu.VMEM(shape, f32) for shape in shapes],
-        in_specs=[vmem if a.dtype == f32 else pl.BlockSpec(memory_space=pl.ANY) for a in arrays],
-        out_specs=[vmem] * len(shapes),
-        compiler_params=pltpu.CompilerParams(vmem_limit_bytes=LIMIT_P),
-        name=name,
-    )(*in_vmem(*arrays))
-
-
-def deal_kernel(keep_ref, other_ref, *outs):
-    half = (outs[0].shape[0] - 8) // 2
-    near = 4 * half
+    lines = []
+    for ref, length in ((mask_ref, length_ref), (other_mask_ref, other_length_ref)):
+        wide = jnp.concatenate([ref[...].astype(f32)] * (width // nblocks), axis=1)
+        lines.append(jnp.sum(jnp.where(lane // nblocks == row, wide, f32(0.0)), axis=0, keepdims=True))
+        lines.append(length[0:1])
+    meta = jnp.concatenate(lines + [jnp.zeros((4, width), f32)], axis=0)
     for k, out in enumerate(outs):
-        out[:half] = keep_ref[k * half : (k + 1) * half]
-        out[half : 2 * half] = other_ref[k * half : (k + 1) * half]
-        row = lax.broadcasted_iota(jnp.int32, (8, out.shape[1]), 0)
-        shifted = pltpu.roll(other_ref[near : near + 8], 2, 0)
-        out[2 * half :] = jnp.where(row < 2, keep_ref[near : near + 8], shifted)
+        for top in range(half // cap):
+            b = held_block(me, bits, 2 * k, top)
+            spot = pl.ds(pl.multiple_of(b * width, width), width)
+            out[top * cap : (top + 1) * cap] = x_ref[:, spot]
+            out[half + top * cap : half + (top + 1) * cap] = other_ref[:, spot]
+        out[2 * half :] = meta
 
 
 def join_kernel(_, *refs):
@@ -169,7 +157,7 @@
     rows = refs[0].shape[0] - 8
     for k, ref in enumerate(refs[:-1]):
         out_ref[k * rows : (k + 1) * rows] = ref[:rows]
-        out_ref[4 * rows + 4 * k : 4 * rows + 4 * k + 4] = ref[rows : rows + 4]
+        out_ref[3 * rows + 4 * k : 3 * rows + 4 * k + 4] = ref[rows : rows + 4]
 
 
 def split_kernel(stay_ref, came_ref, *outs):
@@ -189,7 +177,7 @@
         for top in range(tops):
             row = ((rel & 1) * tops + top) * cap
             b = held_block(me, bits, rel, top)
-            out_ref[:, pl.ds(pl.multiple_of(b * width, width), width)] = refs[rel >> 1][row : row + cap]
+            out_ref[:, pl.ds(pl.multiple_of(b * width, width), width)] = refs[PLACED.index(rel >> 1)][row : row + cap]
 
 
 def place(bits, shape, *arrays):
@@ -280,7 +268,7 @@
                 power[j] = double[j][:, width:]
         for j in both:
             for m in range(len(level)):
-                power_ref[j, n, m * 3 * width : (m + 1) * 3 * width] = rights[j][m]
+                power_ref[j, n, m * 2 * width : (m + 1) * 2 * width] = rights[j][m]
 
 
 def prepare(blocks_of, nb, transition, filter_gain, smoother_gain, after):
@@ -290,10 +278,10 @@
     return pl.pallas_call(
         functools.partial(model_kernel, blocks_of),
         out_shape=[
-            pltpu.VMEM((nb, 3 * width, width), bf16),
-            pltpu.VMEM((nb, 3 * width, 2 * width), bf16),
-            pltpu.VMEM((nb, 3 * width, 4 * width), bf16),
-            pltpu.VMEM((nb, 3 * width, width), bf16),
+            pltpu.VMEM((nb, 2 * width, width), bf16),
+            pltpu.VMEM((nb, 2 * width, 2 * width), bf16),
+            pltpu.VMEM((nb, 2 * width, 4 * width), bf16),
+            pltpu.VMEM((nb, 2 * width, width), bf16),
             pltpu.VMEM((nb, 4 * width, width), f32),
             pltpu.VMEM((nb, 4 * width, width), f32),
             pltpu.VMEM((nb, width, width), f32),
@@ -321,7 +309,7 @@
         out_shape=[
             pltpu.VMEM((nb, 16, width, width), f32),
             pltpu.VMEM((nb, 16, width, width), f32),
-            pltpu.VMEM((nb, len(levels), 9 * width, width), bf16),
+            pltpu.VMEM((nb, len(levels), 6 * width, width), bf16),
         ],
         in_specs=[vmem] * 4 + [pl.BlockSpec(memory_space=pl.ANY)],
         out_specs=[vmem] * 3,
@@ -335,8 +323,17 @@
     bits,
     blocks_of,
     live,
-    held_ref,
-    arrived_ref,
+    nsent,
+    *refs,
+):
+    smoother_body(bits, blocks_of, live, refs[:nsent], *refs[nsent:])
+
+
+def smoother_body(
+    bits,
+    blocks_of,
+    live,
+    sent_refs,
     prior_ref,
     k_ref,
     step_ref,
@@ -372,13 +369,18 @@
     me = lax.axis_index("tm")
     odd = parity(me, bits)
 
-    count = held_ref.shape[0]
-    meta_ref[:count] = held_ref[:, meta_row:].astype(jnp.int32)
-    meta_ref[count:] = arrived_ref[:, meta_row:].astype(jnp.int32)
+    part = 2 * nb * cap
+    for top in range(y_ref.shape[0]):
+        most, last = sent_refs[2 * top], sent_refs[2 * top + 1]
+        y_ref[top, meta_row : meta_row + 12] = most[3 * part : 3 * part + 12]
+        y_ref[top, meta_row + 12 :] = last[part : part + 4]
+    meta_ref[...] = y_ref[:, meta_row:].astype(jnp.int32)
     fetch = pltpu.make_async_copy(meta_ref, meta_smem, sems.at[0])
     fetch.start()
-    y_ref[:count] = held_ref[...]
-    y_ref[count:] = arrived_ref[...]
+    for top in range(y_ref.shape[0]):
+        most, last = sent_refs[2 * top], sent_refs[2 * top + 1]
+        y_ref[top, : 3 * part] = most[: 3 * part]
+        y_ref[top, 3 * part : meta_row] = last[:part]
     places = []
     for g in range(groups):
         d = me ^ g
@@ -407,7 +409,7 @@
                 for top, k, near in places
             ]
         )
-        seen = dot(marks.astype(bf16), ones)
+        seen = jnp.dot(marks.astype(bf16), ones, preferred_element_type=f32)
         gains = jnp.where(seen > 0.5, gains, f32(0.0))
         packed.append((gains, seen))
     fetch.wait()
@@ -499,7 +501,7 @@
             filt_ref[j, :live] = smoothed[j]
         for j in range(nb):
             moved = side([left(filt_ref[j, sh : sh + live]) for sh in level])
-            smoothed[j] = smoothed[j] + dot(moved, power_ref[j, n, : 3 * width * len(level)])
+            smoothed[j] = smoothed[j] + dot(moved, power_ref[j, n, : 2 * width * len(level)])
     for j in range(nb):
         filt_ref[j, :live] = smoothed[j]
     for j in range(nb):
@@ -511,18 +513,19 @@
             (leave_ref if near else stay_ref)[row : row + cap] = value
 
 
-def smooth(bits, blocks_of, nb, cap, live, held, arrived, prior, model):
-    tops = 2 * held.shape[0]
-    rows, width = held.shape[1:]
+def smooth(bits, blocks_of, nb, cap, live, sent, prior, model):
+    tops = len(sent) // 2
+    width = sent[0].shape[1]
+    rows = 8 * nb * cap + 16
     nchunks = live // 4
     levels = shift_levels(live)
     parts = -(-nchunks // width)
     vmem = pl.BlockSpec(memory_space=pltpu.VMEM)
     tail = max(max(level) for level in levels) + cap
     return pl.pallas_call(
-        functools.partial(smoother_kernel, bits, blocks_of, live),
+        functools.partial(smoother_kernel, bits, blocks_of, live, len(sent)),
         out_shape=[pltpu.VMEM((4 * nb * cap, width), f32)] * 2,
-        in_specs=[vmem] * 10,
+        in_specs=[vmem] * (len(sent) + 8),
         out_specs=[vmem] * 2,
         scratch_shapes=[
             pltpu.VMEM((nb, live + cap, width), f32),
@@ -541,7 +544,7 @@
         ],
         compiler_params=pltpu.CompilerParams(vmem_limit_bytes=LIMIT_B),
         name="smooth",
-    )(*in_vmem(held, arrived), prior, *in_vmem(*model))
+    )(*in_vmem(*sent), prior, *in_vmem(*model))
 
 
 def permuted(x, mask):
@@ -561,26 +564,34 @@
         return [held_block(lax.axis_index("tm"), bits, 0, top) for top in range(nb)]
 
     masks = (3, 5, 6)
-    keep, send = pack(bits, observations, outage_mask, group_length, width)
     package = (2 * half + 8, width)
-    dealt = local(deal_kernel, [package] * 4, "deal", keep, permuted(send, 1))
+    other = permuted(observations, 1), permuted(outage_mask, 1)
+    length = jnp.broadcast_to(group_length.astype(f32)[:, None], (8, width))
+    own = fetch(observations, outage_mask)
+    dealt = local(
+        functools.partial(deal_kernel, bits),
+        [package] * 4,
+        "deal",
+        own[0],
+        other[0],
+        length,
+        permuted(length, 1),
+        own[1],
+        other[1],
+    )
     crossed = [permuted(p, mask) for p, mask in zip(dealt[1:], masks)]
-    joined = (8 * half + 16, width)
     gain, step, pair, back, row2, col2, power = prepare(
         blocks_of, nb, transition, filter_gain, smoother_gain, dealt[0]
     )
-    (held,) = local(join_kernel, [joined], "join", gain, dealt[0], *crossed)
-    held = held.reshape(1, *joined)
-    arrived = permuted(held, (1 << EXCHANGED) | 1)
-    for k in range(EXCHANGED + 1, bits):
-        held = jnp.concatenate([held, arrived])
-        arrived = permuted(held, (1 << k) | 1)
-    rowprod, colprod, powers = products(live, pair, row2, col2, power, held)
+    sent = [*local(join_kernel, [(6 * half + 16, width)], "join", gain, dealt[0], *crossed[:2]), crossed[2]]
+    for k in range(EXCHANGED, bits):
+        sent = sent + [permuted(x, (1 << k) | 1) for x in sent]
+    rowprod, colprod, powers = products(live, pair, row2, col2, power, crossed[2])
     model = [gain, step, pair, rowprod, colprod, back, powers]
-    stay, leave = smooth(bits, blocks_of, nb, cap, live, held, arrived, prior_mean.reshape(nblocks, width), model)
+    stay, leave = smooth(bits, blocks_of, nb, cap, live, sent, prior_mean.reshape(nblocks, width), model)
     split = local(split_kernel, [(2 * half, width)] * 4, "split", stay, permuted(leave, 1))
-    crossed = [permuted(p, mask) for p, mask in zip(split[1:], masks)]
-    return place(bits, observations.shape, split[0], *crossed)
+    crossed = [split[0]] + [permuted(p, mask) for p, mask in zip(split[1:], masks)]
+    return place(bits, observations.shape, *(crossed[k] for k in PLACED))
 
 
 def solution(mesh):

time: 31.2 us -> 29.3 us (0.939)
  waiting for transfers between devices: 10.1 us -> 5.81 us
  starting transfers between devices: 9.33 us -> 11.6 us
    ppermute x9 -> x12, waiting for transfers between devices: 10.1 us -> 5.81 us  [permuted(): return lax.ppermute(x, 'tm', [(i, i ^ mask) for i in range(count)])]
    ppermute x9 -> x12, starting transfers between devices: 9.33 us -> 11.6 us  [permuted(): return lax.ppermute(x, 'tm', [(i, i ^ mask) for i in range(count)])]
  transfers between devices with their start and end apart: 9 -> 12, of which waited for: 6 -> 6; matrix products, arithmetic and copies ran while one was open for 0% -> 0% of each run, Pallas kernels for 13% -> 17%
where the time goes in v3:
time: 29.3 us; the launch traced here: 29.1 us
  starting transfers between devices  11.6 us (40%)
  Pallas kernels  11 us (38%)
  waiting for transfers between devices  5.81 us (20%)
  between operations  0.72 us (2%)
    ppermute x12, starting transfers between devices, permuted(): return lax.ppermute(x, 'tm', [(i, i ^ mask) for i in range(count)])  11.6 us
    ppermute x12, waiting for transfers between devices, permuted(): return lax.ppermute(x, 'tm', [(i, i ^ mask) for i in range(count)])  5.81 us
    pallas_call x1, Pallas kernels, smooth(): pl.pallas_call(functools.partial(smoother_kernel, bits, blocks_of, live,...  5.2 us
    pallas_call x1, Pallas kernels, products(): pl.pallas_call(functools.partial(product_kernel, live), out_shape=[pltpu....  2.36 us
    pallas_call x1, Pallas kernels, prepare(): pl.pallas_call(functools.partial(model_kernel, blocks_of), out_shape=[plt...  1.84 us
    pallas_call x1, Pallas kernels, fetch(): pl.pallas_call(fetch_kernel, out_shape=[pltpu.VMEM(observations.shape, f3...  0.86 us
    pallas_call x1, Pallas kernels, place(): pl.pallas_call(functools.partial(place_kernel, bits), out_shape=jax.Shape...  0.64 us
  transfers between devices with their start and end apart: 12, of which 6 were waited for; matrix products, arithmetic and copies ran while one was open for 0% of the time, Pallas kernels for 17%

profile of v3, /device:TPU:0, one launch (start us, length us, event | category | flops | bytes accessed | tf_op | source)
XLA Modules:
  0.0 29.1 jit_solution(11749790698164570333)
XLA Ops:
  0.0 0.5 %collective-permute-start = (f32[8,2048]{1,0:T(8,128)}, f32[8,2048]{1,0:T(8,128)S(1)}, u32[]{:S(2)}, u32[]{:S(2)}) collective-permute-start(f32[8,2048]{1,0:T(8,128)} %x_hbm.1), channel_id=1, source_target_pairs={{0,1},{1,0},{2,3},{3,2},{4,5},{5,4},{6,7},{7,6},{8,9},{9,8},{10,11... | collective-permute-start | bytes 196616 | tf_op jit(solution)/shard_map/ppermute | solution.py:552
  1.1 0.1 collective-permute-start.1
  1.2 0.5 %collective-permute-start.2 = (s32[8,16]{1,0:T(8,128)}, s32[8,16]{1,0:T(8,128)S(1)}, u32[]{:S(2)}, u32[]{:S(2)}) collective-permute-start(s32[8,16]{1,0:T(8,128)} %mask_hbm.1), channel_id=1, source_target_pairs={{0,1},{1,0},{2,3},{3,2},{4,5},{5,4},{6,7},{7,6},{8,9},{9,8},{10,11... | collective-permute-start | bytes 1544 | tf_op jit(solution)/shard_map/ppermute | solution.py:552
  1.7 0.9 %fetch.1 = (f32[8,2048]{1,0:T(8,128)S(1)}, s32[8,16]{1,0:T(8,128)S(1)}) custom-call(f32[8,2048]{1,0:T(8,128)} %x_hbm.1, s32[8,16]{1,0:T(8,128)} %mask_hbm.1), custom_call_target="tpu_custom_call" | custom-call | bytes 1000000 | tf_op jit(solution)/shard_map/fetch/pallas_call | solution.py:121
  2.6 0.2 collective-permute-done.2.other_mask_ref
  2.7 0.0 collective-permute-done.1.other_length_ref
  2.7 0.0 collective-permute-done.other_ref
  2.7 0.1 deal.1
  2.8 3.9 %collective-permute-start.5 = (f32[40,128]{1,0:T(8,128)S(1)}, f32[40,128]{1,0:T(8,128)S(1)}, u32[]{:S(2)}, u32[]{:S(2)}) collective-permute-start(f32[40,128]{1,0:T(8,128)S(1)} %get-tuple-element.33), channel_id=1, source_target_pairs={{0,6},{1,7},{2,4},{3,5},{4,2},{5,3},{6,0},{7,1},{8,14},{9,15},{10,... | collective-permute-start | bytes 61448 | tf_op jit(solution)/shard_map/ppermute | solution.py:552
  6.8 0.0 collective-permute-start.3
  6.8 0.4 %collective-permute-start.4 = (f32[40,128]{1,0:T(8,128)S(1)}, f32[40,128]{1,0:T(8,128)S(1)}, u32[]{:S(2)}, u32[]{:S(2)}) collective-permute-start(f32[40,128]{1,0:T(8,128)S(1)} %get-tuple-element.32), channel_id=1, source_target_pairs={{0,5},{1,4},{2,7},{3,6},{4,1},{5,0},{6,3},{7,2},{8,13},{9,12},{10,... | collective-permute-start | bytes 61448 | tf_op jit(solution)/shard_map/ppermute | solution.py:552
  7.1 1.8 %prepare.1 = (bf16[2,256,128]{2,1,0:T(8,128)(2,1)S(1)}, bf16[2,256,256]{2,1,0:T(8,128)(2,1)S(1)}, bf16[2,256,512]{2,1,0:T(8,128)(2,1)S(1)}, bf16[2,256,128]{2,1,...) custom-call(f32[16,128,128]{2,1,0:T(8,128)} %t_hbm.1, ...), custom_call_target="tpu_custom_call" | custom-call | flops 1000000000 | bytes 4000000 | tf_op jit(solution)/shard_map/prepare/pallas_call | solution.py:278
  9.0 0.0 copy-start
  9.0 1.1 %collective-permute-done.3.refs_1_ = f32[40,128]{1,0:T(8,128)S(1)} collective-permute-done((f32[40,128]{1,0:T(8,128)S(1)}, f32[40,128]{1,0:T(8,128)S(1)}, u32[]{:S(2)}, u32[]{:S(2)}) %collective-permute-start.3) | collective-permute-done | bytes 20512 | tf_op jit(solution)/shard_map/ppermute | solution.py:552
  10.1 0.0 collective-permute-done.4.refs_2_
  10.1 2.7 %collective-permute-start.6 = (f32[112,128]{1,0:T(8,128)S(1)}, f32[112,128]{1,0:T(8,128)S(1)}, u32[]{:S(2)}, u32[]{:S(2)}) collective-permute-start(f32[112,128]{1,0:T(8,128)S(1)} %join.1.refs_0_), channel_id=1, source_target_pairs={{0,9},{1,8},{2,11},{3,10},{4,13},{5,12},{6,15},{7,14},{8,1},{9,0},... | collective-permute-start | bytes 172040 | tf_op jit(solution)/shard_map/ppermute | solution.py:552
  12.8 0.0 collective-permute-done.5.after_ref.refs_1_
  12.8 0.1 collective-permute-start.7
  12.9 2.4 %products.1 = (f32[2,16,128,128]{3,2,1,0:T(8,128)S(1)}, f32[2,16,128,128]{3,2,1,0:T(8,128)S(1)}, bf16[2,4,768,128]{3,2,1,0:T(8,128)(2,1)S(1)}) custom-call(bf16[2,256,512]{2,1,0:T(8,128)(2,1)S(1)} %get-tuple-element.35.pair_ref.refs_7_, f32[2,512,128]{2,1,0:T(8,128)S(1)} %get-tuple-element.36.row_ref, f32[2,512,128]{2,1,0:T(8,128)S(1)} %get-tuple-element.37.col_ref, ...), custom_call_target="tpu_custom_call" | custom-call | flops 1000000000 | bytes 4000000 | tf_op jit(solution)/shard_map/products/pallas_call | solution.py:307
  15.2 1.8 %collective-permute-done.7.refs_3_ = f32[40,128]{1,0:T(8,128)S(1)} collective-permute-done((f32[40,128]{1,0:T(8,128)S(1)}, f32[40,128]{1,0:T(8,128)S(1)}, u32[]{:S(2)}, u32[]{:S(2)}) %collective-permute-start.7) | collective-permute-done | bytes 20512 | tf_op jit(solution)/shard_map/ppermute | solution.py:552
  17.0 0.0 collective-permute-done.6.refs_2_
  17.0 0.0 copy-done
  17.1 5.2 %smooth.1 = (f32[64,128]{1,0:T(8,128)S(1)}, f32[64,128]{1,0:T(8,128)S(1)}) custom-call(f32[112,128]{1,0:T(8,128)S(1)} %join.1.refs_0_, f32[40,128]{1,0:T(8,128)S(1)} %collective-permute-done.5.after_ref.refs_1_, f32[112,128]{1,0:T(8,128)S(1)} %collective-permute-done.6.refs_2_, f32[40,128]{1,0:T(8,128)S(1)} %collective-permute-done.7.refs_3_, ...), custom_call_target="tpu_custom_call" | custom-call | tf_op jit(solution)/shard_map/smooth/pallas_call | solution.py:525
  22.3 0.3 %collective-permute-start.8 = (f32[64,128]{1,0:T(8,128)S(1)}, f32[64,128]{1,0:T(8,128)S(1)}, u32[]{:S(2)}, u32[]{:S(2)}) collective-permute-start(f32[64,128]{1,0:T(8,128)S(1)} %get-tuple-element.44), channel_id=1, source_target_pairs={{0,1},{1,0},{2,3},{3,2},{4,5},{5,4},{6,7},{7,6},{8,9},{9,8},{10,11... | collective-permute-start | bytes 98312 | tf_op jit(solution)/shard_map/ppermute | solution.py:552
  22.6 1.0 %collective-permute-done.8.came_ref = f32[64,128]{1,0:T(8,128)S(1)} collective-permute-done((f32[64,128]{1,0:T(8,128)S(1)}, f32[64,128]{1,0:T(8,128)S(1)}, u32[]{:S(2)}, u32[]{:S(2)}) %collective-permute-start.8) | collective-permute-done | bytes 32800 | tf_op jit(solution)/shard_map/ppermute | solution.py:552
  23.5 1.4 %collective-permute-start.10 = (f32[32,128]{1,0:T(8,128)S(1)}, f32[32,128]{1,0:T(8,128)S(1)}, u32[]{:S(2)}, u32[]{:S(2)}) collective-permute-start(f32[32,128]{1,0:T(8,128)S(1)} %get-tuple-element.47), channel_id=1, source_target_pairs={{0,6},{1,7},{2,4},{3,5},{4,2},{5,3},{6,0},{7,1},{8,14},{9,15},{10,... | collective-permute-start | bytes 49160 | tf_op jit(solution)/shard_map/ppermute | solution.py:552
  24.9 0.4 %collective-permute-start.11 = (f32[32,128]{1,0:T(8,128)S(1)}, f32[32,128]{1,0:T(8,128)S(1)}, u32[]{:S(2)}, u32[]{:S(2)}) collective-permute-start(f32[32,128]{1,0:T(8,128)S(1)} %get-tuple-element.48), channel_id=1, source_target_pairs={{0,3},{1,2},{2,1},{3,0},{4,7},{5,6},{6,5},{7,4},{8,11},{9,10},{10,... | collective-permute-start | bytes 49160 | tf_op jit(solution)/shard_map/ppermute | solution.py:552
  25.3 1.4 %collective-permute-start.9 = (f32[32,128]{1,0:T(8,128)S(1)}, f32[32,128]{1,0:T(8,128)S(1)}, u32[]{:S(2)}, u32[]{:S(2)}) collective-permute-start(f32[32,128]{1,0:T(8,128)S(1)} %get-tuple-element.46), channel_id=1, source_target_pairs={{0,5},{1,4},{2,7},{3,6},{4,1},{5,0},{6,3},{7,2},{8,13},{9,12},{10,... | collective-permute-start | bytes 49160 | tf_op jit(solution)/shard_map/ppermute | solution.py:552
  26.7 1.5 %collective-permute-done.10.refs_2_ = f32[32,128]{1,0:T(8,128)S(1)} collective-permute-done((f32[32,128]{1,0:T(8,128)S(1)}, f32[32,128]{1,0:T(8,128)S(1)}, u32[]{:S(2)}, u32[]{:S(2)}) %collective-permute-start.10) | collective-permute-done | bytes 16416 | tf_op jit(solution)/shard_map/ppermute | solution.py:552
  28.3 0.0 collective-permute-done.11.refs_3_
  28.3 0.2 collective-permute-done.9.refs_1_
  28.5 0.6 %place.1 = f32[8,2048]{1,0:T(8,128)} custom-call(f32[32,128]{1,0:T(8,128)S(1)} %get-tuple-element.45.refs_0_, f32[32,128]{1,0:T(8,128)S(1)} %collective-permute-done.9.refs_1_, f32[32,128]{1,0:T(8,128)S(1)} %collective-permute-done.10.refs_2_, f32[32,128]{1,0:T(8,128)S(1)} %collective-permute-done.11.refs_3_), custom_call_target="tpu_custom_call" | custom-call | tf_op jit(solution)/shard_map/place/pallas_call | solution.py:185
  (3 shorter events, 0.0 us)
Async XLA Ops:
  0.0 2.7 %collective-permute-start = (f32[8,2048]{1,0:T(8,128)}, f32[8,2048]{1,0:T(8,128)S(1)}, u32[]{:S(2)}, u32[]{:S(2)}) collective-permute-start(f32[8,2048]{1,0:T(8,128)} %x_hbm.1), channel_id=1, source_target_pairs={{0,1},{1,0},{2,3},{3,2},{4,5},{5,4},{6,7},{7,6},{8,9},{9,8},{10,11... | collective-permute-start | bytes 196616 | tf_op jit(solution)/shard_map/ppermute | solution.py:552
  1.1 1.6 %collective-permute-start.1 = (f32[8,128]{1,0:T(8,128)S(1)}, f32[8,128]{1,0:T(8,128)S(1)}, u32[]{:S(2)}, u32[]{:S(2)}) collective-permute-start(f32[8,128]{1,0:T(8,128)S(1)} %broadcast_in_dim.9.length_ref), channel_id=1, source_target_pairs={{0,1},{1,0},{2,3},{3,2},{4,5},{5,4},{6,7},{7,6},{8,9},{9,8},{10,11... | collective-permute-start | bytes 12296 | tf_op jit(solution)/shard_map/ppermute | solution.py:552
  1.2 1.5 %collective-permute-start.2 = (s32[8,16]{1,0:T(8,128)}, s32[8,16]{1,0:T(8,128)S(1)}, u32[]{:S(2)}, u32[]{:S(2)}) collective-permute-start(s32[8,16]{1,0:T(8,128)} %mask_hbm.1), channel_id=1, source_target_pairs={{0,1},{1,0},{2,3},{3,2},{4,5},{5,4},{6,7},{7,6},{8,9},{9,8},{10,11... | collective-permute-start | bytes 1544 | tf_op jit(solution)/shard_map/ppermute | solution.py:552
  2.8 10.0 %collective-permute-start.5 = (f32[40,128]{1,0:T(8,128)S(1)}, f32[40,128]{1,0:T(8,128)S(1)}, u32[]{:S(2)}, u32[]{:S(2)}) collective-permute-start(f32[40,128]{1,0:T(8,128)S(1)} %get-tuple-element.33), channel_id=1, source_target_pairs={{0,6},{1,7},{2,4},{3,5},{4,2},{5,3},{6,0},{7,1},{8,14},{9,15},{10,... | collective-permute-start | bytes 61448 | tf_op jit(solution)/shard_map/ppermute | solution.py:552
  6.8 3.4 %collective-permute-start.3 = (f32[40,128]{1,0:T(8,128)S(1)}, f32[40,128]{1,0:T(8,128)S(1)}, u32[]{:S(2)}, u32[]{:S(2)}) collective-permute-start(f32[40,128]{1,0:T(8,128)S(1)} %get-tuple-element.31), channel_id=1, source_target_pairs={{0,3},{1,2},{2,1},{3,0},{4,7},{5,6},{6,5},{7,4},{8,11},{9,10},{10,... | collective-permute-start | bytes 61448 | tf_op jit(solution)/shard_map/ppermute | solution.py:552
  6.8 3.4 %collective-permute-start.4 = (f32[40,128]{1,0:T(8,128)S(1)}, f32[40,128]{1,0:T(8,128)S(1)}, u32[]{:S(2)}, u32[]{:S(2)}) collective-permute-start(f32[40,128]{1,0:T(8,128)S(1)} %get-tuple-element.32), channel_id=1, source_target_pairs={{0,5},{1,4},{2,7},{3,6},{4,1},{5,0},{6,3},{7,2},{8,13},{9,12},{10,... | collective-permute-start | bytes 61448 | tf_op jit(solution)/shard_map/ppermute | solution.py:552
  9.0 8.1 %copy-start = (f32[2048]{0:T(1024)S(1)}, f32[2048]{0:T(1024)}, u32[]{:S(2)}) copy-start(f32[2048]{0:T(1024)} %param.10) | copy-start | bytes 24580
  10.1 6.9 %collective-permute-start.6 = (f32[112,128]{1,0:T(8,128)S(1)}, f32[112,128]{1,0:T(8,128)S(1)}, u32[]{:S(2)}, u32[]{:S(2)}) collective-permute-start(f32[112,128]{1,0:T(8,128)S(1)} %join.1.refs_0_), channel_id=1, source_target_pairs={{0,9},{1,8},{2,11},{3,10},{4,13},{5,12},{6,15},{7,14},{8,1},{9,0},... | collective-permute-start | bytes 172040 | tf_op jit(solution)/shard_map/ppermute | solution.py:552
  12.8 4.2 %collective-permute-start.7 = (f32[40,128]{1,0:T(8,128)S(1)}, f32[40,128]{1,0:T(8,128)S(1)}, u32[]{:S(2)}, u32[]{:S(2)}) collective-permute-start(f32[40,128]{1,0:T(8,128)S(1)} %collective-permute-done.5.after_ref.refs_1_), channel_id=1, source_target_pairs={{0,9},{1,8},{2,11},{3,10},{4,13},{5,12},{6,15},{7,14},{8,1},{9,0},... | collective-permute-start | bytes 61448 | tf_op jit(solution)/shard_map/ppermute | solution.py:552
  22.3 1.3 %collective-permute-start.8 = (f32[64,128]{1,0:T(8,128)S(1)}, f32[64,128]{1,0:T(8,128)S(1)}, u32[]{:S(2)}, u32[]{:S(2)}) collective-permute-start(f32[64,128]{1,0:T(8,128)S(1)} %get-tuple-element.44), channel_id=1, source_target_pairs={{0,1},{1,0},{2,3},{3,2},{4,5},{5,4},{6,7},{7,6},{8,9},{9,8},{10,11... | collective-permute-start | bytes 98312 | tf_op jit(solution)/shard_map/ppermute | solution.py:552
  23.5 4.7 %collective-permute-start.10 = (f32[32,128]{1,0:T(8,128)S(1)}, f32[32,128]{1,0:T(8,128)S(1)}, u32[]{:S(2)}, u32[]{:S(2)}) collective-permute-start(f32[32,128]{1,0:T(8,128)S(1)} %get-tuple-element.47), channel_id=1, source_target_pairs={{0,6},{1,7},{2,4},{3,5},{4,2},{5,3},{6,0},{7,1},{8,14},{9,15},{10,... | collective-permute-start | bytes 49160 | tf_op jit(solution)/shard_map/ppermute | solution.py:552
  24.9 3.4 %collective-permute-start.11 = (f32[32,128]{1,0:T(8,128)S(1)}, f32[32,128]{1,0:T(8,128)S(1)}, u32[]{:S(2)}, u32[]{:S(2)}) collective-permute-start(f32[32,128]{1,0:T(8,128)S(1)} %get-tuple-element.48), channel_id=1, source_target_pairs={{0,3},{1,2},{2,1},{3,0},{4,7},{5,6},{6,5},{7,4},{8,11},{9,10},{10,... | collective-permute-start | bytes 49160 | tf_op jit(solution)/shard_map/ppermute | solution.py:552
  25.3 3.2 %collective-permute-start.9 = (f32[32,128]{1,0:T(8,128)S(1)}, f32[32,128]{1,0:T(8,128)S(1)}, u32[]{:S(2)}, u32[]{:S(2)}) collective-permute-start(f32[32,128]{1,0:T(8,128)S(1)} %get-tuple-element.46), channel_id=1, source_target_pairs={{0,5},{1,4},{2,7},{3,6},{4,1},{5,0},{6,3},{7,2},{8,13},{9,12},{10,... | collective-permute-start | bytes 49160 | tf_op jit(solution)/shard_map/ppermute | solution.py:552

commit v4 on v3

--- a/solution.py
+++ b/solution.py
@@ -69,6 +69,7 @@
 
 
 EXCHANGED = 3
+PARTS = ((0,), (1, 2, 3))
 PLACED = (0, 2, 3, 1)
 
 
@@ -106,31 +107,39 @@
     )(*in_vmem(*arrays))
 
 
-def fetch_kernel(x_hbm, mask_hbm, x_ref, mask_ref, sems):
+def fetch_kernel(blocks_of, x_hbm, mask_hbm, t_hbm, k_hbm, s_hbm, x_ref, mask_ref, t_ref, k_ref, s_ref, sems):
     copies = [
         pltpu.make_async_copy(x_hbm, x_ref, sems.at[0]),
         pltpu.make_async_copy(mask_hbm, mask_ref, sems.at[1]),
     ]
+    for j, b in enumerate(blocks_of()):
+        for n, (src, dst) in enumerate(((t_hbm, t_ref), (k_hbm, k_ref), (s_hbm, s_ref))):
+            copies.append(pltpu.make_async_copy(src.at[b], dst.at[j], sems.at[2 + 3 * j + n]))
     for c in copies:
         c.start()
     for c in copies:
         c.wait()
 
 
-def fetch(observations, outage_mask):
+def fetch(blocks_of, nb, observations, outage_mask, *mats):
+    width = mats[0].shape[1]
     return pl.pallas_call(
-        fetch_kernel,
-        out_shape=[pltpu.VMEM(observations.shape, f32), pltpu.VMEM(outage_mask.shape, jnp.int32)],
-        in_specs=[pl.BlockSpec(memory_space=pltpu.HBM)] * 2,
-        out_specs=[pl.BlockSpec(memory_space=pltpu.VMEM)] * 2,
-        scratch_shapes=[pltpu.SemaphoreType.DMA((2,))],
+        functools.partial(fetch_kernel, blocks_of),
+        out_shape=[
+            pltpu.VMEM(observations.shape, f32),
+            pltpu.VMEM(outage_mask.shape, jnp.int32),
+        ]
+        + [pltpu.VMEM((nb, width, width), f32)] * 3,
+        in_specs=[pl.BlockSpec(memory_space=pltpu.HBM)] * 5,
+        out_specs=[pl.BlockSpec(memory_space=pltpu.VMEM)] * 5,
+        scratch_shapes=[pltpu.SemaphoreType.DMA((2 + 3 * nb,))],
         compiler_params=pltpu.CompilerParams(vmem_limit_bytes=LIMIT_P),
         cost_estimate=pl.CostEstimate(flops=0, bytes_accessed=10**6, transcendentals=0),
         name="fetch",
-    )(*in_hbm(observations, outage_mask))
-
-
-def deal_kernel(bits, x_ref, other_ref, length_ref, other_length_ref, mask_ref, other_mask_ref, *outs):
+    )(*in_hbm(observations, outage_mask, *mats))
+
+
+def deal_kernel(bits, x_ref, other_ref, mask_ref, other_mask_ref, length_ref, other_length_ref, *outs):
     cap, nblocks = mask_ref.shape
     width = length_ref.shape[1]
     half = (outs[0].shape[0] - 8) // 2
@@ -155,9 +164,10 @@
 def join_kernel(_, *refs):
     out_ref = refs[-1]
     rows = refs[0].shape[0] - 8
+    count = len(refs) - 1
     for k, ref in enumerate(refs[:-1]):
         out_ref[k * rows : (k + 1) * rows] = ref[:rows]
-        out_ref[3 * rows + 4 * k : 3 * rows + 4 * k + 4] = ref[rows : rows + 4]
+        out_ref[count * rows + 4 * k : count * rows + 4 * k + 4] = ref[rows : rows + 4]
 
 
 def split_kernel(stay_ref, came_ref, *outs):
@@ -193,10 +203,9 @@
 
 
 def model_kernel(
-    blocks_of,
-    t_hbm,
-    k_hbm,
-    s_hbm,
+    t_ref,
+    k_ref,
+    s_ref,
     after_ref,
     gain_ref,
     step_ref,
@@ -205,20 +214,8 @@
     row_ref,
     col_ref,
     power_ref,
-    t_ref,
-    k_ref,
-    s_ref,
-    sems,
 ):
     nb, width = t_ref.shape[0], t_ref.shape[1]
-    copies = []
-    for j, b in enumerate(blocks_of()):
-        for n, (src, dst) in enumerate(((t_hbm, t_ref), (k_hbm, k_ref), (s_hbm, s_ref))):
-            copies.append(pltpu.make_async_copy(src.at[b], dst.at[j], sems.at[j, n]))
-    for c in copies:
-        c.start()
-    for c in copies:
-        c.wait()
     eye = (
         lax.broadcasted_iota(jnp.int32, (width, width), 0)
         == lax.broadcasted_iota(jnp.int32, (width, width), 1)
@@ -271,12 +268,11 @@
                 power_ref[j, n, m * 2 * width : (m + 1) * 2 * width] = rights[j][m]
 
 
-def prepare(blocks_of, nb, transition, filter_gain, smoother_gain, after):
-    width = transition.shape[1]
-    hbm = pl.BlockSpec(memory_space=pltpu.HBM)
+def prepare(mats, after):
+    nb, width = mats[0].shape[:2]
     vmem = pl.BlockSpec(memory_space=pltpu.VMEM)
     return pl.pallas_call(
-        functools.partial(model_kernel, blocks_of),
+        model_kernel,
         out_shape=[
             pltpu.VMEM((nb, 2 * width, width), bf16),
             pltpu.VMEM((nb, 2 * width, 2 * width), bf16),
@@ -286,18 +282,12 @@
             pltpu.VMEM((nb, 4 * width, width), f32),
             pltpu.VMEM((nb, width, width), f32),
         ],
-        in_specs=[hbm] * 3 + [pl.BlockSpec(memory_space=pl.ANY)],
+        in_specs=[vmem] * 3 + [pl.BlockSpec(memory_space=pl.ANY)],
         out_specs=[vmem] * 7,
-        scratch_shapes=[
-            pltpu.VMEM((nb, width, width), f32),
-            pltpu.VMEM((nb, width, width), f32),
-            pltpu.VMEM((nb, width, width), f32),
-            pltpu.SemaphoreType.DMA((nb, 3)),
-        ],
         compiler_params=pltpu.CompilerParams(vmem_limit_bytes=LIMIT_A),
         cost_estimate=pl.CostEstimate(flops=10**9, bytes_accessed=4 * 10**6, transcendentals=0),
         name="prepare",
-    )(*in_hbm(transition, filter_gain, smoother_gain), after)
+    )(*in_vmem(*mats), after)
 
 
 def products(live, pair, row2, col2, gain, after):
@@ -370,17 +360,17 @@
     odd = parity(me, bits)
 
     part = 2 * nb * cap
-    for top in range(y_ref.shape[0]):
-        most, last = sent_refs[2 * top], sent_refs[2 * top + 1]
-        y_ref[top, meta_row : meta_row + 12] = most[3 * part : 3 * part + 12]
-        y_ref[top, meta_row + 12 :] = last[part : part + 4]
+    for n, ref in enumerate(sent_refs):
+        spots = PARTS[n % len(PARTS)]
+        for i, k in enumerate(spots):
+            row = len(spots) * part + 4 * i
+            y_ref[n // len(PARTS), meta_row + 4 * k : meta_row + 4 * k + 4] = ref[row : row + 4]
     meta_ref[...] = y_ref[:, meta_row:].astype(jnp.int32)
     fetch = pltpu.make_async_copy(meta_ref, meta_smem, sems.at[0])
     fetch.start()
-    for top in range(y_ref.shape[0]):
-        most, last = sent_refs[2 * top], sent_refs[2 * top + 1]
-        y_ref[top, : 3 * part] = most[: 3 * part]
-        y_ref[top, 3 * part : meta_row] = last[:part]
+    for n, ref in enumerate(sent_refs):
+        for i, k in enumerate(PARTS[n % len(PARTS)]):
+            y_ref[n // len(PARTS), k * part : (k + 1) * part] = ref[i * part : (i + 1) * part]
     places = []
     for g in range(groups):
         d = me ^ g
@@ -514,7 +504,7 @@
 
 
 def smooth(bits, blocks_of, nb, cap, live, sent, prior, model):
-    tops = len(sent) // 2
+    tops = len(sent) // len(PARTS)
     width = sent[0].shape[1]
     rows = 8 * nb * cap + 16
     nchunks = live // 4
@@ -567,23 +557,28 @@
     package = (2 * half + 8, width)
     other = permuted(observations, 1), permuted(outage_mask, 1)
     length = jnp.broadcast_to(group_length.astype(f32)[:, None], (8, width))
-    own = fetch(observations, outage_mask)
+    own = fetch(blocks_of, nb, observations, outage_mask, transition, filter_gain, smoother_gain)
     dealt = local(
         functools.partial(deal_kernel, bits),
         [package] * 4,
         "deal",
         own[0],
         other[0],
+        own[1],
+        other[1],
         length,
         permuted(length, 1),
-        own[1],
-        other[1],
     )
     crossed = [permuted(p, mask) for p, mask in zip(dealt[1:], masks)]
-    gain, step, pair, back, row2, col2, power = prepare(
-        blocks_of, nb, transition, filter_gain, smoother_gain, dealt[0]
-    )
-    sent = [*local(join_kernel, [(6 * half + 16, width)], "join", gain, dealt[0], *crossed[:2]), crossed[2]]
+    gain, step, pair, back, row2, col2, power = prepare(own[2:], dealt[0])
+    held = [dealt[0], *crossed]
+    sent = []
+    for spots in PARTS:
+        if len(spots) == 1:
+            sent.append(held[spots[0]])
+        else:
+            rows = 2 * half * len(spots) + -(-4 * len(spots) // 8) * 8
+            sent += local(join_kernel, [(rows, width)], "join", gain, *(held[k] for k in spots))
     for k in range(EXCHANGED, bits):
         sent = sent + [permuted(x, (1 << k) | 1) for x in sent]
     rowprod, colprod, powers = products(live, pair, row2, col2, power, crossed[2])

time: 29.3 us -> 28.6 us (0.976)
  starting transfers between devices: 11.6 us -> 14.9 us
  waiting for transfers between devices: 5.81 us -> 2.55 us
  Pallas kernels: 11 us -> 10.2 us
    ppermute x12, starting transfers between devices: 11.6 us -> 14.9 us  [permuted(): return lax.ppermute(x, 'tm', [(i, i ^ mask) for i in range(count)])]
    ppermute x12, waiting for transfers between devices: 5.81 us -> 2.55 us  [permuted(): return lax.ppermute(x, 'tm', [(i, i ^ mask) for i in range(count)])]
    pallas_call x2, Pallas kernels: 2.7 us -> 1.91 us  [the longest x1 1.11 us: fetch(): pl.pallas_call(functools.partial(fetch_kernel, blocks_of), out_shape=[plt...]
  transfers between devices with their start and end apart: 12 -> 12, of which waited for: 6 -> 3; matrix products, arithmetic and copies ran while one was open for 0% -> 0% of each run, Pallas kernels for 17% -> 15%
where the time goes in v4:
time: 28.6 us; the launch traced here: 28.5 us
  starting transfers between devices  14.9 us (52%)
  Pallas kernels  10.2 us (36%)
  waiting for transfers between devices  2.55 us (9%)
  between operations  0.79 us (3%)
    ppermute x12, starting transfers between devices, permuted(): return lax.ppermute(x, 'tm', [(i, i ^ mask) for i in range(count)])  14.9 us
    pallas_call x1, Pallas kernels, smooth(): pl.pallas_call(functools.partial(smoother_kernel, bits, blocks_of, live,...  5.21 us
    ppermute x12, waiting for transfers between devices, permuted(): return lax.ppermute(x, 'tm', [(i, i ^ mask) for i in range(count)])  2.55 us
    pallas_call x1, Pallas kernels, products(): pl.pallas_call(functools.partial(product_kernel, live), out_shape=[pltpu....  2.37 us
    pallas_call x1, Pallas kernels, fetch(): pl.pallas_call(functools.partial(fetch_kernel, blocks_of), out_shape=[plt...  1.11 us
    pallas_call x1, Pallas kernels, prepare(): pl.pallas_call(model_kernel, out_shape=[pltpu.VMEM((nb, 2 * width, width)...  0.79 us
    pallas_call x1, Pallas kernels, place(): pl.pallas_call(functools.partial(place_kernel, bits), out_shape=jax.Shape...  0.64 us
  transfers between devices with their start and end apart: 12, of which 3 were waited for; matrix products, arithmetic and copies ran while one was open for 0% of the time, Pallas kernels for 15%

profile of v4, /device:TPU:0, one launch (start us, length us, event | category | flops | bytes accessed | tf_op | source)
XLA Modules:
  0.0 28.5 jit_solution(11466203584199300287)
XLA Ops:
  0.0 0.5 %collective-permute-start = (f32[8,2048]{1,0:T(8,128)}, f32[8,2048]{1,0:T(8,128)S(1)}, u32[]{:S(2)}, u32[]{:S(2)}) collective-permute-start(f32[8,2048]{1,0:T(8,128)} %x_hbm.1), channel_id=1, source_target_pairs={{0,1},{1,0},{2,3},{3,2},{4,5},{5,4},{6,7},{7,6},{8,9},{9,8},{10,11... | collective-permute-start | bytes 196616 | tf_op jit(solution)/shard_map/ppermute | solution.py:542
  1.1 0.1 collective-permute-start.2
  1.2 0.5 %collective-permute-start.1 = (s32[8,16]{1,0:T(8,128)}, s32[8,16]{1,0:T(8,128)S(1)}, u32[]{:S(2)}, u32[]{:S(2)}) collective-permute-start(s32[8,16]{1,0:T(8,128)} %mask_hbm.1), channel_id=1, source_target_pairs={{0,1},{1,0},{2,3},{3,2},{4,5},{5,4},{6,7},{7,6},{8,9},{9,8},{10,11... | collective-permute-start | bytes 1544 | tf_op jit(solution)/shard_map/ppermute | solution.py:542
  1.7 1.1 %fetch.1 = (f32[8,2048]{1,0:T(8,128)S(1)}, s32[8,16]{1,0:T(8,128)S(1)}, f32[2,128,128]{2,1,0:T(8,128)S(1)}, f32[2,128,128]{2,1,0:T(8,128)S(1)}, f32[2,128,128]{2,1,0:T(8,128)S(1)}) custom-call(f32[8,2048]{1,0:T(8,128)} %x_hbm.1, s32[8,16]{1,0:T(8,128)} %mask_hbm.1, f32[16,128,128]{2,1,0:T(8,128)} %t_hbm.1, f32[16,128,128]{2,1,0:T(8,128)} %k_hbm.1, ...), custom_call_target="tpu_custom_call" | custom-call | bytes 1000000 | tf_op jit(solution)/shard_map/fetch/pallas_call | solution.py:126
  2.8 0.0 collective-permute-done.1.other_mask_ref
  2.8 0.0 collective-permute-done.2.other_length_ref
  2.8 0.0 collective-permute-done.other_ref
  2.8 0.1 deal.1
  2.9 3.8 %collective-permute-start.5 = (f32[40,128]{1,0:T(8,128)S(1)}, f32[40,128]{1,0:T(8,128)S(1)}, u32[]{:S(2)}, u32[]{:S(2)}) collective-permute-start(f32[40,128]{1,0:T(8,128)S(1)} %get-tuple-element.39), channel_id=1, source_target_pairs={{0,6},{1,7},{2,4},{3,5},{4,2},{5,3},{6,0},{7,1},{8,14},{9,15},{10,... | collective-permute-start | bytes 61448 | tf_op jit(solution)/shard_map/ppermute | solution.py:542
  6.8 0.1 collective-permute-start.3
  6.9 0.3 collective-permute-start.4
  7.1 2.5 %collective-permute-start.6 = (f32[40,128]{1,0:T(8,128)S(1)}, f32[40,128]{1,0:T(8,128)S(1)}, u32[]{:S(2)}, u32[]{:S(2)}) collective-permute-start(f32[40,128]{1,0:T(8,128)S(1)} %get-tuple-element.32.after_ref.refs_0_), channel_id=1, source_target_pairs={{0,9},{1,8},{2,11},{3,10},{4,13},{5,12},{6,15},{7,14},{8,1},{9,0},... | collective-permute-start | bytes 61448 | tf_op jit(solution)/shard_map/ppermute | solution.py:542
  9.6 0.8 %prepare.1 = (bf16[2,256,128]{2,1,0:T(8,128)(2,1)S(1)}, bf16[2,256,256]{2,1,0:T(8,128)(2,1)S(1)}, bf16[2,256,512]{2,1,0:T(8,128)(2,1)S(1)}, bf16[2,256,128]{2,1,...) custom-call(f32[2,128,128]{2,1,0:T(8,128)S(1)} %get-tuple-element.33.t_ref, ...), custom_call_target="tpu_custom_call" | custom-call | flops 1000000000 | bytes 4000000 | tf_op jit(solution)/shard_map/prepare/pallas_call | solution.py:274
  10.4 0.0 copy-start
  10.4 0.0 collective-permute-done.5.refs_2_.after_ref
  10.5 0.0 collective-permute-done.3.refs_0_
  10.5 0.0 collective-permute-done.4.refs_1_
  10.5 2.3 %collective-permute-start.7 = (f32[112,128]{1,0:T(8,128)S(1)}, f32[112,128]{1,0:T(8,128)S(1)}, u32[]{:S(2)}, u32[]{:S(2)}) collective-permute-start(f32[112,128]{1,0:T(8,128)S(1)} %join.1.refs_1_), channel_id=1, source_target_pairs={{0,9},{1,8},{2,11},{3,10},{4,13},{5,12},{6,15},{7,14},{8,1},{9,0},... | collective-permute-start | bytes 172040 | tf_op jit(solution)/shard_map/ppermute | solution.py:542
  12.8 2.4 %products.1 = (f32[2,16,128,128]{3,2,1,0:T(8,128)S(1)}, f32[2,16,128,128]{3,2,1,0:T(8,128)S(1)}, bf16[2,4,768,128]{3,2,1,0:T(8,128)(2,1)S(1)}) custom-call(bf16[2,256,512]{2,1,0:T(8,128)(2,1)S(1)} %get-tuple-element.41.pair_ref.refs_7_, f32[2,512,128]{2,1,0:T(8,128)S(1)} %get-tuple-element.42.row_ref, f32[2,512,128]{2,1,0:T(8,128)S(1)} %get-tuple-element.43.col_ref, ...), custom_call_target="tpu_custom_call" | custom-call | flops 1000000000 | bytes 4000000 | tf_op jit(solution)/shard_map/products/pallas_call | solution.py:297
  15.2 0.0 collective-permute-done.6.refs_2_
  15.2 0.0 collective-permute-done.7.refs_3_
  15.2 0.0 copy-done
  15.2 5.2 %smooth.1 = (f32[64,128]{1,0:T(8,128)S(1)}, f32[64,128]{1,0:T(8,128)S(1)}) custom-call(f32[40,128]{1,0:T(8,128)S(1)} %get-tuple-element.32.after_ref.refs_0_, f32[112,128]{1,0:T(8,128)S(1)} %join.1.refs_1_, f32[40,128]{1,0:T(8,128)S(1)} %collective-permute-done.6.refs_2_, f32[112,128]{1,0:T(8,128)S(1)} %collective-permute-done.7.refs_3_, ...), custom_call_target="tpu_custom_call" | custom-call | tf_op jit(solution)/shard_map/smooth/pallas_call | solution.py:515
  20.4 1.7 %collective-permute-start.8 = (f32[64,128]{1,0:T(8,128)S(1)}, f32[64,128]{1,0:T(8,128)S(1)}, u32[]{:S(2)}, u32[]{:S(2)}) collective-permute-start(f32[64,128]{1,0:T(8,128)S(1)} %get-tuple-element.50), channel_id=1, source_target_pairs={{0,1},{1,0},{2,3},{3,2},{4,5},{5,4},{6,7},{7,6},{8,9},{9,8},{10,11... | collective-permute-start | bytes 98312 | tf_op jit(solution)/shard_map/ppermute | solution.py:542
  22.1 0.9 %collective-permute-done.8.came_ref = f32[64,128]{1,0:T(8,128)S(1)} collective-permute-done((f32[64,128]{1,0:T(8,128)S(1)}, f32[64,128]{1,0:T(8,128)S(1)}, u32[]{:S(2)}, u32[]{:S(2)}) %collective-permute-start.8) | collective-permute-done | bytes 32800 | tf_op jit(solution)/shard_map/ppermute | solution.py:542
  22.9 1.3 %collective-permute-start.10 = (f32[32,128]{1,0:T(8,128)S(1)}, f32[32,128]{1,0:T(8,128)S(1)}, u32[]{:S(2)}, u32[]{:S(2)}) collective-permute-start(f32[32,128]{1,0:T(8,128)S(1)} %get-tuple-element.53), channel_id=1, source_target_pairs={{0,6},{1,7},{2,4},{3,5},{4,2},{5,3},{6,0},{7,1},{8,14},{9,15},{10,... | collective-permute-start | bytes 49160 | tf_op jit(solution)/shard_map/ppermute | solution.py:542
  24.3 0.2 collective-permute-start.11
  24.5 1.7 %collective-permute-start.9 = (f32[32,128]{1,0:T(8,128)S(1)}, f32[32,128]{1,0:T(8,128)S(1)}, u32[]{:S(2)}, u32[]{:S(2)}) collective-permute-start(f32[32,128]{1,0:T(8,128)S(1)} %get-tuple-element.52), channel_id=1, source_target_pairs={{0,5},{1,4},{2,7},{3,6},{4,1},{5,0},{6,3},{7,2},{8,13},{9,12},{10,... | collective-permute-start | bytes 49160 | tf_op jit(solution)/shard_map/ppermute | solution.py:542
  26.2 1.5 %collective-permute-done.10.refs_2_ = f32[32,128]{1,0:T(8,128)S(1)} collective-permute-done((f32[32,128]{1,0:T(8,128)S(1)}, f32[32,128]{1,0:T(8,128)S(1)}, u32[]{:S(2)}, u32[]{:S(2)}) %collective-permute-start.10) | collective-permute-done | bytes 16416 | tf_op jit(solution)/shard_map/ppermute | solution.py:542
  27.6 0.0 collective-permute-done.11.refs_3_
  27.6 0.2 collective-permute-done.9.refs_1_
  27.8 0.6 %place.1 = f32[8,2048]{1,0:T(8,128)} custom-call(f32[32,128]{1,0:T(8,128)S(1)} %get-tuple-element.51.refs_0_, f32[32,128]{1,0:T(8,128)S(1)} %collective-permute-done.9.refs_1_, f32[32,128]{1,0:T(8,128)S(1)} %collective-permute-done.10.refs_2_, f32[32,128]{1,0:T(8,128)S(1)} %collective-permute-done.11.refs_3_), custom_call_target="tpu_custom_call" | custom-call | tf_op jit(solution)/shard_map/place/pallas_call | solution.py:195
  (3 shorter events, 0.0 us)
Async XLA Ops:
  0.0 2.8 %collective-permute-start = (f32[8,2048]{1,0:T(8,128)}, f32[8,2048]{1,0:T(8,128)S(1)}, u32[]{:S(2)}, u32[]{:S(2)}) collective-permute-start(f32[8,2048]{1,0:T(8,128)} %x_hbm.1), channel_id=1, source_target_pairs={{0,1},{1,0},{2,3},{3,2},{4,5},{5,4},{6,7},{7,6},{8,9},{9,8},{10,11... | collective-permute-start | bytes 196616 | tf_op jit(solution)/shard_map/ppermute | solution.py:542
  1.1 1.7 %collective-permute-start.2 = (f32[8,128]{1,0:T(8,128)S(1)}, f32[8,128]{1,0:T(8,128)S(1)}, u32[]{:S(2)}, u32[]{:S(2)}) collective-permute-start(f32[8,128]{1,0:T(8,128)S(1)} %broadcast_in_dim.9.length_ref), channel_id=1, source_target_pairs={{0,1},{1,0},{2,3},{3,2},{4,5},{5,4},{6,7},{7,6},{8,9},{9,8},{10,11... | collective-permute-start | bytes 12296 | tf_op jit(solution)/shard_map/ppermute | solution.py:542
  1.2 1.6 %collective-permute-start.1 = (s32[8,16]{1,0:T(8,128)}, s32[8,16]{1,0:T(8,128)S(1)}, u32[]{:S(2)}, u32[]{:S(2)}) collective-permute-start(s32[8,16]{1,0:T(8,128)} %mask_hbm.1), channel_id=1, source_target_pairs={{0,1},{1,0},{2,3},{3,2},{4,5},{5,4},{6,7},{7,6},{8,9},{9,8},{10,11... | collective-permute-start | bytes 1544 | tf_op jit(solution)/shard_map/ppermute | solution.py:542
  2.9 7.5 %collective-permute-start.5 = (f32[40,128]{1,0:T(8,128)S(1)}, f32[40,128]{1,0:T(8,128)S(1)}, u32[]{:S(2)}, u32[]{:S(2)}) collective-permute-start(f32[40,128]{1,0:T(8,128)S(1)} %get-tuple-element.39), channel_id=1, source_target_pairs={{0,6},{1,7},{2,4},{3,5},{4,2},{5,3},{6,0},{7,1},{8,14},{9,15},{10,... | collective-permute-start | bytes 61448 | tf_op jit(solution)/shard_map/ppermute | solution.py:542
  6.8 3.7 %collective-permute-start.3 = (f32[40,128]{1,0:T(8,128)S(1)}, f32[40,128]{1,0:T(8,128)S(1)}, u32[]{:S(2)}, u32[]{:S(2)}) collective-permute-start(f32[40,128]{1,0:T(8,128)S(1)} %get-tuple-element.37), channel_id=1, source_target_pairs={{0,3},{1,2},{2,1},{3,0},{4,7},{5,6},{6,5},{7,4},{8,11},{9,10},{10,... | collective-permute-start | bytes 61448 | tf_op jit(solution)/shard_map/ppermute | solution.py:542
  6.9 3.6 %collective-permute-start.4 = (f32[40,128]{1,0:T(8,128)S(1)}, f32[40,128]{1,0:T(8,128)S(1)}, u32[]{:S(2)}, u32[]{:S(2)}) collective-permute-start(f32[40,128]{1,0:T(8,128)S(1)} %get-tuple-element.38), channel_id=1, source_target_pairs={{0,5},{1,4},{2,7},{3,6},{4,1},{5,0},{6,3},{7,2},{8,13},{9,12},{10,... | collective-permute-start | bytes 61448 | tf_op jit(solution)/shard_map/ppermute | solution.py:542
  7.1 8.0 %collective-permute-start.6 = (f32[40,128]{1,0:T(8,128)S(1)}, f32[40,128]{1,0:T(8,128)S(1)}, u32[]{:S(2)}, u32[]{:S(2)}) collective-permute-start(f32[40,128]{1,0:T(8,128)S(1)} %get-tuple-element.32.after_ref.refs_0_), channel_id=1, source_target_pairs={{0,9},{1,8},{2,11},{3,10},{4,13},{5,12},{6,15},{7,14},{8,1},{9,0},... | collective-permute-start | bytes 61448 | tf_op jit(solution)/shard_map/ppermute | solution.py:542
  10.4 4.8 %copy-start = (f32[2048]{0:T(1024)S(1)}, f32[2048]{0:T(1024)}, u32[]{:S(2)}) copy-start(f32[2048]{0:T(1024)} %param.10) | copy-start | bytes 24580
  10.5 4.7 %collective-permute-start.7 = (f32[112,128]{1,0:T(8,128)S(1)}, f32[112,128]{1,0:T(8,128)S(1)}, u32[]{:S(2)}, u32[]{:S(2)}) collective-permute-start(f32[112,128]{1,0:T(8,128)S(1)} %join.1.refs_1_), channel_id=1, source_target_pairs={{0,9},{1,8},{2,11},{3,10},{4,13},{5,12},{6,15},{7,14},{8,1},{9,0},... | collective-permute-start | bytes 172040 | tf_op jit(solution)/shard_map/ppermute | solution.py:542
  20.4 2.5 %collective-permute-start.8 = (f32[64,128]{1,0:T(8,128)S(1)}, f32[64,128]{1,0:T(8,128)S(1)}, u32[]{:S(2)}, u32[]{:S(2)}) collective-permute-start(f32[64,128]{1,0:T(8,128)S(1)} %get-tuple-element.50), channel_id=1, source_target_pairs={{0,1},{1,0},{2,3},{3,2},{4,5},{5,4},{6,7},{7,6},{8,9},{9,8},{10,11... | collective-permute-start | bytes 98312 | tf_op jit(solution)/shard_map/ppermute | solution.py:542
  22.9 4.7 %collective-permute-start.10 = (f32[32,128]{1,0:T(8,128)S(1)}, f32[32,128]{1,0:T(8,128)S(1)}, u32[]{:S(2)}, u32[]{:S(2)}) collective-permute-start(f32[32,128]{1,0:T(8,128)S(1)} %get-tuple-element.53), channel_id=1, source_target_pairs={{0,6},{1,7},{2,4},{3,5},{4,2},{5,3},{6,0},{7,1},{8,14},{9,15},{10,... | collective-permute-start | bytes 49160 | tf_op jit(solution)/shard_map/ppermute | solution.py:542
  24.3 3.4 %collective-permute-start.11 = (f32[32,128]{1,0:T(8,128)S(1)}, f32[32,128]{1,0:T(8,128)S(1)}, u32[]{:S(2)}, u32[]{:S(2)}) collective-permute-start(f32[32,128]{1,0:T(8,128)S(1)} %get-tuple-element.54), channel_id=1, source_target_pairs={{0,3},{1,2},{2,1},{3,0},{4,7},{5,6},{6,5},{7,4},{8,11},{9,10},{10,... | collective-permute-start | bytes 49160 | tf_op jit(solution)/shard_map/ppermute | solution.py:542
  24.5 3.3 %collective-permute-start.9 = (f32[32,128]{1,0:T(8,128)S(1)}, f32[32,128]{1,0:T(8,128)S(1)}, u32[]{:S(2)}, u32[]{:S(2)}) collective-permute-start(f32[32,128]{1,0:T(8,128)S(1)} %get-tuple-element.52), channel_id=1, source_target_pairs={{0,5},{1,4},{2,7},{3,6},{4,1},{5,0},{6,3},{7,2},{8,13},{9,12},{10,... | collective-permute-start | bytes 49160 | tf_op jit(solution)/shard_map/ppermute | solution.py:542

commit v5 on v4

--- a/solution.py
+++ b/solution.py
@@ -69,7 +69,7 @@
 
 
 EXCHANGED = 3
-PARTS = ((0,), (1, 2, 3))
+PARTS = ((0,), (3, 1, 2))
 PLACED = (0, 2, 3, 1)
 
 
@@ -161,7 +161,7 @@
         out[2 * half :] = meta
 
 
-def join_kernel(_, *refs):
+def join_kernel(*refs):
     out_ref = refs[-1]
     rows = refs[0].shape[0] - 8
     count = len(refs) - 1
@@ -570,7 +570,6 @@
         permuted(length, 1),
     )
     crossed = [permuted(p, mask) for p, mask in zip(dealt[1:], masks)]
-    gain, step, pair, back, row2, col2, power = prepare(own[2:], dealt[0])
     held = [dealt[0], *crossed]
     sent = []
     for spots in PARTS:
@@ -578,10 +577,11 @@
             sent.append(held[spots[0]])
         else:
             rows = 2 * half * len(spots) + -(-4 * len(spots) // 8) * 8
-            sent += local(join_kernel, [(rows, width)], "join", gain, *(held[k] for k in spots))
+            sent += local(join_kernel, [(rows, width)], "join", *(held[k] for k in spots))
+    gain, step, pair, back, row2, col2, power = prepare(own[2:], sent[-1])
     for k in range(EXCHANGED, bits):
         sent = sent + [permuted(x, (1 << k) | 1) for x in sent]
-    rowprod, colprod, powers = products(live, pair, row2, col2, power, crossed[2])
+    rowprod, colprod, powers = products(live, pair, row2, col2, power, sent[len(PARTS) - 1])
     model = [gain, step, pair, rowprod, colprod, back, powers]
     stay, leave = smooth(bits, blocks_of, nb, cap, live, sent, prior_mean.reshape(nblocks, width), model)
     split = local(split_kernel, [(2 * half, width)] * 4, "split", stay, permuted(leave, 1))

time: 28.6 us -> 28.1 us (0.983)
  starting transfers between devices: 14.9 us -> 14 us
  waiting for transfers between devices: 2.55 us -> 2.97 us
    ppermute x12, starting transfers between devices: 14.9 us -> 14 us  [permuted(): return lax.ppermute(x, 'tm', [(i, i ^ mask) for i in range(count)])]
    ppermute x12, waiting for transfers between devices: 2.55 us -> 2.97 us  [permuted(): return lax.ppermute(x, 'tm', [(i, i ^ mask) for i in range(count)])]
  transfers between devices with their start and end apart: 12 -> 12, of which waited for: 3 -> 4; matrix products, arithmetic and copies ran while one was open for 0% -> 0% of each run, Pallas kernels for 15% -> 15%
where the time goes in v5:
time: 28.1 us; the launch traced here: 28 us
  starting transfers between devices  14 us (50%)
  Pallas kernels  10.2 us (36%)
  waiting for transfers between devices  2.97 us (11%)
  between operations  0.76 us (3%)
    ppermute x12, starting transfers between devices, permuted(): return lax.ppermute(x, 'tm', [(i, i ^ mask) for i in range(count)])  14 us
    pallas_call x1, Pallas kernels, smooth(): pl.pallas_call(functools.partial(smoother_kernel, bits, blocks_of, live,...  5.2 us
    ppermute x12, waiting for transfers between devices, permuted(): return lax.ppermute(x, 'tm', [(i, i ^ mask) for i in range(count)])  2.97 us
    pallas_call x1, Pallas kernels, products(): pl.pallas_call(functools.partial(product_kernel, live), out_shape=[pltpu....  2.36 us
    pallas_call x1, Pallas kernels, fetch(): pl.pallas_call(functools.partial(fetch_kernel, blocks_of), out_shape=[plt...  1.11 us
    pallas_call x1, Pallas kernels, prepare(): pl.pallas_call(model_kernel, out_shape=[pltpu.VMEM((nb, 2 * width, width)...  0.79 us
    pallas_call x1, Pallas kernels, place(): pl.pallas_call(functools.partial(place_kernel, bits), out_shape=jax.Shape...  0.64 us
  transfers between devices with their start and end apart: 12, of which 4 were waited for; matrix products, arithmetic and copies ran while one was open for 0% of the time, Pallas kernels for 15%

profile of v5, /device:TPU:0, one launch (start us, length us, event | category | flops | bytes accessed | tf_op | source)
XLA Modules:
  0.0 28.0 jit_solution(8302575539833411059)
XLA Ops:
  0.0 0.5 %collective-permute-start = (f32[8,2048]{1,0:T(8,128)}, f32[8,2048]{1,0:T(8,128)S(1)}, u32[]{:S(2)}, u32[]{:S(2)}) collective-permute-start(f32[8,2048]{1,0:T(8,128)} %x_hbm.1), channel_id=1, source_target_pairs={{0,1},{1,0},{2,3},{3,2},{4,5},{5,4},{6,7},{7,6},{8,9},{9,8},{10,11... | collective-permute-start | bytes 196616 | tf_op jit(solution)/shard_map/ppermute | solution.py:542
  1.1 0.1 collective-permute-start.2
  1.2 0.5 %collective-permute-start.1 = (s32[8,16]{1,0:T(8,128)}, s32[8,16]{1,0:T(8,128)S(1)}, u32[]{:S(2)}, u32[]{:S(2)}) collective-permute-start(s32[8,16]{1,0:T(8,128)} %mask_hbm.1), channel_id=1, source_target_pairs={{0,1},{1,0},{2,3},{3,2},{4,5},{5,4},{6,7},{7,6},{8,9},{9,8},{10,11... | collective-permute-start | bytes 1544 | tf_op jit(solution)/shard_map/ppermute | solution.py:542
  1.7 1.1 %fetch.1 = (f32[8,2048]{1,0:T(8,128)S(1)}, s32[8,16]{1,0:T(8,128)S(1)}, f32[2,128,128]{2,1,0:T(8,128)S(1)}, f32[2,128,128]{2,1,0:T(8,128)S(1)}, f32[2,128,128]{2,1,0:T(8,128)S(1)}) custom-call(f32[8,2048]{1,0:T(8,128)} %x_hbm.1, s32[8,16]{1,0:T(8,128)} %mask_hbm.1, f32[16,128,128]{2,1,0:T(8,128)} %t_hbm.1, f32[16,128,128]{2,1,0:T(8,128)} %k_hbm.1, ...), custom_call_target="tpu_custom_call" | custom-call | bytes 1000000 | tf_op jit(solution)/shard_map/fetch/pallas_call | solution.py:126
  2.8 0.0 collective-permute-done.1.other_mask_ref
  2.8 0.0 collective-permute-done.2.other_length_ref
  2.8 0.0 collective-permute-done.other_ref
  2.8 0.1 deal.1
  2.9 3.8 %collective-permute-start.3 = (f32[40,128]{1,0:T(8,128)S(1)}, f32[40,128]{1,0:T(8,128)S(1)}, u32[]{:S(2)}, u32[]{:S(2)}) collective-permute-start(f32[40,128]{1,0:T(8,128)S(1)} %get-tuple-element.33), channel_id=1, source_target_pairs={{0,6},{1,7},{2,4},{3,5},{4,2},{5,3},{6,0},{7,1},{8,14},{9,15},{10,... | collective-permute-start | bytes 61448 | tf_op jit(solution)/shard_map/ppermute | solution.py:542
  6.8 0.1 collective-permute-start.4
  6.9 0.3 collective-permute-start.5
  7.1 2.5 %collective-permute-start.6 = (f32[40,128]{1,0:T(8,128)S(1)}, f32[40,128]{1,0:T(8,128)S(1)}, u32[]{:S(2)}, u32[]{:S(2)}) collective-permute-start(f32[40,128]{1,0:T(8,128)S(1)} %get-tuple-element.32.refs_0_), channel_id=1, source_target_pairs={{0,9},{1,8},{2,11},{3,10},{4,13},{5,12},{6,15},{7,14},{8,1},{9,0},... | collective-permute-start | bytes 61448 | tf_op jit(solution)/shard_map/ppermute | solution.py:542
  9.6 0.0 collective-permute-done.3.refs_0_
  9.6 0.4 %collective-permute-done.4.refs_1_ = f32[40,128]{1,0:T(8,128)S(1)} collective-permute-done((f32[40,128]{1,0:T(8,128)S(1)}, f32[40,128]{1,0:T(8,128)S(1)}, u32[]{:S(2)}, u32[]{:S(2)}) %collective-permute-start.4) | collective-permute-done | bytes 20512 | tf_op jit(solution)/shard_map/ppermute | solution.py:542
  10.0 0.1 collective-permute-done.5.refs_2_
  10.1 2.7 %collective-permute-start.7 = (f32[112,128]{1,0:T(8,128)S(1)}, f32[112,128]{1,0:T(8,128)S(1)}, u32[]{:S(2)}, u32[]{:S(2)}) collective-permute-start(f32[112,128]{1,0:T(8,128)S(1)} %join.1.after_ref.refs_1_), channel_id=1, source_target_pairs={{0,9},{1,8},{2,11},{3,10},{4,13},{5,12},{6,15},{7,14},{8,1},{9,0},... | collective-permute-start | bytes 172040 | tf_op jit(solution)/shard_map/ppermute | solution.py:542
  12.8 0.8 %prepare.1 = (bf16[2,256,128]{2,1,0:T(8,128)(2,1)S(1)}, bf16[2,256,256]{2,1,0:T(8,128)(2,1)S(1)}, bf16[2,256,512]{2,1,0:T(8,128)(2,1)S(1)}, bf16[2,256,128]{2,1,...) custom-call(f32[2,128,128]{2,1,0:T(8,128)S(1)} %get-tuple-element.36.t_ref, ...), custom_call_target="tpu_custom_call" | custom-call | flops 1000000000 | bytes 4000000 | tf_op jit(solution)/shard_map/prepare/pallas_call | solution.py:274
  13.6 0.0 copy-start
  13.6 2.4 %products.1 = (f32[2,16,128,128]{3,2,1,0:T(8,128)S(1)}, f32[2,16,128,128]{3,2,1,0:T(8,128)S(1)}, bf16[2,4,768,128]{3,2,1,0:T(8,128)(2,1)S(1)}) custom-call(bf16[2,256,512]{2,1,0:T(8,128)(2,1)S(1)} %get-tuple-element.41.pair_ref.refs_7_, f32[2,512,128]{2,1,0:T(8,128)S(1)} %get-tuple-element.42.row_ref, f32[2,512,128]{2,1,0:T(8,128)S(1)} %get-tuple-element.43.col_ref, ...), custom_call_target="tpu_custom_call" | custom-call | flops 1000000000 | bytes 4000000 | tf_op jit(solution)/shard_map/products/pallas_call | solution.py:297
  16.0 0.0 collective-permute-done.6.refs_2_
  16.0 0.0 collective-permute-done.7.refs_3_
  16.0 0.0 copy-done
  16.0 5.2 %smooth.1 = (f32[64,128]{1,0:T(8,128)S(1)}, f32[64,128]{1,0:T(8,128)S(1)}) custom-call(f32[40,128]{1,0:T(8,128)S(1)} %get-tuple-element.32.refs_0_, f32[112,128]{1,0:T(8,128)S(1)} %join.1.after_ref.refs_1_, f32[40,128]{1,0:T(8,128)S(1)} %collective-permute-done.6.refs_2_, f32[112,128]{1,0:T(8,128)S(1)} %collective-permute-done.7.refs_3_, ...), custom_call_target="tpu_custom_call" | custom-call | tf_op jit(solution)/shard_map/smooth/pallas_call | solution.py:515
  21.2 0.4 %collective-permute-start.8 = (f32[64,128]{1,0:T(8,128)S(1)}, f32[64,128]{1,0:T(8,128)S(1)}, u32[]{:S(2)}, u32[]{:S(2)}) collective-permute-start(f32[64,128]{1,0:T(8,128)S(1)} %get-tuple-element.50), channel_id=1, source_target_pairs={{0,1},{1,0},{2,3},{3,2},{4,5},{5,4},{6,7},{7,6},{8,9},{9,8},{10,11... | collective-permute-start | bytes 98312 | tf_op jit(solution)/shard_map/ppermute | solution.py:542
  21.6 0.9 %collective-permute-done.8.came_ref = f32[64,128]{1,0:T(8,128)S(1)} collective-permute-done((f32[64,128]{1,0:T(8,128)S(1)}, f32[64,128]{1,0:T(8,128)S(1)}, u32[]{:S(2)}, u32[]{:S(2)}) %collective-permute-start.8) | collective-permute-done | bytes 32800 | tf_op jit(solution)/shard_map/ppermute | solution.py:542
  22.5 1.4 %collective-permute-start.10 = (f32[32,128]{1,0:T(8,128)S(1)}, f32[32,128]{1,0:T(8,128)S(1)}, u32[]{:S(2)}, u32[]{:S(2)}) collective-permute-start(f32[32,128]{1,0:T(8,128)S(1)} %get-tuple-element.53), channel_id=1, source_target_pairs={{0,6},{1,7},{2,4},{3,5},{4,2},{5,3},{6,0},{7,1},{8,14},{9,15},{10,... | collective-permute-start | bytes 49160 | tf_op jit(solution)/shard_map/ppermute | solution.py:542
  23.9 0.1 collective-permute-start.11
  24.0 1.7 %collective-permute-start.9 = (f32[32,128]{1,0:T(8,128)S(1)}, f32[32,128]{1,0:T(8,128)S(1)}, u32[]{:S(2)}, u32[]{:S(2)}) collective-permute-start(f32[32,128]{1,0:T(8,128)S(1)} %get-tuple-element.52), channel_id=1, source_target_pairs={{0,5},{1,4},{2,7},{3,6},{4,1},{5,0},{6,3},{7,2},{8,13},{9,12},{10,... | collective-permute-start | bytes 49160 | tf_op jit(solution)/shard_map/ppermute | solution.py:542
  25.7 1.5 %collective-permute-done.10.refs_2_ = f32[32,128]{1,0:T(8,128)S(1)} collective-permute-done((f32[32,128]{1,0:T(8,128)S(1)}, f32[32,128]{1,0:T(8,128)S(1)}, u32[]{:S(2)}, u32[]{:S(2)}) %collective-permute-start.10) | collective-permute-done | bytes 16416 | tf_op jit(solution)/shard_map/ppermute | solution.py:542
  27.2 0.0 collective-permute-done.11.refs_3_
  27.3 0.0 collective-permute-done.9.refs_1_
  27.3 0.6 %place.1 = f32[8,2048]{1,0:T(8,128)} custom-call(f32[32,128]{1,0:T(8,128)S(1)} %get-tuple-element.51.refs_0_, f32[32,128]{1,0:T(8,128)S(1)} %collective-permute-done.9.refs_1_, f32[32,128]{1,0:T(8,128)S(1)} %collective-permute-done.10.refs_2_, f32[32,128]{1,0:T(8,128)S(1)} %collective-permute-done.11.refs_3_), custom_call_target="tpu_custom_call" | custom-call | tf_op jit(solution)/shard_map/place/pallas_call | solution.py:195
  (3 shorter events, 0.0 us)
Async XLA Ops:
  0.0 2.8 %collective-permute-start = (f32[8,2048]{1,0:T(8,128)}, f32[8,2048]{1,0:T(8,128)S(1)}, u32[]{:S(2)}, u32[]{:S(2)}) collective-permute-start(f32[8,2048]{1,0:T(8,128)} %x_hbm.1), channel_id=1, source_target_pairs={{0,1},{1,0},{2,3},{3,2},{4,5},{5,4},{6,7},{7,6},{8,9},{9,8},{10,11... | collective-permute-start | bytes 196616 | tf_op jit(solution)/shard_map/ppermute | solution.py:542
  1.1 1.7 %collective-permute-start.2 = (f32[8,128]{1,0:T(8,128)S(1)}, f32[8,128]{1,0:T(8,128)S(1)}, u32[]{:S(2)}, u32[]{:S(2)}) collective-permute-start(f32[8,128]{1,0:T(8,128)S(1)} %broadcast_in_dim.9.length_ref), channel_id=1, source_target_pairs={{0,1},{1,0},{2,3},{3,2},{4,5},{5,4},{6,7},{7,6},{8,9},{9,8},{10,11... | collective-permute-start | bytes 12296 | tf_op jit(solution)/shard_map/ppermute | solution.py:542
  1.2 1.6 %collective-permute-start.1 = (s32[8,16]{1,0:T(8,128)}, s32[8,16]{1,0:T(8,128)S(1)}, u32[]{:S(2)}, u32[]{:S(2)}) collective-permute-start(s32[8,16]{1,0:T(8,128)} %mask_hbm.1), channel_id=1, source_target_pairs={{0,1},{1,0},{2,3},{3,2},{4,5},{5,4},{6,7},{7,6},{8,9},{9,8},{10,11... | collective-permute-start | bytes 1544 | tf_op jit(solution)/shard_map/ppermute | solution.py:542
  2.9 6.7 %collective-permute-start.3 = (f32[40,128]{1,0:T(8,128)S(1)}, f32[40,128]{1,0:T(8,128)S(1)}, u32[]{:S(2)}, u32[]{:S(2)}) collective-permute-start(f32[40,128]{1,0:T(8,128)S(1)} %get-tuple-element.33), channel_id=1, source_target_pairs={{0,6},{1,7},{2,4},{3,5},{4,2},{5,3},{6,0},{7,1},{8,14},{9,15},{10,... | collective-permute-start | bytes 61448 | tf_op jit(solution)/shard_map/ppermute | solution.py:542
  6.8 3.2 %collective-permute-start.4 = (f32[40,128]{1,0:T(8,128)S(1)}, f32[40,128]{1,0:T(8,128)S(1)}, u32[]{:S(2)}, u32[]{:S(2)}) collective-permute-start(f32[40,128]{1,0:T(8,128)S(1)} %get-tuple-element.34), channel_id=1, source_target_pairs={{0,3},{1,2},{2,1},{3,0},{4,7},{5,6},{6,5},{7,4},{8,11},{9,10},{10,... | collective-permute-start | bytes 61448 | tf_op jit(solution)/shard_map/ppermute | solution.py:542
  6.9 3.2 %collective-permute-start.5 = (f32[40,128]{1,0:T(8,128)S(1)}, f32[40,128]{1,0:T(8,128)S(1)}, u32[]{:S(2)}, u32[]{:S(2)}) collective-permute-start(f32[40,128]{1,0:T(8,128)S(1)} %get-tuple-element.35), channel_id=1, source_target_pairs={{0,5},{1,4},{2,7},{3,6},{4,1},{5,0},{6,3},{7,2},{8,13},{9,12},{10,... | collective-permute-start | bytes 61448 | tf_op jit(solution)/shard_map/ppermute | solution.py:542
  7.1 8.9 %collective-permute-start.6 = (f32[40,128]{1,0:T(8,128)S(1)}, f32[40,128]{1,0:T(8,128)S(1)}, u32[]{:S(2)}, u32[]{:S(2)}) collective-permute-start(f32[40,128]{1,0:T(8,128)S(1)} %get-tuple-element.32.refs_0_), channel_id=1, source_target_pairs={{0,9},{1,8},{2,11},{3,10},{4,13},{5,12},{6,15},{7,14},{8,1},{9,0},... | collective-permute-start | bytes 61448 | tf_op jit(solution)/shard_map/ppermute | solution.py:542
  10.1 5.9 %collective-permute-start.7 = (f32[112,128]{1,0:T(8,128)S(1)}, f32[112,128]{1,0:T(8,128)S(1)}, u32[]{:S(2)}, u32[]{:S(2)}) collective-permute-start(f32[112,128]{1,0:T(8,128)S(1)} %join.1.after_ref.refs_1_), channel_id=1, source_target_pairs={{0,9},{1,8},{2,11},{3,10},{4,13},{5,12},{6,15},{7,14},{8,1},{9,0},... | collective-permute-start | bytes 172040 | tf_op jit(solution)/shard_map/ppermute | solution.py:542
  13.6 2.4 %copy-start = (f32[2048]{0:T(1024)S(1)}, f32[2048]{0:T(1024)}, u32[]{:S(2)}) copy-start(f32[2048]{0:T(1024)} %param.10) | copy-start | bytes 24580
  21.2 1.3 %collective-permute-start.8 = (f32[64,128]{1,0:T(8,128)S(1)}, f32[64,128]{1,0:T(8,128)S(1)}, u32[]{:S(2)}, u32[]{:S(2)}) collective-permute-start(f32[64,128]{1,0:T(8,128)S(1)} %get-tuple-element.50), channel_id=1, source_target_pairs={{0,1},{1,0},{2,3},{3,2},{4,5},{5,4},{6,7},{7,6},{8,9},{9,8},{10,11... | collective-permute-start | bytes 98312 | tf_op jit(solution)/shard_map/ppermute | solution.py:542
  22.5 4.7 %collective-permute-start.10 = (f32[32,128]{1,0:T(8,128)S(1)}, f32[32,128]{1,0:T(8,128)S(1)}, u32[]{:S(2)}, u32[]{:S(2)}) collective-permute-start(f32[32,128]{1,0:T(8,128)S(1)} %get-tuple-element.53), channel_id=1, source_target_pairs={{0,6},{1,7},{2,4},{3,5},{4,2},{5,3},{6,0},{7,1},{8,14},{9,15},{10,... | collective-permute-start | bytes 49160 | tf_op jit(solution)/shard_map/ppermute | solution.py:542
  23.9 3.4 %collective-permute-start.11 = (f32[32,128]{1,0:T(8,128)S(1)}, f32[32,128]{1,0:T(8,128)S(1)}, u32[]{:S(2)}, u32[]{:S(2)}) collective-permute-start(f32[32,128]{1,0:T(8,128)S(1)} %get-tuple-element.54), channel_id=1, source_target_pairs={{0,3},{1,2},{2,1},{3,0},{4,7},{5,6},{6,5},{7,4},{8,11},{9,10},{10,... | collective-permute-start | bytes 49160 | tf_op jit(solution)/shard_map/ppermute | solution.py:542
  24.0 3.3 %collective-permute-start.9 = (f32[32,128]{1,0:T(8,128)S(1)}, f32[32,128]{1,0:T(8,128)S(1)}, u32[]{:S(2)}, u32[]{:S(2)}) collective-permute-start(f32[32,128]{1,0:T(8,128)S(1)} %get-tuple-element.52), channel_id=1, source_target_pairs={{0,5},{1,4},{2,7},{3,6},{4,1},{5,0},{6,3},{7,2},{8,13},{9,12},{10,... | collective-permute-start | bytes 49160 | tf_op jit(solution)/shard_map/ppermute | solution.py:542

commit v6 on v5

--- a/solution.py
+++ b/solution.py
@@ -461,7 +461,7 @@
             moved.append(row)
         return tuple(moved)
 
-    lax.fori_loop(0, nchunks // 2, two_steps, tuple(prior_ref[pl.ds(b, 1), :] for b in blocks))
+    lax.fori_loop(0, nchunks // 2, two_steps, tuple(prior_ref[pl.ds(b, 1), :] for b in blocks), unroll=2)
 
     for j in range(nb):
         for n in range(col_ref.shape[1]):
@@ -490,8 +490,12 @@
         for j in range(nb):
             filt_ref[j, :live] = smoothed[j]
         for j in range(nb):
-            moved = side([left(filt_ref[j, sh : sh + live]) for sh in level])
-            smoothed[j] = smoothed[j] + dot(moved, power_ref[j, n, : 2 * width * len(level)])
+            reach = -(-(live - level[0]) // 8) * 8
+            moved = side([left(filt_ref[j, sh : sh + reach]) for sh in level])
+            moved = dot(moved, power_ref[j, n, : 2 * width * len(level)])
+            if reach < live:
+                moved = below([moved, jnp.zeros((live - reach, width), f32)])
+            smoothed[j] = smoothed[j] + moved
     for j in range(nb):
         filt_ref[j, :live] = smoothed[j]
     for j in range(nb):

time: 28.1 us -> 28.1 us (level)
  no operation moved by 1% of the time
where the time goes in v6:
time: 28.1 us; the launch traced here: 27.9 us
  starting transfers between devices  14 us (50%)
  Pallas kernels  10.1 us (36%)
  waiting for transfers between devices  2.97 us (11%)
  between operations  0.76 us (3%)
    ppermute x12, starting transfers between devices, permuted(): return lax.ppermute(x, 'tm', [(i, i ^ mask) for i in range(count)])  14 us
    pallas_call x1, Pallas kernels, smooth(): pl.pallas_call(functools.partial(smoother_kernel, bits, blocks_of, live,...  5.12 us
    ppermute x12, waiting for transfers between devices, permuted(): return lax.ppermute(x, 'tm', [(i, i ^ mask) for i in range(count)])  2.97 us
    pallas_call x1, Pallas kernels, products(): pl.pallas_call(functools.partial(product_kernel, live), out_shape=[pltpu....  2.36 us
    pallas_call x1, Pallas kernels, fetch(): pl.pallas_call(functools.partial(fetch_kernel, blocks_of), out_shape=[plt...  1.11 us
    pallas_call x1, Pallas kernels, prepare(): pl.pallas_call(model_kernel, out_shape=[pltpu.VMEM((nb, 2 * width, width)...  0.79 us
    pallas_call x1, Pallas kernels, place(): pl.pallas_call(functools.partial(place_kernel, bits), out_shape=jax.Shape...  0.64 us
  transfers between devices with their start and end apart: 12, of which 4 were waited for; matrix products, arithmetic and copies ran while one was open for 0% of the time, Pallas kernels for 15%

profile of v6, /device:TPU:0, one launch (start us, length us, event | category | flops | bytes accessed | tf_op | source)
XLA Modules:
  0.0 27.9 jit_solution(3353050237819902028)
XLA Ops:
  0.0 0.5 %collective-permute-start = (f32[8,2048]{1,0:T(8,128)}, f32[8,2048]{1,0:T(8,128)S(1)}, u32[]{:S(2)}, u32[]{:S(2)}) collective-permute-start(f32[8,2048]{1,0:T(8,128)} %x_hbm.1), channel_id=1, source_target_pairs={{0,1},{1,0},{2,3},{3,2},{4,5},{5,4},{6,7},{7,6},{8,9},{9,8},{10,11... | collective-permute-start | bytes 196616 | tf_op jit(solution)/shard_map/ppermute | solution.py:546
  1.1 0.1 collective-permute-start.2
  1.2 0.5 %collective-permute-start.1 = (s32[8,16]{1,0:T(8,128)}, s32[8,16]{1,0:T(8,128)S(1)}, u32[]{:S(2)}, u32[]{:S(2)}) collective-permute-start(s32[8,16]{1,0:T(8,128)} %mask_hbm.1), channel_id=1, source_target_pairs={{0,1},{1,0},{2,3},{3,2},{4,5},{5,4},{6,7},{7,6},{8,9},{9,8},{10,11... | collective-permute-start | bytes 1544 | tf_op jit(solution)/shard_map/ppermute | solution.py:546
  1.7 1.1 %fetch.1 = (f32[8,2048]{1,0:T(8,128)S(1)}, s32[8,16]{1,0:T(8,128)S(1)}, f32[2,128,128]{2,1,0:T(8,128)S(1)}, f32[2,128,128]{2,1,0:T(8,128)S(1)}, f32[2,128,128]{2,1,0:T(8,128)S(1)}) custom-call(f32[8,2048]{1,0:T(8,128)} %x_hbm.1, s32[8,16]{1,0:T(8,128)} %mask_hbm.1, f32[16,128,128]{2,1,0:T(8,128)} %t_hbm.1, f32[16,128,128]{2,1,0:T(8,128)} %k_hbm.1, ...), custom_call_target="tpu_custom_call" | custom-call | bytes 1000000 | tf_op jit(solution)/shard_map/fetch/pallas_call | solution.py:126
  2.8 0.0 collective-permute-done.1.other_mask_ref
  2.8 0.0 collective-permute-done.2.other_length_ref
  2.8 0.0 collective-permute-done.other_ref
  2.8 0.1 deal.1
  2.9 3.8 %collective-permute-start.3 = (f32[40,128]{1,0:T(8,128)S(1)}, f32[40,128]{1,0:T(8,128)S(1)}, u32[]{:S(2)}, u32[]{:S(2)}) collective-permute-start(f32[40,128]{1,0:T(8,128)S(1)} %get-tuple-element.33), channel_id=1, source_target_pairs={{0,6},{1,7},{2,4},{3,5},{4,2},{5,3},{6,0},{7,1},{8,14},{9,15},{10,... | collective-permute-start | bytes 61448 | tf_op jit(solution)/shard_map/ppermute | solution.py:546
  6.8 0.1 collective-permute-start.4
  6.9 0.3 collective-permute-start.5
  7.1 2.5 %collective-permute-start.6 = (f32[40,128]{1,0:T(8,128)S(1)}, f32[40,128]{1,0:T(8,128)S(1)}, u32[]{:S(2)}, u32[]{:S(2)}) collective-permute-start(f32[40,128]{1,0:T(8,128)S(1)} %get-tuple-element.32.refs_0_), channel_id=1, source_target_pairs={{0,9},{1,8},{2,11},{3,10},{4,13},{5,12},{6,15},{7,14},{8,1},{9,0},... | collective-permute-start | bytes 61448 | tf_op jit(solution)/shard_map/ppermute | solution.py:546
  9.6 0.0 collective-permute-done.3.refs_0_
  9.6 0.4 %collective-permute-done.4.refs_1_ = f32[40,128]{1,0:T(8,128)S(1)} collective-permute-done((f32[40,128]{1,0:T(8,128)S(1)}, f32[40,128]{1,0:T(8,128)S(1)}, u32[]{:S(2)}, u32[]{:S(2)}) %collective-permute-start.4) | collective-permute-done | bytes 20512 | tf_op jit(solution)/shard_map/ppermute | solution.py:546
  10.0 0.1 collective-permute-done.5.refs_2_
  10.1 2.7 %collective-permute-start.7 = (f32[112,128]{1,0:T(8,128)S(1)}, f32[112,128]{1,0:T(8,128)S(1)}, u32[]{:S(2)}, u32[]{:S(2)}) collective-permute-start(f32[112,128]{1,0:T(8,128)S(1)} %join.1.after_ref.refs_1_), channel_id=1, source_target_pairs={{0,9},{1,8},{2,11},{3,10},{4,13},{5,12},{6,15},{7,14},{8,1},{9,0},... | collective-permute-start | bytes 172040 | tf_op jit(solution)/shard_map/ppermute | solution.py:546
  12.8 0.8 %prepare.1 = (bf16[2,256,128]{2,1,0:T(8,128)(2,1)S(1)}, bf16[2,256,256]{2,1,0:T(8,128)(2,1)S(1)}, bf16[2,256,512]{2,1,0:T(8,128)(2,1)S(1)}, bf16[2,256,128]{2,1,...) custom-call(f32[2,128,128]{2,1,0:T(8,128)S(1)} %get-tuple-element.36.t_ref, ...), custom_call_target="tpu_custom_call" | custom-call | flops 1000000000 | bytes 4000000 | tf_op jit(solution)/shard_map/prepare/pallas_call | solution.py:274
  13.6 0.0 copy-start
  13.6 2.4 %products.1 = (f32[2,16,128,128]{3,2,1,0:T(8,128)S(1)}, f32[2,16,128,128]{3,2,1,0:T(8,128)S(1)}, bf16[2,4,768,128]{3,2,1,0:T(8,128)(2,1)S(1)}) custom-call(bf16[2,256,512]{2,1,0:T(8,128)(2,1)S(1)} %get-tuple-element.41.pair_ref.refs_7_, f32[2,512,128]{2,1,0:T(8,128)S(1)} %get-tuple-element.42.row_ref, f32[2,512,128]{2,1,0:T(8,128)S(1)} %get-tuple-element.43.col_ref, ...), custom_call_target="tpu_custom_call" | custom-call | flops 1000000000 | bytes 4000000 | tf_op jit(solution)/shard_map/products/pallas_call | solution.py:297
  16.0 0.0 collective-permute-done.6.refs_2_
  16.0 0.0 collective-permute-done.7.refs_3_
  16.0 0.0 copy-done
  16.0 5.1 %smooth.1 = (f32[64,128]{1,0:T(8,128)S(1)}, f32[64,128]{1,0:T(8,128)S(1)}) custom-call(f32[40,128]{1,0:T(8,128)S(1)} %get-tuple-element.32.refs_0_, f32[112,128]{1,0:T(8,128)S(1)} %join.1.after_ref.refs_1_, f32[40,128]{1,0:T(8,128)S(1)} %collective-permute-done.6.refs_2_, f32[112,128]{1,0:T(8,128)S(1)} %collective-permute-done.7.refs_3_, ...), custom_call_target="tpu_custom_call" | custom-call | tf_op jit(solution)/shard_map/smooth/pallas_call | solution.py:519
  21.1 0.4 %collective-permute-start.8 = (f32[64,128]{1,0:T(8,128)S(1)}, f32[64,128]{1,0:T(8,128)S(1)}, u32[]{:S(2)}, u32[]{:S(2)}) collective-permute-start(f32[64,128]{1,0:T(8,128)S(1)} %get-tuple-element.50), channel_id=1, source_target_pairs={{0,1},{1,0},{2,3},{3,2},{4,5},{5,4},{6,7},{7,6},{8,9},{9,8},{10,11... | collective-permute-start | bytes 98312 | tf_op jit(solution)/shard_map/ppermute | solution.py:546
  21.5 0.9 %collective-permute-done.8.came_ref = f32[64,128]{1,0:T(8,128)S(1)} collective-permute-done((f32[64,128]{1,0:T(8,128)S(1)}, f32[64,128]{1,0:T(8,128)S(1)}, u32[]{:S(2)}, u32[]{:S(2)}) %collective-permute-start.8) | collective-permute-done | bytes 32800 | tf_op jit(solution)/shard_map/ppermute | solution.py:546
  22.4 1.4 %collective-permute-start.10 = (f32[32,128]{1,0:T(8,128)S(1)}, f32[32,128]{1,0:T(8,128)S(1)}, u32[]{:S(2)}, u32[]{:S(2)}) collective-permute-start(f32[32,128]{1,0:T(8,128)S(1)} %get-tuple-element.53), channel_id=1, source_target_pairs={{0,6},{1,7},{2,4},{3,5},{4,2},{5,3},{6,0},{7,1},{8,14},{9,15},{10,... | collective-permute-start | bytes 49160 | tf_op jit(solution)/shard_map/ppermute | solution.py:546
  23.8 0.1 collective-permute-start.11
  23.9 1.7 %collective-permute-start.9 = (f32[32,128]{1,0:T(8,128)S(1)}, f32[32,128]{1,0:T(8,128)S(1)}, u32[]{:S(2)}, u32[]{:S(2)}) collective-permute-start(f32[32,128]{1,0:T(8,128)S(1)} %get-tuple-element.52), channel_id=1, source_target_pairs={{0,5},{1,4},{2,7},{3,6},{4,1},{5,0},{6,3},{7,2},{8,13},{9,12},{10,... | collective-permute-start | bytes 49160 | tf_op jit(solution)/shard_map/ppermute | solution.py:546
  25.6 1.5 %collective-permute-done.10.refs_2_ = f32[32,128]{1,0:T(8,128)S(1)} collective-permute-done((f32[32,128]{1,0:T(8,128)S(1)}, f32[32,128]{1,0:T(8,128)S(1)}, u32[]{:S(2)}, u32[]{:S(2)}) %collective-permute-start.10) | collective-permute-done | bytes 16416 | tf_op jit(solution)/shard_map/ppermute | solution.py:546
  27.2 0.0 collective-permute-done.11.refs_3_
  27.2 0.0 collective-permute-done.9.refs_1_
  27.2 0.6 %place.1 = f32[8,2048]{1,0:T(8,128)} custom-call(f32[32,128]{1,0:T(8,128)S(1)} %get-tuple-element.51.refs_0_, f32[32,128]{1,0:T(8,128)S(1)} %collective-permute-done.9.refs_1_, f32[32,128]{1,0:T(8,128)S(1)} %collective-permute-done.10.refs_2_, f32[32,128]{1,0:T(8,128)S(1)} %collective-permute-done.11.refs_3_), custom_call_target="tpu_custom_call" | custom-call | tf_op jit(solution)/shard_map/place/pallas_call | solution.py:195
  (3 shorter events, 0.0 us)
Async XLA Ops:
  0.0 2.8 %collective-permute-start = (f32[8,2048]{1,0:T(8,128)}, f32[8,2048]{1,0:T(8,128)S(1)}, u32[]{:S(2)}, u32[]{:S(2)}) collective-permute-start(f32[8,2048]{1,0:T(8,128)} %x_hbm.1), channel_id=1, source_target_pairs={{0,1},{1,0},{2,3},{3,2},{4,5},{5,4},{6,7},{7,6},{8,9},{9,8},{10,11... | collective-permute-start | bytes 196616 | tf_op jit(solution)/shard_map/ppermute | solution.py:546
  1.1 1.7 %collective-permute-start.2 = (f32[8,128]{1,0:T(8,128)S(1)}, f32[8,128]{1,0:T(8,128)S(1)}, u32[]{:S(2)}, u32[]{:S(2)}) collective-permute-start(f32[8,128]{1,0:T(8,128)S(1)} %broadcast_in_dim.9.length_ref), channel_id=1, source_target_pairs={{0,1},{1,0},{2,3},{3,2},{4,5},{5,4},{6,7},{7,6},{8,9},{9,8},{10,11... | collective-permute-start | bytes 12296 | tf_op jit(solution)/shard_map/ppermute | solution.py:546
  1.2 1.6 %collective-permute-start.1 = (s32[8,16]{1,0:T(8,128)}, s32[8,16]{1,0:T(8,128)S(1)}, u32[]{:S(2)}, u32[]{:S(2)}) collective-permute-start(s32[8,16]{1,0:T(8,128)} %mask_hbm.1), channel_id=1, source_target_pairs={{0,1},{1,0},{2,3},{3,2},{4,5},{5,4},{6,7},{7,6},{8,9},{9,8},{10,11... | collective-permute-start | bytes 1544 | tf_op jit(solution)/shard_map/ppermute | solution.py:546
  2.9 6.7 %collective-permute-start.3 = (f32[40,128]{1,0:T(8,128)S(1)}, f32[40,128]{1,0:T(8,128)S(1)}, u32[]{:S(2)}, u32[]{:S(2)}) collective-permute-start(f32[40,128]{1,0:T(8,128)S(1)} %get-tuple-element.33), channel_id=1, source_target_pairs={{0,6},{1,7},{2,4},{3,5},{4,2},{5,3},{6,0},{7,1},{8,14},{9,15},{10,... | collective-permute-start | bytes 61448 | tf_op jit(solution)/shard_map/ppermute | solution.py:546
  6.8 3.2 %collective-permute-start.4 = (f32[40,128]{1,0:T(8,128)S(1)}, f32[40,128]{1,0:T(8,128)S(1)}, u32[]{:S(2)}, u32[]{:S(2)}) collective-permute-start(f32[40,128]{1,0:T(8,128)S(1)} %get-tuple-element.34), channel_id=1, source_target_pairs={{0,3},{1,2},{2,1},{3,0},{4,7},{5,6},{6,5},{7,4},{8,11},{9,10},{10,... | collective-permute-start | bytes 61448 | tf_op jit(solution)/shard_map/ppermute | solution.py:546
  6.9 3.2 %collective-permute-start.5 = (f32[40,128]{1,0:T(8,128)S(1)}, f32[40,128]{1,0:T(8,128)S(1)}, u32[]{:S(2)}, u32[]{:S(2)}) collective-permute-start(f32[40,128]{1,0:T(8,128)S(1)} %get-tuple-element.35), channel_id=1, source_target_pairs={{0,5},{1,4},{2,7},{3,6},{4,1},{5,0},{6,3},{7,2},{8,13},{9,12},{10,... | collective-permute-start | bytes 61448 | tf_op jit(solution)/shard_map/ppermute | solution.py:546
  7.1 8.9 %collective-permute-start.6 = (f32[40,128]{1,0:T(8,128)S(1)}, f32[40,128]{1,0:T(8,128)S(1)}, u32[]{:S(2)}, u32[]{:S(2)}) collective-permute-start(f32[40,128]{1,0:T(8,128)S(1)} %get-tuple-element.32.refs_0_), channel_id=1, source_target_pairs={{0,9},{1,8},{2,11},{3,10},{4,13},{5,12},{6,15},{7,14},{8,1},{9,0},... | collective-permute-start | bytes 61448 | tf_op jit(solution)/shard_map/ppermute | solution.py:546
  10.1 5.9 %collective-permute-start.7 = (f32[112,128]{1,0:T(8,128)S(1)}, f32[112,128]{1,0:T(8,128)S(1)}, u32[]{:S(2)}, u32[]{:S(2)}) collective-permute-start(f32[112,128]{1,0:T(8,128)S(1)} %join.1.after_ref.refs_1_), channel_id=1, source_target_pairs={{0,9},{1,8},{2,11},{3,10},{4,13},{5,12},{6,15},{7,14},{8,1},{9,0},... | collective-permute-start | bytes 172040 | tf_op jit(solution)/shard_map/ppermute | solution.py:546
  13.6 2.4 %copy-start = (f32[2048]{0:T(1024)S(1)}, f32[2048]{0:T(1024)}, u32[]{:S(2)}) copy-start(f32[2048]{0:T(1024)} %param.10) | copy-start | bytes 24580
  21.1 1.3 %collective-permute-start.8 = (f32[64,128]{1,0:T(8,128)S(1)}, f32[64,128]{1,0:T(8,128)S(1)}, u32[]{:S(2)}, u32[]{:S(2)}) collective-permute-start(f32[64,128]{1,0:T(8,128)S(1)} %get-tuple-element.50), channel_id=1, source_target_pairs={{0,1},{1,0},{2,3},{3,2},{4,5},{5,4},{6,7},{7,6},{8,9},{9,8},{10,11... | collective-permute-start | bytes 98312 | tf_op jit(solution)/shard_map/ppermute | solution.py:546
  22.4 4.7 %collective-permute-start.10 = (f32[32,128]{1,0:T(8,128)S(1)}, f32[32,128]{1,0:T(8,128)S(1)}, u32[]{:S(2)}, u32[]{:S(2)}) collective-permute-start(f32[32,128]{1,0:T(8,128)S(1)} %get-tuple-element.53), channel_id=1, source_target_pairs={{0,6},{1,7},{2,4},{3,5},{4,2},{5,3},{6,0},{7,1},{8,14},{9,15},{10,... | collective-permute-start | bytes 49160 | tf_op jit(solution)/shard_map/ppermute | solution.py:546
  23.8 3.4 %collective-permute-start.11 = (f32[32,128]{1,0:T(8,128)S(1)}, f32[32,128]{1,0:T(8,128)S(1)}, u32[]{:S(2)}, u32[]{:S(2)}) collective-permute-start(f32[32,128]{1,0:T(8,128)S(1)} %get-tuple-element.54), channel_id=1, source_target_pairs={{0,3},{1,2},{2,1},{3,0},{4,7},{5,6},{6,5},{7,4},{8,11},{9,10},{10,... | collective-permute-start | bytes 49160 | tf_op jit(solution)/shard_map/ppermute | solution.py:546
  23.9 3.3 %collective-permute-start.9 = (f32[32,128]{1,0:T(8,128)S(1)}, f32[32,128]{1,0:T(8,128)S(1)}, u32[]{:S(2)}, u32[]{:S(2)}) collective-permute-start(f32[32,128]{1,0:T(8,128)S(1)} %get-tuple-element.52), channel_id=1, source_target_pairs={{0,5},{1,4},{2,7},{3,6},{4,1},{5,0},{6,3},{7,2},{8,13},{9,12},{10,... | collective-permute-start | bytes 49160 | tf_op jit(solution)/shard_map/ppermute | solution.py:546
